TPU v7x, 32 devices: a whole 2x2x4 slice. The times are simulated.
32 devices in a mesh: exp: 8 (over z, y), tp: 4 (over x, core).
Axes of the slice: x: 2, y: 2, z: 4, core: 2. Of those that a mesh axis runs over, the one named last changes fastest.
Arguments:
- tokens: bfloat16 [4096, 2048], P(('exp', 'tp')), may hold values from -6 to 6
- out_grad: bfloat16 [4096, 2048], P(('exp', 'tp')), may hold values from -6 to 6
- first_gain: float32 [2048], replicated, may hold values from 0.5 to 1.5
- second_gain: float32 [2048], replicated, may hold values from 0.5 to 1.5
- query_gain: float32 [128], replicated, may hold values from 0.1 to 1.9
- key_gain: float32 [128], replicated, may hold values from 0.1 to 1.9
- query_weight: bfloat16 [2048, 4096], P('exp', 'tp'), may hold values from -0.125 to 0.125
- key_weight: bfloat16 [2048, 512], P('exp', 'tp'), may hold values from -0.125 to 0.125
- value_weight: bfloat16 [2048, 512], P('exp', 'tp'), may hold values from -0.125 to 0.125
- output_weight: bfloat16 [4096, 2048], P('tp', 'exp'), may hold values from -0.75 to 0.75
- router_weight: bfloat16 [2048, 32], replicated, may hold values from -0.125 to 0.125
- gate_weight: bfloat16 [32, 2048, 768], P(('exp', 'tp')), may hold values from -0.125 to 0.125
- up_weight: bfloat16 [32, 2048, 768], P(('exp', 'tp')), may hold values from -0.125 to 0.125
- down_weight: bfloat16 [32, 768, 2048], P(('exp', 'tp')), may hold values from -0.4375 to 0.4375
- expert_ids: int32 [4096, 8], P(('exp', 'tp')), may hold values from 0 to 31, all different within a row
- router_order: int32 [32, 128], P(('exp', 'tp')), may hold values from 0 to 127, each once within a row
- image_starts: int32 [4, 2], replicated, may hold values from 0 to 768, as said below
Outputs:
- block_out: bfloat16 [4096, 2048], P(('exp', 'tp'))
- tokens_grad: float32 [4096, 2048], P(('exp', 'tp'))
- first_gain_grad: float32 [2048], replicated
- second_gain_grad: float32 [2048], replicated
- query_gain_grad: float32 [128], replicated
- key_gain_grad: float32 [128], replicated
- query_grad: float32 [2048, 4096], P('exp', 'tp')
- key_grad: float32 [2048, 512], P('exp', 'tp')
- value_grad: float32 [2048, 512], P('exp', 'tp')
- output_grad: float32 [4096, 2048], P('tp', 'exp')
- router_grad: float32 [2048, 32], replicated
- gate_grad: float32 [32, 2048, 768], P(('exp', 'tp'))
- up_grad: float32 [32, 2048, 768], P(('exp', 'tp'))
- down_grad: float32 [32, 768, 2048], P(('exp', 'tp'))
Inputs may be any that keep to these rules, and one draw needn't show every extreme that they name: `image_starts`: in each sequence the k-th image piece (k from 0) starts between k * 512 and (k + 1) * 512 - 256, so pieces never intersect. `router_order`: each device's row orders its 128 tokens, each number once. `expert_ids`: each row names 8 different experts.
All inputs are finite; a program needn't handle non-finite values.
Results may differ from a plain program's by a relative error of at most 0.02.
Values may be sent and summed in bfloat16 or wider, within the bound.
A program may use at most 256 MiB of HBM per device.

v0:
```python
import jax
import jax.numpy as jnp
from jax import lax
from jax.sharding import PartitionSpec as P

HD = 128
TOP = 8
IMG_LEN = 256


EPSILON = 1e-06
THETA = 1000000.0
NEGATIVE = -1e30


def from_behind(array, axis, by):
    devices = lax.axis_size(axis)
    pairs = [(i, i + by) for i in range(devices) if 0 <= i + by < devices]
    return lax.ppermute(array, axis, pairs)


def rms_scale(values):
    return lax.rsqrt(jnp.mean(values * values, axis=-1, keepdims=True) + EPSILON)


def rotary_tables(positions, width):
    half = width // 2
    freqs = THETA ** (-(jnp.arange(half, dtype=jnp.float32) * 2.0 / width))
    angles = positions.astype(jnp.float32)[:, None] * freqs[None, :]
    return (jnp.cos(angles), jnp.sin(angles))


def rotate(values, cosine, sine):
    half = values.shape[-1] // 2
    first = values[..., :half]
    second = values[..., half:]
    return jnp.concatenate(
        [first * cosine - second * sine, second * cosine + first * sine], axis=-1
    )


def unrotate(values, cosine, sine):
    half = values.shape[-1] // 2
    first = values[..., :half]
    second = values[..., half:]
    return jnp.concatenate(
        [first * cosine + second * sine, second * cosine - first * sine], axis=-1
    )


def piece_ids(positions, starts):
    inside = (positions[:, None] >= starts[None, :]) & (
        positions[:, None] < starts[None, :] + IMG_LEN
    )
    labels = jnp.arange(1, starts.shape[0] + 1, dtype=jnp.int32)
    return jnp.sum(jnp.where(inside, labels[None, :], 0), axis=1)


def allowed_mask(query_pos, key_pos, query_piece, key_piece):
    causal = key_pos[None, :] <= query_pos[:, None]
    same = (query_piece[:, None] == key_piece[None, :]) & (query_piece[:, None] > 0)
    return causal | same


def norm_back(grad_norm, hat, rms, gain):
    scaled = grad_norm * gain
    inner_mean = jnp.mean(scaled * hat, axis=-1, keepdims=True)
    lead_axes = tuple(range(grad_norm.ndim - 1))
    return (rms * (scaled - hat * inner_mean), jnp.sum(grad_norm * hat, axis=lead_axes))


def gather_rows(rows):
    return lax.all_gather(rows, "tp", axis=0, tiled=True)


def sum_rows(partial_rows):
    return lax.psum_scatter(partial_rows, "tp", scatter_dimension=0, tiled=True)


def route_rows(buffer):
    return lax.all_to_all(buffer, ("exp", "tp"), split_axis=0, concat_axis=0, tiled=True)


def local(
    tokens,
    out_grad,
    first_gain,
    second_gain,
    query_gain,
    key_gain,
    query_weight,
    key_weight,
    value_weight,
    output_weight,
    router_weight,
    gate_weight,
    up_weight,
    down_weight,
    expert_ids,
    router_order,
    image_starts,
):
    f32 = jnp.float32
    bf16 = jnp.bfloat16
    tok_dev, width = tokens.shape
    tp_count = lax.axis_size("tp")
    experts = lax.axis_size("exp") * tp_count
    capacity = (9 * tok_dev * TOP + 8 * experts - 1) // (8 * experts)
    half_len = tok_dev * tp_count
    heads = query_weight.shape[1] // HD
    block = min(512, half_len)
    block_count = half_len // block
    scale = HD ** (-0.5)
    exp_index = lax.axis_index("exp")
    half_index = exp_index % 2
    starts = lax.dynamic_slice_in_dim(image_starts, exp_index // 2, 1, 0)[0]
    full_query, full_key, full_value, full_output = (
        lax.all_gather(query_weight, "exp", axis=0, tiled=True),
        lax.all_gather(key_weight, "exp", axis=0, tiled=True),
        lax.all_gather(value_weight, "exp", axis=0, tiled=True),
        lax.all_gather(output_weight, "exp", axis=1, tiled=True),
    )
    resid_in = tokens.astype(f32)
    first_rms = rms_scale(resid_in)
    first_hat = resid_in * first_rms
    first_norm = (first_hat * first_gain).astype(bf16)
    seq_norm = gather_rows(first_norm)
    own_pos = half_index * half_len + jnp.arange(half_len, dtype=jnp.int32)
    query_pre = jnp.dot(seq_norm, full_query, preferred_element_type=f32).reshape(
        half_len, heads, HD
    )
    key_pre = jnp.dot(seq_norm, full_key, preferred_element_type=f32)
    value_rows = jnp.dot(seq_norm, full_value, preferred_element_type=f32).astype(bf16)
    cosine, sine = rotary_tables(own_pos, HD)
    query_rms = rms_scale(query_pre)
    query_hat = query_pre * query_rms
    query_rot = rotate(query_hat * query_gain, cosine[:, None, :], sine[:, None, :]).astype(bf16)
    key_rms = rms_scale(key_pre)
    key_hat = key_pre * key_rms
    key_rot = rotate(key_hat * key_gain, cosine, sine).astype(bf16)
    remote_key, remote_value = from_behind((key_rot, value_rows), "exp", 1)
    key_all = jnp.concatenate([remote_key, key_rot], axis=0)
    value_all = jnp.concatenate([remote_value, value_rows], axis=0)
    key_pos = jnp.concatenate([own_pos - half_len, own_pos], axis=0)
    key_usable = jnp.concatenate(
        [jnp.broadcast_to(half_index == 1, (half_len,)), jnp.ones((half_len,), bool)], axis=0
    )
    own_pieces = piece_ids(own_pos, starts)
    key_pieces = piece_ids(key_pos, starts)
    query_blocks = query_rot.reshape(block_count, block, heads, HD)
    block_index = jnp.arange(block_count, dtype=jnp.int32)

    def block_scores(query_blk, index_here):
        row_start = index_here * block
        rows_pos = half_index * half_len + row_start + jnp.arange(block, dtype=jnp.int32)
        mask = allowed_mask(rows_pos, key_pos, own_pieces, key_pieces) & key_usable[None, :]
        scores = jnp.einsum("qhd,kd->hqk", query_blk, key_all, preferred_element_type=f32) * scale
        return jnp.where(mask[None], scores, NEGATIVE)

    def forward_block(inputs):
        scores = block_scores(inputs[0], inputs[1])
        top_score = jnp.max(scores, axis=-1, keepdims=True)
        expo = jnp.exp(scores - top_score)
        total = jnp.sum(expo, axis=-1, keepdims=True)
        probs_low = (expo / total).astype(bf16)
        context = jnp.einsum("hqk,kd->qhd", probs_low, value_all, preferred_element_type=f32)
        return (context.astype(bf16), (top_score + jnp.log(total))[..., 0])

    contexts, log_norm = lax.map(forward_block, (query_blocks, block_index))
    context_rows = contexts.reshape(half_len, heads * HD)
    attention = sum_rows(jnp.dot(context_rows, full_output, preferred_element_type=f32))
    resid_mid = resid_in + attention
    second_rms = rms_scale(resid_mid)
    second_hat = resid_mid * second_rms
    second_norm = (second_hat * second_gain).astype(bf16)
    logits = jnp.dot(second_norm, router_weight, preferred_element_type=f32)
    expert_axis = jnp.arange(experts, dtype=jnp.int32)
    onehot = expert_ids[:, :, None] == expert_axis[None, None, :]
    chosen = jnp.sum(jnp.where(onehot, logits[:, None, :], 0.0), axis=2)
    mix = jax.nn.softmax(chosen, axis=-1)
    member = jnp.any(onehot, axis=1).astype(bf16)
    order_here = router_order[0]
    earlier = (order_here[None, :] < order_here[:, None]).astype(bf16)
    counts = jnp.dot(earlier, member, preferred_element_type=f32)
    slots = jnp.sum(jnp.where(onehot, counts[:, None, :], 0.0), axis=2).astype(jnp.int32)
    keep = slots < capacity
    total_slots = experts * capacity
    dest = jnp.where(keep, expert_ids * capacity + slots, total_slots)
    flat_dest = dest.reshape(-1)
    token_index = jnp.broadcast_to(
        jnp.arange(tok_dev, dtype=jnp.int32)[:, None], (tok_dev, TOP)
    ).reshape(-1)
    pair_index = jnp.arange(tok_dev * TOP, dtype=jnp.int32)
    slot_token = (
        jnp.full((total_slots,), tok_dev, jnp.int32).at[flat_dest].set(token_index, mode="drop")
    )
    slot_pair = (
        jnp.full((total_slots,), tok_dev * TOP, jnp.int32)
        .at[flat_dest]
        .set(pair_index, mode="drop")
    )
    padded_norm = jnp.concatenate([second_norm, jnp.zeros((1, width), bf16)], axis=0)
    send_rows = padded_norm[slot_token].reshape(experts, capacity, width)
    arrived = route_rows(send_rows).reshape(total_slots, width)
    gate_val = jnp.dot(arrived, gate_weight[0], preferred_element_type=f32)
    up_val = jnp.dot(arrived, up_weight[0], preferred_element_type=f32)
    gate_sig = jax.nn.sigmoid(gate_val)
    gate_act = gate_val * gate_sig
    inner = (gate_act * up_val).astype(bf16)
    result = jnp.dot(inner, down_weight[0], preferred_element_type=f32).astype(bf16)
    returned = route_rows(result.reshape(experts, capacity, width)).reshape(total_slots, width)
    padded_back = jnp.concatenate([returned, jnp.zeros((1, width), bf16)], axis=0)
    per_pair = padded_back[dest]
    keep_mix = jnp.where(keep, mix, 0.0)
    mixture = jnp.sum(keep_mix[:, :, None] * per_pair.astype(f32), axis=1)
    block_out = (resid_mid + mixture).astype(bf16)
    grad_out = out_grad.astype(f32)
    mix_grad = jnp.sum(grad_out[:, None, :] * per_pair.astype(f32), axis=2)
    pair_grad = (keep_mix[:, :, None] * grad_out[:, None, :]).astype(bf16)
    padded_pair = jnp.concatenate(
        [pair_grad.reshape(tok_dev * TOP, width), jnp.zeros((1, width), bf16)], axis=0
    )
    send_grad = padded_pair[slot_pair].reshape(experts, capacity, width)
    arrived_grad = route_rows(send_grad).reshape(total_slots, width)
    inner_grad = jnp.dot(arrived_grad, down_weight[0].T, preferred_element_type=f32)
    down_grad = jnp.dot(inner.T, arrived_grad, preferred_element_type=f32)[None]
    gate_back = (inner_grad * up_val * gate_sig * (1.0 + gate_val * (1.0 - gate_sig))).astype(bf16)
    up_back = (inner_grad * gate_act).astype(bf16)
    gate_grad = jnp.dot(arrived.T, gate_back, preferred_element_type=f32)[None]
    up_grad = jnp.dot(arrived.T, up_back, preferred_element_type=f32)[None]
    pair_back = jnp.dot(gate_back, gate_weight[0].T, preferred_element_type=f32) + jnp.dot(
        up_back, up_weight[0].T, preferred_element_type=f32
    )
    returned_grad = route_rows(pair_back.astype(bf16).reshape(experts, capacity, width)).reshape(
        total_slots, width
    )
    padded_grad = jnp.concatenate([returned_grad, jnp.zeros((1, width), bf16)], axis=0)
    pairs_sum = jnp.sum(padded_grad[dest].astype(f32), axis=1)
    chosen_grad = mix * (mix_grad - jnp.sum(mix * mix_grad, axis=1, keepdims=True))
    logit_grad = jnp.sum(jnp.where(onehot, chosen_grad[:, :, None], 0.0), axis=1).astype(bf16)
    router_part = jnp.dot(second_norm.T, logit_grad, preferred_element_type=f32)
    norm2_back = pairs_sum + jnp.dot(logit_grad, router_weight.T, preferred_element_type=f32)
    mid_from_norm, second_gain_part = norm_back(norm2_back, second_hat, second_rms, second_gain)
    middle_grad = grad_out + mid_from_norm
    back_query, back_key, back_value, back_output = (full_query, full_key, full_value, full_output)
    seq_grad = gather_rows(middle_grad.astype(bf16))
    output_part = jnp.dot(context_rows.T, seq_grad, preferred_element_type=f32)
    context_back = jnp.dot(seq_grad, back_output.T, preferred_element_type=f32).astype(bf16)
    context_blocks = context_back.reshape(block_count, block, heads, HD)

    def backward_block(carry, inputs):
        key_acc, value_acc = carry
        query_blk, grad_blk, norm_blk, index_here = inputs
        scores = block_scores(query_blk, index_here)
        probs = jnp.exp(scores - norm_blk[..., None])
        probs_low = probs.astype(bf16)
        value_acc = value_acc + jnp.einsum(
            "hqk,qhd->kd", probs_low, grad_blk, preferred_element_type=f32
        )
        probs_back = jnp.einsum("qhd,kd->hqk", grad_blk, value_all, preferred_element_type=f32)
        delta = jnp.sum(probs * probs_back, axis=-1, keepdims=True)
        score_back = (probs * (probs_back - delta)).astype(bf16)
        query_part = (
            jnp.einsum("hqk,kd->qhd", score_back, key_all, preferred_element_type=f32) * scale
        )
        key_acc = (
            key_acc
            + jnp.einsum("hqk,qhd->kd", score_back, query_blk, preferred_element_type=f32) * scale
        )
        return ((key_acc, value_acc), query_part)

    start_acc = (jnp.zeros((2 * half_len, HD), f32), jnp.zeros((2 * half_len, HD), f32))
    accums, rot_query_back = lax.scan(
        backward_block, start_acc, (query_blocks, context_blocks, log_norm, block_index)
    )
    key_acc, value_acc = accums
    came_key, came_value = (
        from_behind(key_acc[:half_len].astype(jnp.bfloat16), "exp", -1).astype(jnp.float32),
        from_behind(value_acc[:half_len].astype(jnp.bfloat16), "exp", -1).astype(jnp.float32),
    )
    take_remote = half_index == 0
    rot_key_back = key_acc[half_len:] + jnp.where(take_remote, came_key, 0.0)
    value_back = value_acc[half_len:] + jnp.where(take_remote, came_value, 0.0)
    rot_query_back = rot_query_back.reshape(half_len, heads, HD)
    query_gained = unrotate(rot_query_back, cosine[:, None, :], sine[:, None, :])
    query_back, query_gain_part = norm_back(query_gained, query_hat, query_rms, query_gain)
    key_gained = unrotate(rot_key_back, cosine, sine)
    key_back, key_gain_part = norm_back(key_gained, key_hat, key_rms, key_gain)
    query_back = query_back.reshape(half_len, heads * HD).astype(bf16)
    key_back = key_back.astype(bf16)
    value_back = value_back.astype(bf16)
    query_part = jnp.dot(seq_norm.T, query_back, preferred_element_type=f32)
    key_part = jnp.dot(seq_norm.T, key_back, preferred_element_type=f32)
    value_part = jnp.dot(seq_norm.T, value_back, preferred_element_type=f32)
    norm1_seq = jnp.dot(query_back, back_query.T, preferred_element_type=f32)
    norm1_seq = norm1_seq + jnp.dot(key_back, back_key.T, preferred_element_type=f32)
    norm1_seq = norm1_seq + jnp.dot(value_back, back_value.T, preferred_element_type=f32)
    norm1_back = sum_rows(norm1_seq)
    tok_from_norm, first_gain_part = norm_back(norm1_back, first_hat, first_rms, first_gain)
    tokens_grad = middle_grad + tok_from_norm
    query_grad, key_grad, value_grad, output_grad = (
        lax.psum_scatter(
            query_part.astype(jnp.bfloat16), "exp", scatter_dimension=0, tiled=True
        ).astype(jnp.float32),
        lax.psum_scatter(
            key_part.astype(jnp.bfloat16), "exp", scatter_dimension=0, tiled=True
        ).astype(jnp.float32),
        lax.psum_scatter(
            value_part.astype(jnp.bfloat16), "exp", scatter_dimension=0, tiled=True
        ).astype(jnp.float32),
        lax.psum_scatter(
            output_part.astype(jnp.bfloat16), "exp", scatter_dimension=1, tiled=True
        ).astype(jnp.float32),
    )
    first_gain_grad, second_gain_grad, query_gain_grad, key_gain_grad, router_grad = lax.psum(
        (first_gain_part, second_gain_part, query_gain_part, key_gain_part, router_part),
        ("exp", "tp"),
    )
    return (
        block_out,
        tokens_grad,
        first_gain_grad,
        second_gain_grad,
        query_gain_grad,
        key_gain_grad,
        query_grad,
        key_grad,
        value_grad,
        output_grad,
        router_grad,
        gate_grad,
        up_grad,
        down_grad,
    )


def solution(mesh):
    in_specs = (
        P(("exp", "tp"), None),
        P(("exp", "tp"), None),
        P(),
        P(),
        P(),
        P(),
        P("exp", "tp"),
        P("exp", "tp"),
        P("exp", "tp"),
        P("tp", "exp"),
        P(),
        P(("exp", "tp"), None, None),
        P(("exp", "tp"), None, None),
        P(("exp", "tp"), None, None),
        P(("exp", "tp"), None),
        P(("exp", "tp"), None),
        P(),
    )
    out_specs = (
        P(("exp", "tp"), None),
        P(("exp", "tp"), None),
        P(),
        P(),
        P(),
        P(),
        P("exp", "tp"),
        P("exp", "tp"),
        P("exp", "tp"),
        P("tp", "exp"),
        P(),
        P(("exp", "tp"), None, None),
        P(("exp", "tp"), None, None),
        P(("exp", "tp"), None, None),
    )
    return jax.shard_map(local, mesh=mesh, in_specs=in_specs, out_specs=out_specs, check_vma=False)
```

profile of v0, /device:TPU:8, one launch (start us, length us, event | category | flops | bytes accessed | tf_op | source)
XLA Modules:
  0.0 1394.8 jit_solution(3036712145099953546)
XLA Ops:
  12.9 31.2 %all_gather.20 = bf16[2048,128]{1,0:T(8,128)(2,1)} all-gather(bf16[256,128]{1,0:T(8,128)(2,1)} %param.24), channel_id=1, replica_groups=mesh['exp'=8,'tp'=4] {'exp'}, dimensions={0}, use_global_device_ids=true | all-gather | bytes 589824 | tf_op jit(solution)/shard_map/all_gather | solution.py:119
  44.5 34.8 %all_gather.19 = bf16[2048,128]{1,0:T(8,128)(2,1)} all-gather(bf16[256,128]{1,0:T(8,128)(2,1)S(1)} %copy-done.45), channel_id=1, replica_groups=mesh['exp'=8,'tp'=4] {'exp'}, dimensions={0}, use_global_device_ids=true | all-gather | bytes 589824 | tf_op jit(solution)/shard_map/all_gather | solution.py:120
  89.2 3.8 collective-permute-start.1
  98.0 20.6 %all-gather.7.cloned.1.call-done = bf16[2048,1024]{1,0:T(8,128)(2,1)} async-done(((bf16[256,1024]{1,0:T(8,128)(2,1)}), bf16[2048,1024]{1,0:T(8,128)(2,1)}) %all-gather.7.cloned.1.call-update) | async-done | bytes 4194320 | tf_op jit(solution)/shard_map/all_gather | solution.py:118
  118.6 5.1 fusion.92
  131.7 8.8 fusion.91
  140.6 8.1 fusion.3
  149.3 10.2 fusion.32
  159.5 34.1 %all-gather.9.cloned.1.call-done = bf16[1024,2048]{1,0:T(8,128)(2,1)} async-done(((bf16[1024,256]{1,0:T(8,128)(2,1)}), bf16[1024,2048]{1,0:T(8,128)(2,1)}) %all-gather.9.cloned.1.call-update) | async-done | bytes 4194320 | tf_op jit(solution)/shard_map/all_gather | solution.py:121
  193.6 6.9 fusion.93
  201.4 43.8 %reduce-scatter.7.cloned.1.call-done = f32[128,2048]{1,0:T(8,128)} async-done(((f32[512,2048]{1,0:T(8,128)}), f32[128,2048]{1,0:T(8,128)}) %reduce-scatter.7.cloned.1.call-update) | async-done | bytes 1048592 | tf_op jit(solution)/shard_map/reduce_scatter | solution.py:77
  251.2 4.3 scatter_custom_fusion
  255.5 12.0 gather_fusion
  267.5 7.2 reshape.447
  274.7 4.9 all-to-all-start
  286.3 4.3 scatter_custom_fusion.1
  290.7 13.4 gather_fusion.2
  304.0 7.2 reshape.451
  311.2 81.8 %all-to-all-done = bf16[32,36,2048]{2,1,0:T(8,128)(2,1)} async-done(((bf16[32,36,2048]{2,1,0:T(8,128)(2,1)}), bf16[32,36,2048]{2,1,0:T(8,128)(2,1)}, u32[]{:S(2)}, u32[]{:S(2)}) %all-to-all-start) | async-done | bytes 4718624 | tf_op jit(solution)/shard_map/all_to_all | solution.py:81
  393.0 7.6 all-to-all-start.2
  400.6 7.2 reshape.448
  407.8 9.1 fusion.17
  417.0 5.7 fusion.21
  422.6 91.1 %all-to-all-done.2 = bf16[32,36,2048]{2,1,0:T(8,128)(2,1)} async-done(((bf16[32,36,2048]{2,1,0:T(8,128)(2,1)}), bf16[32,36,2048]{2,1,0:T(8,128)(2,1)}, u32[]{:S(2)}, u32[]{:S(2)}) %all-to-all-start.2) | async-done | bytes 4718624 | tf_op jit(solution)/shard_map/all_to_all | solution.py:81
  513.7 7.2 reshape.452
  520.9 9.9 multiply_convert_fusion
  532.1 5.4 convolution_convert_fusion
  537.5 7.2 reshape.449
  544.7 7.6 all-to-all-start.1
  552.3 5.5 fusion.19
  557.9 5.6 add_convert_fusion
  563.5 7.2 reshape.453
  570.7 94.7 %all-to-all-done.1 = bf16[32,36,2048]{2,1,0:T(8,128)(2,1)} async-done(((bf16[32,36,2048]{2,1,0:T(8,128)(2,1)}), bf16[32,36,2048]{2,1,0:T(8,128)(2,1)}, u32[]{:S(2)}, u32[]{:S(2)}) %all-to-all-start.1) | async-done | bytes 4718624 | tf_op jit(solution)/shard_map/all_to_all | solution.py:81
  665.4 7.2 all-to-all-start.3
  672.8 7.2 reshape.450
  680.1 5.3 concatenate.47
  685.3 11.9 gather_fusion.1
  697.2 5.8 fusion.6
  703.2 82.8 %all-to-all-done.3 = bf16[32,36,2048]{2,1,0:T(8,128)(2,1)} async-done(((bf16[32,36,2048]{2,1,0:T(8,128)(2,1)}), bf16[32,36,2048]{2,1,0:T(8,128)(2,1)}, u32[]{:S(2)}, u32[]{:S(2)}) %all-to-all-start.3) | async-done | bytes 4718624 | tf_op jit(solution)/shard_map/all_to_all | solution.py:81
  785.9 7.2 reshape.454
  793.1 5.3 concatenate.49
  798.4 11.8 gather_fusion.3
  810.2 5.2 convert_reduce_fusion
  817.6 24.4 %all-gather.11.cloned.1.call-done = bf16[512,2048]{1,0:T(8,128)(2,1)} async-done(((bf16[128,2048]{1,0:T(8,128)(2,1)}), bf16[512,2048]{1,0:T(8,128)(2,1)}) %all-gather.11.cloned.1.call-update) | async-done | bytes 2097168 | tf_op jit(solution)/shard_map/all_gather | solution.py:73
  842.0 5.2 fusion.33
  847.2 7.3 fusion.34
  854.6 3.4 collective-permute-start.3
  857.9 10.9 fusion
  868.8 12.4 fusion.2
  888.0 4.3 multiply_bitcast_fusion
  906.8 4.4 convolution_convert_fusion.2
  912.4 5.9 convolution_convert_fusion.1
  919.5 4.6 fusion.95
  929.4 8.7 convolution_bitcast_fusion
  938.1 8.6 convolution_bitcast_fusion.1
  946.7 6.3 convolution_bitcast_fusion.2
  954.0 7.0 reduce-scatter.15.cloned.1.call-done
  962.5 62.8 %reduce-scatter.13.cloned.1.call-done = bf16[256,128]{1,0:T(8,128)(2,1)} async-done(((bf16[2048,128]{1,0:T(8,128)(2,1)}), bf16[256,128]{1,0:T(8,128)(2,1)}) %reduce-scatter.13.cloned.1.call-update) | async-done | bytes 65552 | tf_op jit(solution)/shard_map/reduce_scatter | solution.py:305
  1026.8 90.0 %reduce-scatter.11.cloned.1.call-done = bf16[256,1024]{1,0:T(8,128)(2,1)} async-done(((bf16[2048,1024]{1,0:T(8,128)(2,1)}), bf16[256,1024]{1,0:T(8,128)(2,1)}) %reduce-scatter.11.cloned.1.call-update) | async-done | bytes 524304 | tf_op jit(solution)/shard_map/reduce_scatter | solution.py:302
  1118.9 89.8 %reduce-scatter.17.cloned.1.call-done = bf16[1024,256]{1,0:T(8,128)(2,1)} async-done(((bf16[1024,2048]{1,0:T(8,128)(2,1)}), bf16[1024,256]{1,0:T(8,128)(2,1)}) %reduce-scatter.17.cloned.1.call-update) | async-done | bytes 524304 | tf_op jit(solution)/shard_map/reduce_scatter | solution.py:311
  1210.8 44.5 %reduce-scatter.9.cloned.1.call-done = f32[128,2048]{1,0:T(8,128)} async-done(((f32[512,2048]{1,0:T(8,128)}), f32[128,2048]{1,0:T(8,128)}) %reduce-scatter.9.cloned.1.call-update) | async-done | bytes 1048592 | tf_op jit(solution)/shard_map/reduce_scatter | solution.py:77
  1256.9 4.2 fusion.42
  1261.1 39.7 %all-reduce.5 = (f32[2048]{0:T(1024)}, f32[2048]{0:T(1024)}, f32[128]{0:T(128)}, f32[128]{0:T(128)}) all-reduce(f32[2048]{0:T(1024)S(1)} %get-tuple-element.79, f32[2048]{0:T(1024)S(1)} %get-tuple-element.77, f32[128]{0:T(128)S(1)} %bitcast_reduce_fusion, f32[128]{0:T(128)S(1)} %get-tuple-element.81), channel_id=1, replica_groups=mesh['exp'=8,'tp'=4] {'exp','tp'}, use_global_device_ids=true, to_apply=%region_28.29 | all-reduce | flops 4352 | bytes 34816 | tf_op jit(solution)/shard_map/psum | solution.py:315
  1300.9 85.5 %all-reduce.8.cloned.1.call-done = f32[2048,32]{0,1:T(8,128)} async-done(((f32[2048,32]{0,1:T(8,128)}), f32[2048,32]{0,1:T(8,128)}) %all-reduce.8.cloned.1.call-update) | async-done | bytes 262160 | tf_op jit(solution)/shard_map/psum | solution.py:315
  (276 shorter events, 86.6 us)
Async XLA Ops:
  7.2 513.7 %copy-start = (bf16[1,768,2048]{2,1,0:T(8,128)(2,1)S(1)}, bf16[1,768,2048]{2,1,0:T(8,128)(2,1)}, u32[]{:S(2)}) copy-start(bf16[1,768,2048]{2,1,0:T(8,128)(2,1)} %param.30) | copy-start | bytes 9437188
  7.2 36.9 %copy-start.62 = (s32[4,2]{0,1:T(2,128)S(1)}, s32[4,2]{0,1:T(2,128)}, u32[]{:S(2)}) copy-start(s32[4,2]{0,1:T(2,128)} %param.33) | copy-start | bytes 100
  7.2 37.3 %copy-start.45 = (bf16[256,128]{1,0:T(8,128)(2,1)S(1)}, bf16[256,128]{1,0:T(8,128)(2,1)}, u32[]{:S(2)}) copy-start(bf16[256,128]{1,0:T(8,128)(2,1)} %param.25) | copy-start | bytes 196612
  7.2 73.8 %all-gather.5.cloned.1.call-start = ((), (), s32[]{:S(2)}) async-start(), calls=%async_computation.10 | async-start | bytes 2621440 | tf_op jit(solution)/shard_map/all_gather | solution.py:73
  9.2 74.9 %copy-start.58 = (f32[128]{0:T(128)S(1)}, f32[128]{0:T(128)}, u32[]{:S(2)}) copy-start(f32[128]{0:T(128)} %param.22) | copy-start | bytes 1540
  11.3 107.3 %all-gather.7.cloned.1.call-start = ((), (), s32[]{:S(2)}) async-start(), calls=%async_computation.11 | async-start | bytes 4718592 | tf_op jit(solution)/shard_map/all_gather | solution.py:118
  12.0 181.5 %all-gather.9.cloned.1.call-start = ((), (), s32[]{:S(2)}) async-start(), calls=%async_computation.12 | async-start | bytes 4718592 | tf_op jit(solution)/shard_map/all_gather | solution.py:121
  12.8 232.4 %reduce-scatter.7.cloned.1.call-start = ((), (), s32[]{:S(2)}) async-start(), calls=%async_computation.13 | async-start | bytes 5242880 | tf_op jit(solution)/shard_map/reduce_scatter | solution.py:77
  12.9 72.7 %copy-start.51 = (f32[512]{0:T(512)}, f32[512]{0:T(512)S(1)}, u32[]{:S(2)}) copy-start(f32[512]{0:T(512)S(1)} %get-tuple-element.135) | copy-start | bytes 6148
  44.5 41.1 %copy-start.60 = (f32[64]{0:T(128)}, f32[64]{0:T(128)S(1)}, u32[]{:S(2)}) copy-start(f32[64]{0:T(128)S(1)} %negate_power_fusion) | copy-start | bytes 772
  85.5 46.0 %copy-start.30 = (bf16[512,64]{0,1:T(8,128)(2,1)}, bf16[512,64]{0,1:T(8,128)(2,1)S(1)}, u32[]{:S(2)}) copy-start(bf16[512,64]{0,1:T(8,128)(2,1)S(1)} %get-tuple-element.124) | copy-start | bytes 196612
  85.6 46.0 %copy-start.32 = (bf16[512,64]{0,1:T(8,128)(2,1)}, bf16[512,64]{0,1:T(8,128)(2,1)S(1)}, u32[]{:S(2)}) copy-start(bf16[512,64]{0,1:T(8,128)(2,1)S(1)} %get-tuple-element.125) | copy-start | bytes 196612
  86.6 44.0 %copy-start.25 = (f32[512,64]{1,0:T(8,128)}, f32[512,64]{1,0:T(8,128)S(1)}, u32[]{:S(2)}) copy-start(f32[512,64]{1,0:T(8,128)S(1)} %copy.151) | copy-start | bytes 393220
  89.2 42.3 %collective-permute-start.1 = (bf16[512,128]{0,1:T(8,128)(2,1)}, bf16[512,128]{0,1:T(8,128)(2,1)}, u32[]{:S(2)}, u32[]{:S(2)}) collective-permute-start(bf16[512,128]{0,1:T(8,128)(2,1)} %pad_maximum_fusion.5), channel_id=1, source_target_pairs={{0,4},{4,8},{8,12},{12,16},{16,20},{20,24},{24,28},{1,5},{5,9},{9,... | collective-permute-start | bytes 393224 | tf_op jit(solution)/shard_map/ppermute | solution.py:19
  96.1 52.7 %collective-permute-start = (bf16[512,128]{1,0:T(8,128)(2,1)}, bf16[512,128]{1,0:T(8,128)(2,1)}, u32[]{:S(2)}, u32[]{:S(2)}) collective-permute-start(bf16[512,128]{1,0:T(8,128)(2,1)} %convolution_convert_fusion.6), channel_id=1, source_target_pairs={{0,4},{4,8},{8,12},{12,16},{16,20},{20,24},{24,28},{1,5},{5,9},{9,... | collective-permute-start | bytes 393224 | tf_op jit(solution)/shard_map/ppermute | solution.py:19
  131.5 9.1 copy-start.9
  131.5 9.1 copy-start.11
  140.6 8.1 copy-start.40
  200.5 47.3 %copy-start.42 = (f32[2048]{0:T(1024)S(1)}, f32[2048]{0:T(1024)}, u32[]{:S(2)}) copy-start(f32[2048]{0:T(1024)} %param.20) | copy-start | bytes 24580
  200.5 48.2 %copy-start.36 = (bf16[2048,32]{0,1:T(8,128)(2,1)S(1)}, bf16[2048,32]{0,1:T(8,128)(2,1)}, u32[]{:S(2)}) copy-start(bf16[2048,32]{0,1:T(8,128)(2,1)} %param.27) | copy-start | bytes 393220
  274.7 118.3 %all-to-all-start = ((bf16[32,36,2048]{2,1,0:T(8,128)(2,1)}), bf16[32,36,2048]{2,1,0:T(8,128)(2,1)}, u32[]{:S(2)}, u32[]{:S(2)}) async-start(bf16[32,36,2048]{2,1,0:T(8,128)(2,1)} %reshape.447), calls=%async_computation.1 | async-start | bytes 10485760 | tf_op jit(solution)/shard_map/all_to_all | solution.py:81
  393.0 120.7 %all-to-all-start.2 = ((bf16[32,36,2048]{2,1,0:T(8,128)(2,1)}), bf16[32,36,2048]{2,1,0:T(8,128)(2,1)}, u32[]{:S(2)}, u32[]{:S(2)}) async-start(bf16[32,36,2048]{2,1,0:T(8,128)(2,1)} %reshape.451), calls=%async_computation.3 | async-start | bytes 10485760 | tf_op jit(solution)/shard_map/all_to_all | solution.py:81
  407.8 9.1 copy-start.20
  407.8 9.1 copy-start.63
  544.7 7.6 copy-start.64
  544.7 120.7 %all-to-all-start.1 = ((bf16[32,36,2048]{2,1,0:T(8,128)(2,1)}), bf16[32,36,2048]{2,1,0:T(8,128)(2,1)}, u32[]{:S(2)}, u32[]{:S(2)}) async-start(bf16[32,36,2048]{2,1,0:T(8,128)(2,1)} %reshape.449), calls=%async_computation.2 | async-start | bytes 10485760 | tf_op jit(solution)/shard_map/all_to_all | solution.py:81
  552.3 5.6 copy-start.65
  552.3 5.6 copy-start.70
  665.4 120.5 %all-to-all-start.3 = ((bf16[32,36,2048]{2,1,0:T(8,128)(2,1)}), bf16[32,36,2048]{2,1,0:T(8,128)(2,1)}, u32[]{:S(2)}, u32[]{:S(2)}) async-start(bf16[32,36,2048]{2,1,0:T(8,128)(2,1)} %reshape.453), calls=%async_computation.4 | async-start | bytes 10485760 | tf_op jit(solution)/shard_map/all_to_all | solution.py:81
  672.6 169.4 %all-gather.11.cloned.1.call-start = ((), (), s32[]{:S(2)}) async-start(), calls=%async_computation.14 | async-start | bytes 2621440 | tf_op jit(solution)/shard_map/all_gather | solution.py:73
  685.3 11.9 copy-start.14
  810.2 5.2 copy-start.7
  810.2 5.2 copy-start.37
  810.2 5.2 copy-start.43
  810.2 5.2 copy-start.54
  810.2 5.8 copy-start.19
  816.0 31.2 %copy-start.13 = (f32[128,2048]{1,0:T(8,128)}, f32[128,2048]{1,0:T(8,128)S(1)}, u32[]{:S(2)}) copy-start(f32[128,2048]{1,0:T(8,128)S(1)} %get-tuple-element.132) | copy-start | bytes 3145732
  817.2 143.8 %reduce-scatter.15.cloned.1.call-start = ((), (), s32[]{:S(2)}) async-start(), calls=%async_computation.18 | async-start | bytes 589824 | tf_op jit(solution)/shard_map/reduce_scatter | solution.py:308
  854.6 42.1 %collective-permute-start.3 = (bf16[512,128]{0,1:T(8,128)(2,1)S(1)}, bf16[512,128]{0,1:T(8,128)(2,1)S(1)}, u32[]{:S(2)}, u32[]{:S(2)}) collective-permute-start(bf16[512,128]{0,1:T(8,128)(2,1)S(1)} %slice.92), channel_id=1, source_target_pairs={{4,0},{8,4},{12,8},{16,12},{20,16},{24,20},{28,24},{5,1},{9,5},{13... | collective-permute-start | bytes 393224 | tf_op jit(solution)/shard_map/ppermute | solution.py:19
  868.8 12.4 copy-start.10
  868.8 12.4 copy-start.12
  881.3 6.7 copy-start.31
  881.3 6.7 copy-start.33
  885.0 7.3 copy-start.26
  885.0 7.3 copy-start.28
  885.0 13.4 collective-permute-start.2
  896.7 3.3 copy-start.23
  896.7 3.3 copy-start.50
  896.7 3.3 copy-start.59
  898.3 127.0 %reduce-scatter.13.cloned.1.call-start = ((), (), s32[]{:S(2)}) async-start(), calls=%async_computation.17 | async-start | bytes 589824 | tf_op jit(solution)/shard_map/reduce_scatter | solution.py:305
  901.8 215.0 %reduce-scatter.11.cloned.1.call-start = ((), (), s32[]{:S(2)}) async-start(), calls=%async_computation.16 | async-start | bytes 4718592 | tf_op jit(solution)/shard_map/reduce_scatter | solution.py:302
  911.2 297.5 %reduce-scatter.17.cloned.1.call-start = ((), (), s32[]{:S(2)}) async-start(), calls=%async_computation.19 | async-start | bytes 4718592 | tf_op jit(solution)/shard_map/reduce_scatter | solution.py:311
  918.3 5.8 copy-start.18
  918.3 336.9 %reduce-scatter.9.cloned.1.call-start = ((), (), s32[]{:S(2)}) async-start(), calls=%async_computation.15 | async-start | bytes 5242880 | tf_op jit(solution)/shard_map/reduce_scatter | solution.py:77
  928.0 458.4 %all-reduce.8.cloned.1.call-start = ((), (), s32[]{:S(2)}) async-start(), calls=%async_computation.20 | async-start | bytes 524288 | tf_op jit(solution)/shard_map/psum | solution.py:315
  929.4 8.7 copy-start.71
  929.4 17.2 %slice-start = ((s8[4718592]{0:T(1024)(128)(4,1)}), s8[4194304]{0:T(1024)(128)(4,1)S(1)}, s32[]{:S(2)}) async-start(s8[4718592]{0:T(1024)(128)(4,1)} %bitcast.175), calls=%async_computation.21 | async-start | bytes 8388608
  938.1 8.6 slice-start.1
  938.1 8.6 copy-start.69
  946.7 6.3 copy-start.16
  953.0 302.3 %copy-start.8 = (bf16[128,2048]{1,0:T(8,128)(2,1)S(1)}, bf16[128,2048]{1,0:T(8,128)(2,1)}, u32[]{:S(2)}) copy-start(bf16[128,2048]{1,0:T(8,128)(2,1)} %param.17) | copy-start | bytes 1572868
  953.0 302.3 %copy-start.44 = (f32[2048]{0:T(1024)S(1)}, f32[2048]{0:T(1024)}, u32[]{:S(2)}) copy-start(f32[2048]{0:T(1024)} %param.19) | copy-start | bytes 24580
  953.0 302.3 %copy-start.56 = (f32[128]{0:T(128)S(1)}, f32[128]{0:T(128)}, u32[]{:S(2)}) copy-start(f32[128]{0:T(128)} %copy-done.55) | copy-start | bytes 1540
  1256.9 131.1 %copy-start.1 = (bf16[1,768,2048]{2,1,0:T(8,128)(2,1)S(1)}, bf16[1,768,2048]{2,1,0:T(8,128)(2,1)}, u32[]{:S(2)}) copy-start(bf16[1,768,2048]{2,1,0:T(8,128)(2,1)} %param.30) | copy-start | bytes 9437188
  (29 other events, 43.0 us)
Sparse Core Ops, SparseCore 0:
  11.4 23.7 all-gather.4
  37.3 81.2 all-gather.6
  120.6 72.9 all-gather.8
  200.6 44.5 reduce-scatter.6
  817.3 24.6 all-gather.10
  898.5 62.4 reduce-scatter.14
  964.3 60.9 reduce-scatter.12
  1029.4 87.3 reduce-scatter.10
  1120.4 88.1 reduce-scatter.16
  1211.2 44.0 reduce-scatter.8
  1261.4 124.9 all-reduce.7
where the time goes:
time: 1400 us; the launch traced here: 1390 us
  waiting for transfers between devices  854 us (61%)
  matrix products  156 us (11%)
  local copies, waits for them, and re-layouts  153 us (11%)
  blocking collectives  106 us (8%)
  other arithmetic  70.5 us (5%)
  starting transfers between devices  40.5 us (3%)
  between operations  15.3 us (1%)
    all_to_all x4, waiting for transfers between devices, route_rows(): lax.all_to_all(buffer, ('exp', 'tp'), split_axis=0, concat_axis=0, tiled=...  350 us
    reduce_scatter x1, waiting for transfers between devices, local(): lax.psum_scatter(query_part.astype(jnp.bfloat16), 'exp', scatter_dimensio...  90 us
    reduce_scatter x1, waiting for transfers between devices, local(): lax.psum_scatter(output_part.astype(jnp.bfloat16), 'exp', scatter_dimensi...  89.8 us
    reduce_scatter x2, waiting for transfers between devices, sum_rows(): return lax.psum_scatter(partial_rows, 'tp', scatter_dimension=0, tiled=True)  88.3 us
    psum x1, waiting for transfers between devices, local(): lax.psum((first_gain_part, second_gain_part, query_gain_part, key_gain_pa...  85.5 us
    reduce_scatter x1, waiting for transfers between devices, local(): lax.psum_scatter(key_part.astype(jnp.bfloat16), 'exp', scatter_dimension=...  62.8 us
    psum x1, blocking collectives, local(): lax.psum((first_gain_part, second_gain_part, query_gain_part, key_gain_pa...  39.7 us
    all_gather x1, blocking collectives, local(): lax.all_gather(value_weight, 'exp', axis=0, tiled=True)  34.8 us
  transfers between devices with their start and end apart: 19, of which 14 were waited for; matrix products, arithmetic and copies ran while one was open for 18% of the time, Pallas kernels for 0%

commit v1 on v0

v1 whole, which is shorter than its diff:
```python
import functools

import jax
import jax.numpy as jnp
from jax import lax
from jax.experimental import pallas as pl
from jax.experimental.pallas import tpu as pltpu
from jax.sharding import PartitionSpec as P

HD = 128
TOP = 8
IMG_LEN = 256
PLANE = 8

EPSILON = 1e-06
THETA = 1000000.0
NEGATIVE = -1e30

MESH = pl.DeviceIdType.MESH
f32 = jnp.float32
bf16 = jnp.bfloat16
VMEM_LIMIT = 60 << 20


def rms_scale(values):
    return lax.rsqrt(jnp.mean(values * values, axis=-1, keepdims=True) + EPSILON)


def rotary_tables(positions, width):
    half = width // 2
    freqs = THETA ** (-(jnp.arange(half, dtype=f32) * 2.0 / width))
    angles = positions.astype(f32)[:, None] * freqs[None, :]
    return (jnp.cos(angles), jnp.sin(angles))


def rotate(values, cosine, sine):
    half = values.shape[-1] // 2
    first = values[..., :half]
    second = values[..., half:]
    return jnp.concatenate(
        [first * cosine - second * sine, second * cosine + first * sine], axis=-1
    )


def unrotate(values, cosine, sine):
    half = values.shape[-1] // 2
    first = values[..., :half]
    second = values[..., half:]
    return jnp.concatenate(
        [first * cosine + second * sine, second * cosine - first * sine], axis=-1
    )


def piece_ids(positions, starts):
    inside = (positions[:, None] >= starts[None, :]) & (
        positions[:, None] < starts[None, :] + IMG_LEN
    )
    labels = jnp.arange(1, starts.shape[0] + 1, dtype=jnp.int32)
    return jnp.sum(jnp.where(inside, labels[None, :], 0), axis=1)


def allowed_mask(query_pos, key_pos, query_piece, key_piece):
    causal = key_pos[None, :] <= query_pos[:, None]
    same = (query_piece[:, None] == key_piece[None, :]) & (query_piece[:, None] > 0)
    return causal | same


def norm_back(grad_norm, hat, rms, gain):
    scaled = grad_norm * gain
    inner_mean = jnp.mean(scaled * hat, axis=-1, keepdims=True)
    lead_axes = tuple(range(grad_norm.ndim - 1))
    return (rms * (scaled - hat * inner_mean), jnp.sum(grad_norm * hat, axis=lead_axes))


class Place:
    def __init__(self):
        self.e = lax.axis_index("exp")
        self.t = lax.axis_index("tp")
        self.z = self.e // 2
        self.y = self.e % 2
        self.x = self.t // 2
        self.c = self.t % 2
        self.p = self.y * 4 + self.t

    def at(self, z, p):
        return (z * 2 + p // 4, p % 4)

    def flip(self, dy=0, dx=0, dc=0):
        y = 1 - self.y if dy else self.y
        x = 1 - self.x if dx else self.x
        c = 1 - self.c if dc else self.c
        return y * 4 + x * 2 + c

    def peer(self, dy=0, dx=0, dc=0):
        return self.at(self.z, self.flip(dy, dx, dc))

    def by(self, k):
        return self.flip((k >> 2) & 1, (k >> 1) & 1, k & 1)


class Sends:
    def __init__(self):
        self.kept = []

    def start(self, src, dst, send_sem, recv_sem, device, when=None):
        def make():
            return pltpu.make_async_remote_copy(
                src_ref=src,
                dst_ref=dst,
                send_sem=send_sem,
                recv_sem=recv_sem,
                device_id=device,
                device_id_type=MESH,
            )

        def go():
            make().start()

        if when is None:
            go()
        else:
            pl.when(when)(go)
        self.kept.append((make, when))

    def finish(self):
        for make, when in self.kept:
            if when is None:
                make().wait_send()
            else:
                pl.when(when)(lambda make=make: make().wait_send())
        self.kept = []


def arrived(dst, recv_sem, when=None):
    def go():
        pltpu.make_async_copy(dst, dst, recv_sem).wait()

    if when is None:
        go()
    else:
        pl.when(when)(go)


def greet(place, zn, ends=False, everyone=True, planes=True):
    bar = pltpu.get_barrier_semaphore()
    count = 0
    if planes:
        for k in range(1, PLANE):
            pl.semaphore_signal(
                bar, inc=1, device_id=place.at(place.z, place.by(k)), device_id_type=MESH
            )
        count += PLANE - 1
    if everyone:
        for k in range(1, zn):
            pl.semaphore_signal(
                bar,
                inc=1,
                device_id=place.at((place.z + k) % zn, place.p),
                device_id_type=MESH,
            )
        count += zn - 1
    pl.semaphore_wait(bar, count)
    if ends:
        bar2 = 0
        del bar2


class PlaneGather:
    sems = 8

    def __init__(self, place, sends, buf, ss, rs):
        self.place, self.sends, self.buf, self.ss, self.rs = place, sends, buf, ss, rs
        half = buf.shape[2] // 2
        self.cols_a = pl.ds(0, half)
        self.cols_b = pl.ds(half, half)

    def _send(self, block, which, device, cols=None):
        ref = self.buf.at[block] if cols is None else self.buf.at[block, :, cols]
        self.sends.start(ref, ref, self.ss.at[which], self.rs.at[which], device)

    def _wait(self, block, which, cols=None):
        ref = self.buf.at[block] if cols is None else self.buf.at[block, :, cols]
        arrived(ref, self.rs.at[which])

    def first(self):
        pc = self.place
        self._send(pc.p, 0, pc.peer(dy=1))
        self._send(pc.p, 1, pc.peer(dx=1))
        self._send(pc.p, 2, pc.peer(dc=1))

    def second(self):
        pc = self.place
        px, py = pc.flip(dx=1), pc.flip(dy=1)
        self._wait(px, 1)
        self._send(px, 3, pc.peer(dy=1), self.cols_a)
        self._send(px, 4, pc.peer(dc=1))
        self._wait(py, 0)
        self._send(py, 5, pc.peer(dx=1), self.cols_b)
        self._send(py, 6, pc.peer(dc=1))

    def third(self):
        pc = self.place
        pd = pc.flip(dy=1, dx=1)
        self._wait(pd, 3, self.cols_a)
        self._wait(pd, 5, self.cols_b)
        self._send(pd, 7, pc.peer(dc=1))

    def last(self):
        pc = self.place
        self._wait(pc.flip(dc=1), 2)
        self._wait(pc.flip(dc=1, dx=1), 4)
        self._wait(pc.flip(dc=1, dy=1), 6)
        self._wait(pc.flip(dc=1, dy=1, dx=1), 7)


def add_rows(dst, first, second, rows, step=32):
    def body(i, carry):
        at = pl.ds(pl.multiple_of(i * step, step), step)
        dst(at, first(at).astype(f32) + second(at).astype(f32))
        return carry

    lax.fori_loop(0, rows // step, body, 0)


class PlaneReduce:
    sems = 4 + 4 + 2

    @staticmethod
    def scratch(rows, width):
        return [
            pltpu.VMEM((4, rows, width), bf16),
            pltpu.VMEM((4, rows, width), bf16),
            pltpu.VMEM((2, rows, width // 2), bf16),
            pltpu.VMEM((2, rows, width // 2), bf16),
            pltpu.VMEM((2, rows, width // 2), bf16),
        ]

    def __init__(self, place, sends, part, out, scratch, ss, rs):
        self.place, self.sends, self.part, self.out = place, sends, part, out
        self.c1, self.s1, self.ra, self.rb, self.last = scratch
        self.ss, self.rs = ss, rs
        self.rows = part.shape[1]
        half = part.shape[2] // 2
        self.half = half
        self.cols_a = pl.ds(0, half)
        self.cols_b = pl.ds(half, half)
        pc = place
        self.chips = [(1, 1), (0, 1), (1, 0), (0, 0)]

    def _chip(self, dy, dx):
        pc = self.place
        y = 1 - pc.y if dy else pc.y
        x = 1 - pc.x if dx else pc.x
        return y, x, y * 2 + x

    def first(self, k):
        pc = self.place
        y, x, j = self._chip(*self.chips[k])
        block = y * 4 + x * 2 + (1 - pc.c)
        self.sends.start(
            self.part.at[block], self.c1.at[j], self.ss.at[k], self.rs.at[k], pc.peer(dc=1)
        )

    def second(self, k):
        pc = self.place
        y, x, j = self._chip(*self.chips[k])
        arrived(self.c1.at[j], self.rs.at[k])
        mine = y * 4 + x * 2 + pc.c

        def put(at, v):
            self.s1[j, at, :] = v.astype(bf16)

        add_rows(put, lambda at: self.part[mine, at, :], lambda at: self.c1[j, at, :], self.rows)
        dy, dx = self.chips[k]
        if dx:
            self.sends.start(
                self.s1.at[j, :, self.cols_a],
                self.ra.at[y],
                self.ss.at[4 + (0 if dy else 1)],
                self.rs.at[4 + (0 if dy else 1)],
                pc.peer(dx=1),
            )
        if dy:
            self.sends.start(
                self.s1.at[j, :, self.cols_b],
                self.rb.at[x],
                self.ss.at[6 + (0 if dx else 1)],
                self.rs.at[6 + (0 if dx else 1)],
                pc.peer(dy=1),
            )

    def third(self):
        pc = self.place
        other_y, other_x = 1 - pc.y, 1 - pc.x
        arrived(self.ra.at[other_y], self.rs.at[4])
        j = other_y * 2 + pc.x

        def put_a(at, v):
            self.ra[other_y, at, :] = v.astype(bf16)

        add_rows(
            put_a,
            lambda at: self.s1[j, at, self.cols_a],
            lambda at: self.ra[other_y, at, :],
            self.rows,
        )
        self.sends.start(
            self.ra.at[other_y], self.last.at[0], self.ss.at[8], self.rs.at[8], pc.peer(dy=1)
        )
        arrived(self.rb.at[other_x], self.rs.at[6])
        i = pc.y * 2 + other_x

        def put_b(at, v):
            self.rb[other_x, at, :] = v.astype(bf16)

        add_rows(
            put_b,
            lambda at: self.s1[i, at, self.cols_b],
            lambda at: self.rb[other_x, at, :],
            self.rows,
        )
        self.sends.start(
            self.rb.at[other_x], self.last.at[1], self.ss.at[9], self.rs.at[9], pc.peer(dx=1)
        )

    def finish(self):
        pc = self.place
        own = pc.y * 2 + pc.x
        arrived(self.ra.at[pc.y], self.rs.at[5])
        arrived(self.rb.at[pc.x], self.rs.at[7])

        def put_a(at, v):
            self.out[at, self.cols_a] = v + self.ra[pc.y, at, :].astype(f32)

        def put_b(at, v):
            self.out[at, self.cols_b] = v + self.rb[pc.x, at, :].astype(f32)

        arrived(self.last.at[0], self.rs.at[8])
        add_rows(
            put_a,
            lambda at: self.s1[own, at, self.cols_a],
            lambda at: self.last[0, at, :],
            self.rows,
        )
        arrived(self.last.at[1], self.rs.at[9])
        add_rows(
            put_b,
            lambda at: self.s1[own, at, self.cols_b],
            lambda at: self.last[1, at, :],
            self.rows,
        )


class ColumnGather:
    def __init__(self, place, sends, zn, pack, full, pair_ss, pair_rs, ss_r, ss_l, rs):
        self.place, self.sends, self.zn = place, sends, zn
        self.pack, self.full = pack, full
        self.pair_ss, self.pair_rs, self.ss_r, self.ss_l, self.rs = pair_ss, pair_rs, ss_r, ss_l, rs

    def _on(self, src, piece, right, left):
        pc = self.place
        if right is not None:
            self.sends.start(
                src,
                self.full.at[piece],
                self.ss_r.at[piece],
                self.rs.at[piece],
                pc.at(jnp.minimum(pc.z + 1, self.zn - 1), pc.p),
                right,
            )
        if left is not None:
            self.sends.start(
                src,
                self.full.at[piece],
                self.ss_l.at[piece],
                self.rs.at[piece],
                pc.at(jnp.maximum(pc.z - 1, 0), pc.p),
                left,
            )

    def pair(self):
        pc = self.place
        self.sends.start(
            self.pack.at[1 - pc.y],
            self.full.at[pc.e],
            self.pair_ss,
            self.pair_rs,
            pc.peer(dy=1),
        )

    def own(self):
        pc = self.place
        self._on(self.pack.at[pc.y], pc.e, pc.z < self.zn - 1, pc.z > 0)

    def keep(self):
        pc = self.place
        self.full[pc.e] = self.pack[pc.y]

    def partner(self):
        pc = self.place
        other = pc.z * 2 + 1 - pc.y
        arrived(self.full.at[other], self.pair_rs)
        self._on(self.full.at[other], other, pc.z < self.zn - 1, pc.z > 0)

    def step(self, k):
        pc = self.place
        for first in (True, False):
            y = pc.y if first else 1 - pc.y
            below = jnp.maximum(pc.z - k, 0) * 2 + y
            has = pc.z - k >= 0
            arrived(self.full.at[below], self.rs.at[below], has)
            self._on(
                self.full.at[below], below, jnp.logical_and(has, pc.z < self.zn - 1), None
            )
            above = jnp.minimum(pc.z + k, self.zn - 1) * 2 + y
            has = pc.z + k < self.zn
            arrived(self.full.at[above], self.rs.at[above], has)
            self._on(self.full.at[above], above, None, jnp.logical_and(has, pc.z > 0))


def open_kernel(zn, own_ref, pq_ref, po_ref, seq_ref, wq_ref, wo_ref, gs, gr, ps, pr, sr, sl, rs):
    place, sends = Place(), Sends()
    greet(place, zn)
    q = ColumnGather(
        place, sends, zn, pq_ref, wq_ref, ps.at[0], pr.at[0], sr.at[0], sl.at[0], rs.at[0]
    )
    o = ColumnGather(
        place, sends, zn, po_ref, wo_ref, ps.at[1], pr.at[1], sr.at[1], sl.at[1], rs.at[1]
    )
    q.pair()
    q.own()
    seq_ref[place.p] = own_ref[...]
    rows = PlaneGather(place, sends, seq_ref, gs, gr)
    rows.first()
    o.pair()
    q.keep()
    o.keep()
    q.partner()
    o.own()
    rows.second()
    o.partner()
    rows.third()
    for k in range(1, zn):
        q.step(k)
    for k in range(1, zn):
        o.step(k)
    rows.last()
    sends.finish()


def dma_sems(*shape):
    return pltpu.SemaphoreType.DMA(shape)


VSPEC = pl.BlockSpec(memory_space=pltpu.VMEM)
ASPEC = pl.BlockSpec(memory_space=pl.ANY)


def params(cid):
    return pltpu.CompilerParams(
        collective_id=cid, has_side_effects=True, vmem_limit_bytes=VMEM_LIMIT
    )


def open_gather(zn, own, pack_q, pack_o):
    rows, width = own.shape
    e = 2 * zn
    return pl.pallas_call(
        functools.partial(open_kernel, zn),
        out_shape=(
            jax.ShapeDtypeStruct((PLANE, rows, width), bf16),
            jax.ShapeDtypeStruct((e,) + pack_q.shape[1:], bf16),
            jax.ShapeDtypeStruct((e,) + pack_o.shape[1:], bf16),
        ),
        in_specs=[VSPEC] * 3,
        out_specs=(VSPEC,) * 3,
        scratch_shapes=[
            dma_sems(8),
            dma_sems(8),
            dma_sems(2),
            dma_sems(2),
            dma_sems(2, e),
            dma_sems(2, e),
            dma_sems(2, e),
        ],
        compiler_params=params(0),
        name="open_gather",
    )(own, pack_q, pack_o)


def rows_kernel(zn, own_ref, seq_ref, gs, gr):
    place, sends = Place(), Sends()
    greet(place, zn, everyone=False)
    seq_ref[place.p] = own_ref[...]
    rows = PlaneGather(place, sends, seq_ref, gs, gr)
    rows.first()
    rows.second()
    rows.third()
    rows.last()
    sends.finish()


def rows_gather(zn, own):
    rows, width = own.shape
    return pl.pallas_call(
        functools.partial(rows_kernel, zn),
        out_shape=jax.ShapeDtypeStruct((PLANE, rows, width), bf16),
        in_specs=[VSPEC],
        out_specs=VSPEC,
        scratch_shapes=[dma_sems(8), dma_sems(8)],
        compiler_params=params(1),
        name="rows_gather",
    )(own)


def rows_sum_kernel(zn, part_ref, out_ref, *rest):
    scratch, (ss, rs) = rest[:5], rest[5:]
    place, sends = Place(), Sends()
    greet(place, zn, everyone=False)
    red = PlaneReduce(place, sends, part_ref, out_ref, scratch, ss, rs)
    for k in range(4):
        red.first(k)
    for k in range(4):
        red.second(k)
    red.third()
    red.finish()
    sends.finish()


def rows_sum(zn, part):
    _, rows, width = part.shape
    return pl.pallas_call(
        functools.partial(rows_sum_kernel, zn),
        out_shape=jax.ShapeDtypeStruct((rows, width), f32),
        in_specs=[VSPEC],
        out_specs=VSPEC,
        scratch_shapes=PlaneReduce.scratch(rows, width) + [dma_sems(10), dma_sems(10)],
        compiler_params=params(2),
        name="rows_sum",
    )(part)


def send_kernel(
    zn, cap, chunk, norm_ref, grad_ref, slot_ref, mix_ref, an_ref, ag_ref, so_ref, mo_ref,
    nb, gb, sn, sg, hot, mixrow, zs, zr, ts, tr, xs, xr,
):
    place, sends = Place(), Sends()
    pc = place
    greet(place, zn)
    width = norm_ref.shape[1]
    chunks = width // chunk
    tok = norm_ref.shape[0]
    far = [(pc.z + k) % zn for k in range(1, zn)]
    for k, d in enumerate(far):
        back = pc.z
        for i, (src, dst) in enumerate(((slot_ref, so_ref), (mix_ref, mo_ref))):
            sends.start(
                src.at[d], dst.at[back], ts.at[i, k], tr.at[i, back], pc.at(d, pc.p)
            )
    for c in range(chunks):
        cols = pl.ds(c * chunk, chunk)
        for k, d in enumerate(far):
            for i, (src, dst) in enumerate(((norm_ref, nb), (grad_ref, gb))):
                sends.start(
                    src.at[:, cols],
                    dst.at[pc.z, :, cols],
                    zs.at[i, c, k],
                    zr.at[i, c, pc.z],
                    pc.at(d, pc.p),
                )
    nb[pc.z] = norm_ref[...]
    gb[pc.z] = grad_ref[...]
    so_ref[pc.z] = slot_ref[pc.z]
    mo_ref[pc.z] = mix_ref[pc.z]
    for k, d in enumerate(far):
        arrived(so_ref.at[d], tr.at[0, d])
        arrived(mo_ref.at[d], tr.at[1, d])
    slots = zn * cap
    row = lax.broadcasted_iota(jnp.int32, (slots, tok), 0).astype(f32)
    for p in range(PLANE):
        total = jnp.zeros((slots, 1), f32)
        for z in range(zn):
            want = so_ref[z, pl.ds(p, 1), :] + float(z * cap)
            want = jnp.where(so_ref[z, pl.ds(p, 1), :] < 0, -1.0, want)
            one = jnp.where(row == want, 1.0, 0.0)
            hot[p, :, pl.ds(z * tok, tok)] = one.astype(bf16)
            total = total + jnp.sum(one * mo_ref[z, pl.ds(p, 1), :], axis=1, keepdims=True)
        mixrow[p] = jnp.broadcast_to(total, (slots, 128))
    for c in range(chunks):
        cols = pl.ds(c * chunk, chunk)
        for d in far:
            arrived(nb.at[d, :, cols], zr.at[0, c, d])
            arrived(gb.at[d, :, cols], zr.at[1, c, d])
        rows_n = nb[:, :, cols].reshape(zn * tok, chunk)
        rows_g = gb[:, :, cols].reshape(zn * tok, chunk)

        for k in [1, 2, 3, 4, 5, 6, 7, 0]:
            p = pc.by(k) if k else pc.p
            one = hot[p]
            got_n = jnp.dot(one, rows_n, preferred_element_type=f32).astype(bf16)
            got_g = jnp.dot(one, rows_g, preferred_element_type=f32)
            got_g = (got_g * mixrow[p][:, :1]).astype(bf16)
            if k:
                sn[p, :, cols] = got_n
                sg[p, :, cols] = got_g
                for i, (src, dst) in enumerate(((sn, an_ref), (sg, ag_ref))):
                    sends.start(
                        src.at[p, :, cols],
                        dst.at[pc.p, :, cols],
                        xs.at[i, c, k],
                        xr.at[i, c, k],
                        pc.at(pc.z, p),
                    )
            else:
                an_ref[pc.p, :, cols] = got_n
                ag_ref[pc.p, :, cols] = got_g
    for c in range(chunks):
        cols = pl.ds(c * chunk, chunk)
        for k in range(1, PLANE):
            p = pc.by(k)
            arrived(an_ref.at[p, :, cols], xr.at[0, c, k])
            arrived(ag_ref.at[p, :, cols], xr.at[1, c, k])
    sends.finish()


def send_rows(zn, cap, norm, grad, slot, mix, chunk=512):
    tok, width = norm.shape
    slots = zn * cap
    chunks = width // chunk
    shape = jax.ShapeDtypeStruct((PLANE, slots, width), bf16)
    small = jax.ShapeDtypeStruct(slot.shape, f32)
    return pl.pallas_call(
        functools.partial(send_kernel, zn, cap, chunk),
        out_shape=(shape, shape, small, small),
        in_specs=[VSPEC] * 4,
        out_specs=(VSPEC,) * 4,
        scratch_shapes=[
            pltpu.VMEM((zn, tok, width), bf16),
            pltpu.VMEM((zn, tok, width), bf16),
            pltpu.VMEM((PLANE, slots, width), bf16),
            pltpu.VMEM((PLANE, slots, width), bf16),
            pltpu.VMEM((PLANE, slots, zn * tok), bf16),
            pltpu.VMEM((PLANE, slots, 128), f32),
            dma_sems(2, chunks, zn),
            dma_sems(2, chunks, zn),
            dma_sems(2, zn),
            dma_sems(2, zn),
            dma_sems(2, chunks, PLANE),
            dma_sems(2, chunks, PLANE),
        ],
        compiler_params=params(3),
        name="send_rows",
    )(norm, grad, slot, mix)


def back_kernel(
    zn, chunk, res_ref, pair_ref, dot_ref, comb_ref, hot_ref, mixture_ref, sum_ref, dots_ref,
    rr, rp, rd, zb, zp, zd, am, ap, xs, xr, ds, dr, zs, zr, es, er,
):
    place, sends = Place(), Sends()
    pc = place
    greet(place, zn)
    width = res_ref.shape[2]
    chunks = width // chunk
    tok = mixture_ref.shape[0]
    slots = res_ref.shape[1]
    far = [(pc.z + k) % zn for k in range(1, zn)]
    both = ((pair_ref, rp), (res_ref, rr))
    for k in range(1, PLANE):
        p = pc.by(k)
        sends.start(dot_ref.at[p], rd.at[pc.p], ds.at[k], dr.at[k], pc.at(pc.z, p))
    for i, (src, dst) in enumerate(both):
        for c in range(chunks):
            cols = pl.ds(c * chunk, chunk)
            for k in range(1, PLANE):
                p = pc.by(k)
                sends.start(
                    src.at[p, :, cols],
                    dst.at[pc.p, :, cols],
                    xs.at[i, c, k],
                    xr.at[i, c, k],
                    pc.at(pc.z, p),
                )
    rd[pc.p] = dot_ref[pc.p]
    own = [
        pltpu.make_async_copy(src.at[pc.p], dst.at[pc.p], xr.at[i, 0, 0])
        for i, (src, dst) in enumerate(both)
    ]
    for copy in own:
        copy.start()
    for k in range(1, PLANE):
        arrived(rd.at[pc.by(k)], dr.at[k])
    zd[...] = jnp.dot(
        hot_ref[...], rd[...].reshape(PLANE * slots, 128), preferred_element_type=f32
    ).reshape(zn, tok, 128)
    for k, d in enumerate(far):
        sends.start(zd.at[d], dots_ref.at[pc.z], es.at[k], er.at[pc.z], pc.at(d, pc.p))
    dots_ref[pc.z] = zd[pc.z]
    for i, (buf, mat, out) in enumerate(((rp, hot_ref, zp), (rr, comb_ref, zb))):
        land = (ap, am)[i]
        own[i].wait()
        for c in range(chunks):
            cols = pl.ds(c * chunk, chunk)
            for k in range(1, PLANE):
                arrived(buf.at[pc.by(k), :, cols], xr.at[i, c, k])
            got = jnp.dot(
                mat[...],
                buf[:, :, cols].reshape(PLANE * slots, chunk),
                preferred_element_type=f32,
            )
            out[:, :, cols] = got.astype(bf16).reshape(zn, tok, chunk)
            for k, d in enumerate(far):
                sends.start(
                    out.at[d, :, cols],
                    land.at[pc.z, :, cols],
                    zs.at[i, c, k],
                    zr.at[i, c, pc.z],
                    pc.at(d, pc.p),
                )
    for i, (land, out, dst) in enumerate(((ap, zp, sum_ref), (am, zb, mixture_ref))):
        for c in range(chunks):
            cols = pl.ds(c * chunk, chunk)
            total = out[pc.z, :, cols].astype(f32)
            for d in far:
                arrived(land.at[d, :, cols], zr.at[i, c, d])
                total = total + land[d, :, cols].astype(f32)
            dst[:, cols] = total
    for d in far:
        arrived(dots_ref.at[d], er.at[d])
    sends.finish()


def back_rows(zn, tok, res, pair, dots, comb, hot, chunk=512):
    _, slots, width = res.shape
    chunks = width // chunk
    shape = jax.ShapeDtypeStruct((tok, width), f32)
    return pl.pallas_call(
        functools.partial(back_kernel, zn, chunk),
        out_shape=(shape, shape, jax.ShapeDtypeStruct((zn, tok, 128), f32)),
        in_specs=[ASPEC] * 2 + [VSPEC] * 3,
        out_specs=(VSPEC,) * 3,
        scratch_shapes=[
            pltpu.VMEM((PLANE, slots, width), bf16),
            pltpu.VMEM((PLANE, slots, width), bf16),
            pltpu.VMEM((PLANE, slots, 128), bf16),
            pltpu.VMEM((zn, tok, width), bf16),
            pltpu.VMEM((zn, tok, width), bf16),
            pltpu.VMEM((zn, tok, 128), f32),
            pltpu.VMEM((zn, tok, width), bf16),
            pltpu.VMEM((zn, tok, width), bf16),
            dma_sems(2, chunks, PLANE),
            dma_sems(2, chunks, PLANE),
            dma_sems(PLANE),
            dma_sems(PLANE),
            dma_sems(2, chunks, zn),
            dma_sems(2, chunks, zn),
            dma_sems(zn),
            dma_sems(zn),
        ],
        compiler_params=params(4),
        name="back_rows",
    )(res, pair, dots, comb, hot)


class ColumnReduce:
    def __init__(self, place, sends, zn, part, up, down, give, take, out, ss_r, ss_l, rs_r, rs_l, ps, pr):
        self.place, self.sends, self.zn = place, sends, zn
        self.part, self.up, self.down, self.give, self.take, self.out = part, up, down, give, take, out
        self.ss_r, self.ss_l, self.rs_r, self.rs_l, self.ps, self.pr = ss_r, ss_l, rs_r, rs_l, ps, pr

    def _hop(self, buf, rs, ss, d, start, inner, device):
        rows = self.part.shape[2]

        def add():
            arrived(buf.at[d], rs.at[d])
            for h in range(2):

                def put(at, v):
                    buf[d, h, at, :] = v.astype(bf16)

                add_rows(
                    put,
                    lambda at: self.part[d, h, at, :],
                    lambda at: buf[d, h, at, :],
                    rows,
                )

        pl.when(jnp.logical_and(start, inner))(add)
        self.sends.start(
            buf.at[d], buf.at[d], ss.at[d], rs.at[d], device, jnp.logical_and(start, inner)
        )
        self.sends.start(
            self.part.at[d],
            buf.at[d],
            ss.at[d],
            rs.at[d],
            device,
            jnp.logical_and(start, jnp.logical_not(inner)),
        )

    def step(self, k):
        pc, zn = self.place, self.zn
        d = zn - 1 - k
        right = pc.at(jnp.minimum(pc.z + 1, zn - 1), pc.p)
        left = pc.at(jnp.maximum(pc.z - 1, 0), pc.p)
        self._hop(self.up, self.rs_r, self.ss_r, d, pc.z < d, pc.z > 0, right)
        d = k
        self._hop(self.down, self.rs_l, self.ss_l, d, pc.z > d, pc.z < zn - 1, left)

    def pair(self):
        pc, zn = self.place, self.zn
        rows = self.part.shape[2]
        lower, upper = pc.z > 0, pc.z < zn - 1
        arrived(self.up.at[pc.z], self.rs_r.at[pc.z], lower)
        arrived(self.down.at[pc.z], self.rs_l.at[pc.z], upper)

        def total(h, at):
            v = self.part[pc.z, h, at, :].astype(f32)
            v = v + jnp.where(lower, self.up[pc.z, h, at, :].astype(f32), 0.0)
            return v + jnp.where(upper, self.down[pc.z, h, at, :].astype(f32), 0.0)

        def give(i, carry):
            at = pl.ds(pl.multiple_of(i * 32, 32), 32)
            self.give[at, :] = total(1 - pc.y, at).astype(bf16)
            return carry

        lax.fori_loop(0, rows // 32, give, 0)
        self.sends.start(self.give, self.take, self.ps, self.pr, pc.peer(dy=1))

        def keep(i, carry):
            at = pl.ds(pl.multiple_of(i * 32, 32), 32)
            self.out[pc.y, at, :] = total(pc.y, at)
            return carry

        lax.fori_loop(0, rows // 32, keep, 0)

    def finish(self):
        pc = self.place
        arrived(self.take, self.pr)
        self.out[1 - pc.y] = self.take[...].astype(f32)


def close_kernel(
    zn, part_ref, gq_ref, go_ref, out_ref, oq_ref, oo_ref,
    c1, s1, ra, rb, last, uq, dq, uo, do, vq, tq, vo, to, gs, gr, sr, sl, rr, rl, ps, pr,
):
    place, sends = Place(), Sends()
    greet(place, zn)
    rows = PlaneReduce(place, sends, part_ref, out_ref, (c1, s1, ra, rb, last), gs, gr)
    o = ColumnReduce(
        place, sends, zn, go_ref, uo, do, vo, to, oo_ref,
        sr.at[1], sl.at[1], rr.at[1], rl.at[1], ps.at[1], pr.at[1],
    )
    q = ColumnReduce(
        place, sends, zn, gq_ref, uq, dq, vq, tq, oq_ref,
        sr.at[0], sl.at[0], rr.at[0], rl.at[0], ps.at[0], pr.at[0],
    )
    for k in range(4):
        rows.first(k)
    o.step(0)
    q.step(0)
    for k in range(4):
        rows.second(k)
    rows.third()
    for k in range(1, zn - 1):
        o.step(k)
        q.step(k)
    o.pair()
    q.pair()
    rows.finish()
    o.finish()
    q.finish()
    sends.finish()


def close_sum(zn, part, gq, go):
    _, rows, width = part.shape
    _, _, r, wq = gq.shape
    wo = go.shape[3]
    return pl.pallas_call(
        functools.partial(close_kernel, zn),
        out_shape=(
            jax.ShapeDtypeStruct((rows, width), f32),
            jax.ShapeDtypeStruct((2, r, wq), f32),
            jax.ShapeDtypeStruct((2, r, wo), f32),
        ),
        in_specs=[VSPEC] * 3,
        out_specs=(VSPEC,) * 3,
        scratch_shapes=PlaneReduce.scratch(rows, width)
        + [
            pltpu.VMEM((zn, 2, r, wq), bf16),
            pltpu.VMEM((zn, 2, r, wq), bf16),
            pltpu.VMEM((zn, 2, r, wo), bf16),
            pltpu.VMEM((zn, 2, r, wo), bf16),
            pltpu.VMEM((r, wq), bf16),
            pltpu.VMEM((r, wq), bf16),
            pltpu.VMEM((r, wo), bf16),
            pltpu.VMEM((r, wo), bf16),
            dma_sems(10),
            dma_sems(10),
            dma_sems(2, zn),
            dma_sems(2, zn),
            dma_sems(2, zn),
            dma_sems(2, zn),
            dma_sems(2),
            dma_sems(2),
        ],
        compiler_params=params(5),
        name="close_sum",
    )(part, gq, go)


def small_kernel(zn, in_ref, out_ref, l1, mid, l2, as_, ar, bs, br, cs, cr):
    place, sends = Place(), Sends()
    pc = place
    greet(place, zn)
    far = [(pc.z + k) % zn for k in range(1, zn)]
    for k in range(1, PLANE):
        p = pc.by(k)
        sends.start(in_ref.at[p], l1.at[k], as_.at[k], ar.at[k], pc.at(pc.z, p))
    total = in_ref[pc.p]
    for k in range(1, PLANE):
        arrived(l1.at[k], ar.at[k])
        total = total + l1[k]
    mid[...] = total
    for k, d in enumerate(far):
        sends.start(mid, l2.at[pc.z], bs.at[k], br.at[pc.z], pc.at(d, pc.p))
    l2[pc.z] = total
    for d in far:
        arrived(l2.at[d], br.at[d])
    total = l2[0]
    for z in range(1, zn):
        total = total + l2[z]
    out_ref[pc.p] = total
    for k in range(1, PLANE):
        p = pc.by(k)
        sends.start(out_ref.at[pc.p], out_ref.at[pc.p], cs.at[k], cr.at[k], pc.at(pc.z, p))
    for k in range(1, PLANE):
        p = pc.by(k)
        arrived(out_ref.at[p], cr.at[k])
    sends.finish()


def small_sum(zn, flat):
    _, rows, lanes = flat.shape
    return pl.pallas_call(
        functools.partial(small_kernel, zn),
        out_shape=jax.ShapeDtypeStruct(flat.shape, f32),
        in_specs=[VSPEC],
        out_specs=VSPEC,
        scratch_shapes=[
            pltpu.VMEM((PLANE, rows, lanes), f32),
            pltpu.VMEM((rows, lanes), f32),
            pltpu.VMEM((zn, rows, lanes), f32),
            dma_sems(PLANE),
            dma_sems(PLANE),
            dma_sems(zn),
            dma_sems(zn),
            dma_sems(PLANE),
            dma_sems(PLANE),
        ],
        compiler_params=params(6),
        name="small_sum",
    )(flat)


def local(
    tokens,
    out_grad,
    first_gain,
    second_gain,
    query_gain,
    key_gain,
    query_weight,
    key_weight,
    value_weight,
    output_weight,
    router_weight,
    gate_weight,
    up_weight,
    down_weight,
    expert_ids,
    router_order,
    image_starts,
):
    tok, width = tokens.shape
    zn = lax.axis_size("exp") // 2
    experts = PLANE * zn
    cap = (9 * tok * TOP + 8 * experts - 1) // (8 * experts)
    slots = zn * cap
    length = PLANE * tok
    own_rows = query_weight.shape[0]
    half = query_weight.shape[1] // 2
    heads = half // HD
    scale = HD ** (-0.5)
    exp_index = lax.axis_index("exp")
    starts = lax.dynamic_slice_in_dim(image_starts, exp_index // 2, 1, 0)[0]

    expert_axis = jnp.arange(experts, dtype=jnp.int32)
    member = jnp.any(expert_ids[:, :, None] == expert_axis[None, None, :], axis=1)
    order_here = router_order[0]
    earlier = (order_here[None, :] < order_here[:, None]).astype(bf16)
    counts = jnp.dot(earlier, member.astype(bf16), preferred_element_type=f32)
    keep = member & (counts < cap)
    slot_of = jnp.where(keep, counts, -1.0)

    resid_in = tokens.astype(f32)
    first_rms = rms_scale(resid_in)
    first_hat = resid_in * first_rms
    first_norm = (first_hat * first_gain).astype(bf16)
    q_halves = query_weight.reshape(own_rows, 2, half).transpose(1, 0, 2)
    kv = jnp.concatenate([key_weight, value_weight], axis=1)
    pack_q = jnp.concatenate([q_halves, jnp.broadcast_to(kv[None], (2,) + kv.shape)], axis=2)
    pack_o = output_weight.reshape(2, half, own_rows).transpose(0, 2, 1)
    seq_norm, full_q, full_o = open_gather(zn, first_norm, pack_q, pack_o)
    seq_norm = seq_norm.reshape(length, width)
    full_q = full_q.reshape(width, half + 2 * HD)
    full_o = full_o.reshape(width, half)
    pre = jnp.dot(seq_norm, full_q, preferred_element_type=f32)
    query_pre = pre[:, :half].reshape(length, heads, HD)
    key_pre = pre[:, half : half + HD]
    value_rows = pre[:, half + HD :].astype(bf16)
    pos = jnp.arange(length, dtype=jnp.int32)
    cosine, sine = rotary_tables(pos, HD)
    query_rms = rms_scale(query_pre)
    query_hat = query_pre * query_rms
    query_rot = rotate(query_hat * query_gain, cosine[:, None, :], sine[:, None, :]).astype(bf16)
    key_rms = rms_scale(key_pre)
    key_hat = key_pre * key_rms
    key_rot = rotate(key_hat * key_gain, cosine, sine).astype(bf16)
    pieces = piece_ids(pos, starts)
    mask = allowed_mask(pos, pos, pieces, pieces)

    def scores_of():
        scores = jnp.einsum("qhd,kd->hqk", query_rot, key_rot, preferred_element_type=f32) * scale
        return jnp.where(mask[None], scores, NEGATIVE)

    scores = scores_of()
    top_score = jnp.max(scores, axis=-1, keepdims=True)
    expo = jnp.exp(scores - top_score)
    total = jnp.sum(expo, axis=-1, keepdims=True)
    probs_low = (expo / total).astype(bf16)
    log_norm = top_score + jnp.log(total)
    context = jnp.einsum("hqk,kd->qhd", probs_low, value_rows, preferred_element_type=f32)
    context_rows = context.astype(bf16).reshape(length, half)
    part = lax.dot_general(
        context_rows, full_o, (((1,), (1,)), ((), ())), preferred_element_type=f32
    )
    attention = rows_sum(zn, part.astype(bf16).reshape(PLANE, tok, width))
    resid_mid = resid_in + attention
    second_rms = rms_scale(resid_mid)
    second_hat = resid_mid * second_rms
    second_norm = (second_hat * second_gain).astype(bf16)
    logits = jnp.dot(second_norm, router_weight, preferred_element_type=f32)
    mix = jax.nn.softmax(jnp.where(member, logits, NEGATIVE), axis=-1)
    mix = jnp.where(member, mix, 0.0)
    keep_mix = jnp.where(keep, mix, 0.0)
    slot_t = slot_of.T.reshape(zn, PLANE, tok)
    mix_t = keep_mix.T.reshape(zn, PLANE, tok)
    rows_n, rows_g, slots_all, mix_all = send_rows(zn, cap, second_norm, out_grad, slot_t, mix_t)
    arrived_n = rows_n.reshape(PLANE * slots, width)
    arrived_g = rows_g.reshape(PLANE * slots, width)

    gate_val = jnp.dot(arrived_n, gate_weight[0], preferred_element_type=f32)
    up_val = jnp.dot(arrived_n, up_weight[0], preferred_element_type=f32)
    gate_sig = jax.nn.sigmoid(gate_val)
    gate_act = gate_val * gate_sig
    inner = (gate_act * up_val).astype(bf16)
    result = jnp.dot(inner, down_weight[0], preferred_element_type=f32).astype(bf16)
    inner_grad = jnp.dot(arrived_g, down_weight[0].T, preferred_element_type=f32)
    down_grad = jnp.dot(inner.T, arrived_g, preferred_element_type=f32)[None]
    gate_back = (inner_grad * up_val * gate_sig * (1.0 + gate_val * (1.0 - gate_sig))).astype(bf16)
    up_back = (inner_grad * gate_act).astype(bf16)
    gate_grad = jnp.dot(arrived_n.T, gate_back, preferred_element_type=f32)[None]
    up_grad = jnp.dot(arrived_n.T, up_back, preferred_element_type=f32)[None]
    pair_back = jnp.dot(gate_back, gate_weight[0].T, preferred_element_type=f32) + jnp.dot(
        up_back, up_weight[0].T, preferred_element_type=f32
    )
    pair_back = pair_back.astype(bf16)
    dots = jnp.sum(arrived_g.astype(f32) * result.astype(f32), axis=1, keepdims=True)
    dots_high = dots.astype(bf16)
    dots_low = (dots - dots_high.astype(f32)).astype(bf16)
    place = (exp_index % 2) * 4 + lax.axis_index("tp")
    lane = jnp.arange(128, dtype=jnp.int32)[None, :]
    zero = jnp.zeros((), bf16)
    dot_lanes = jnp.where(lane == place, dots_high, zero) + jnp.where(
        lane == place + PLANE, dots_low, zero
    )

    slot_col = slots_all.transpose(0, 2, 1).reshape(zn, tok, PLANE, 1)
    mix_col = mix_all.transpose(0, 2, 1).reshape(zn, tok, PLANE, 1)
    want = jnp.where(slot_col < 0, -1.0, slot_col + (jnp.arange(zn, dtype=f32) * cap)[:, None, None, None])
    hot = want == jnp.arange(slots, dtype=f32)[None, None, None, :]
    comb = jnp.where(hot, mix_col, 0.0).astype(bf16).reshape(zn * tok, PLANE * slots)
    hot = hot.astype(bf16).reshape(zn * tok, PLANE * slots)
    mixture, pairs_sum, dots_all = back_rows(
        zn,
        tok,
        result.reshape(PLANE, slots, width),
        pair_back.reshape(PLANE, slots, width),
        dot_lanes.reshape(PLANE, slots, 128),
        comb,
        hot,
    )
    block_out = (resid_mid + mixture).astype(bf16)
    grad_out = out_grad.astype(f32)
    mix_dots = dots_all[:, :, :PLANE] + dots_all[:, :, PLANE : 2 * PLANE]
    mix_dots = mix_dots.transpose(1, 0, 2).reshape(tok, experts)
    chosen_grad = mix_dots - mix * jnp.sum(mix_dots, axis=1, keepdims=True)
    logit_grad = chosen_grad.astype(bf16)
    router_part = jnp.dot(second_norm.T, logit_grad, preferred_element_type=f32)
    norm2_back = pairs_sum + jnp.dot(logit_grad, router_weight.T, preferred_element_type=f32)
    mid_from_norm, second_gain_part = norm_back(norm2_back, second_hat, second_rms, second_gain)
    middle_grad = grad_out + mid_from_norm

    seq_grad = rows_gather(zn, middle_grad.astype(bf16)).reshape(length, width)
    output_part = lax.dot_general(
        seq_grad, context_rows, (((0,), (0,)), ((), ())), preferred_element_type=f32
    )
    context_back = jnp.dot(seq_grad, full_o, preferred_element_type=f32).astype(bf16)
    context_back = context_back.reshape(length, heads, HD)
    probs = jnp.exp(scores_of() - log_norm)
    value_back = jnp.einsum(
        "hqk,qhd->kd", probs.astype(bf16), context_back, preferred_element_type=f32
    )
    probs_back = jnp.einsum("qhd,kd->hqk", context_back, value_rows, preferred_element_type=f32)
    delta = jnp.sum(probs * probs_back, axis=-1, keepdims=True)
    score_back = (probs * (probs_back - delta)).astype(bf16)
    rot_query_back = (
        jnp.einsum("hqk,kd->qhd", score_back, key_rot, preferred_element_type=f32) * scale
    )
    rot_key_back = (
        jnp.einsum("hqk,qhd->kd", score_back, query_rot, preferred_element_type=f32) * scale
    )
    query_gained = unrotate(rot_query_back, cosine[:, None, :], sine[:, None, :])
    query_back, query_gain_part = norm_back(query_gained, query_hat, query_rms, query_gain)
    key_gained = unrotate(rot_key_back, cosine, sine)
    key_back, key_gain_part = norm_back(key_gained, key_hat, key_rms, key_gain)
    all_back = jnp.concatenate(
        [query_back.reshape(length, half), key_back, value_back], axis=1
    ).astype(bf16)
    grad_q = lax.dot_general(
        seq_norm, all_back, (((0,), (0,)), ((), ())), preferred_element_type=f32
    )
    norm1_part = lax.dot_general(
        all_back, full_q, (((1,), (1,)), ((), ())), preferred_element_type=f32
    )
    norm1_back, sum_q, sum_o = close_sum(
        zn,
        norm1_part.astype(bf16).reshape(PLANE, tok, width),
        grad_q.astype(bf16).reshape(zn, 2, own_rows, half + 2 * HD),
        output_part.astype(bf16).reshape(zn, 2, own_rows, half),
    )
    query_grad = jnp.concatenate([sum_q[0, :, :half], sum_q[1, :, :half]], axis=1)
    kv_grad = sum_q[0, :, half:] + sum_q[1, :, half:]
    key_grad, value_grad = kv_grad[:, :HD], kv_grad[:, HD:]
    output_grad = jnp.concatenate([sum_o[0].T, sum_o[1].T], axis=0)
    tok_from_norm, first_gain_part = norm_back(norm1_back, first_hat, first_rms, first_gain)
    tokens_grad = middle_grad + tok_from_norm

    flat = jnp.concatenate(
        [
            router_part.reshape(-1),
            first_gain_part,
            second_gain_part,
            query_gain_part,
            key_gain_part,
        ]
    )
    count = flat.shape[0]
    unit = PLANE * 8 * 128
    padded = -(-count // unit) * unit
    flat = jnp.pad(flat, (0, padded - count)).reshape(PLANE, padded // (PLANE * 128), 128)
    flat = small_sum(zn, flat).reshape(-1)
    n_router = width * experts
    router_grad = flat[:n_router].reshape(width, experts)
    rest = flat[n_router:]
    first_gain_grad = rest[:width]
    second_gain_grad = rest[width : 2 * width]
    query_gain_grad = rest[2 * width : 2 * width + HD]
    key_gain_grad = rest[2 * width + HD : 2 * width + 2 * HD]
    return (
        block_out,
        tokens_grad,
        first_gain_grad,
        second_gain_grad,
        query_gain_grad,
        key_gain_grad,
        query_grad,
        key_grad,
        value_grad,
        output_grad,
        router_grad,
        gate_grad,
        up_grad,
        down_grad,
    )


def solution(mesh):
    both = ("exp", "tp")
    in_specs = (
        P(both, None),
        P(both, None),
        P(),
        P(),
        P(),
        P(),
        P("exp", "tp"),
        P("exp", "tp"),
        P("exp", "tp"),
        P("tp", "exp"),
        P(),
        P(both, None, None),
        P(both, None, None),
        P(both, None, None),
        P(both, None),
        P(both, None),
        P(),
    )
    out_specs = (
        P(both, None),
        P(both, None),
        P(),
        P(),
        P(),
        P(),
        P("exp", "tp"),
        P("exp", "tp"),
        P("exp", "tp"),
        P("tp", "exp"),
        P(),
        P(both, None, None),
        P(both, None, None),
        P(both, None, None),
    )
    return jax.shard_map(local, mesh=mesh, in_specs=in_specs, out_specs=out_specs, check_vma=False)
```

time: 1400 us -> 828 us (0.59)
  waiting for transfers between devices: 854 us -> 0 us
  Pallas kernels: 0 us -> 571 us
  local copies, waits for them, and re-layouts: 153 us -> 46.4 us
  blocking collectives: 106 us -> 0 us
  starting transfers between devices: 40.5 us -> 0 us
  matrix products: 156 us -> 137 us
    pallas_call x0 -> x7, Pallas kernels: none -> 571 us  [the longest x1 156 us: send_rows(): pl.pallas_call(functools.partial(send_kernel, zn, cap, chunk), out_shape=...]
    all_to_all x4 -> x0, waiting for transfers between devices: 350 us -> none  [route_rows(): lax.all_to_all(buffer, ('exp', 'tp'), split_axis=0, concat_axis=0, tiled=...]
    reduce_scatter x6 -> x0, waiting for transfers between devices: 338 us -> none  [the longest x1 90 us: local(): lax.psum_scatter(query_part.astype(jnp.bfloat16), 'exp', scatter_dimensio...]
    psum x1 -> x0, waiting for transfers between devices: 85.5 us -> none  [local(): lax.psum((first_gain_part, second_gain_part, query_gain_part, key_gain_pa...]
    all_gather x4 -> x0, waiting for transfers between devices: 79.1 us -> none  [the longest x1 34.1 us: local(): lax.all_gather(output_weight, 'exp', axis=1, tiled=True)]
    all_gather x2 -> x0, blocking collectives: 66 us -> none  [the longest x1 34.8 us: local(): lax.all_gather(value_weight, 'exp', axis=0, tiled=True)]
    reshape x10 -> x4, local copies, waits for them, and re-layouts: 57.7 us -> 7.29 us  [the longest x1 2.93 us: local(): query_pre = pre[:, :half].reshape(length, heads, HD)]
    gather x4 -> x0, local copies, waits for them, and re-layouts: 49 us -> none  [the longest x1 13.4 us: local(): send_grad = padded_pair[slot_pair].reshape(experts, capacity, width)]
  transfers between devices with their start and end apart: 19 -> 0, of which waited for: 14 -> 0; matrix products, arithmetic and copies ran while one was open for 18% -> 0% of each run, Pallas kernels for 0% -> 0%
where the time goes in v1:
time: 828 us; the launch traced here: 818 us
  Pallas kernels  571 us (69%)
  matrix products  137 us (17%)
  other arithmetic  61.2 us (7%)
  local copies, waits for them, and re-layouts  46.4 us (6%)
    pallas_call x1, Pallas kernels, send_rows(): pl.pallas_call(functools.partial(send_kernel, zn, cap, chunk), out_shape=...  156 us
    pallas_call x1, Pallas kernels, back_rows(): pl.pallas_call(functools.partial(back_kernel, zn, chunk), out_shape=(shap...  128 us
    pallas_call x1, Pallas kernels, close_sum(): pl.pallas_call(functools.partial(close_kernel, zn), out_shape=(jax.ShapeD...  115 us
    pallas_call x1, Pallas kernels, open_gather(): pl.pallas_call(functools.partial(open_kernel, zn), out_shape=(jax.ShapeDt...  96.6 us
    pallas_call x1, Pallas kernels, rows_sum(): pl.pallas_call(functools.partial(rows_sum_kernel, zn), out_shape=jax.Shap...  26.7 us
    pallas_call x1, Pallas kernels, rows_gather(): pl.pallas_call(functools.partial(rows_kernel, zn), out_shape=jax.ShapeDty...  26.6 us
    pallas_call x1, Pallas kernels, small_sum(): pl.pallas_call(functools.partial(small_kernel, zn), out_shape=jax.ShapeDt...  22.3 us

profile of v1, /device:TPU:8, one launch (start us, length us, event | category | flops | bytes accessed | tf_op | source)
XLA Modules:
  0.0 818.4 jit_solution(5764514956781406643)
XLA Ops:
  1.9 1.8 fusion.9
  5.5 2.0 fusion.36.own_ref
  7.5 2.0 copy.76
  9.5 2.0 copy.77
  11.6 2.0 pad_maximum_fusion.5.pq_ref
  13.6 2.0 copy.78
  15.6 96.6 %open_gather.1 = (bf16[8,128,2048]{2,1,0:T(8,128)(2,1)}, bf16[8,256,768]{2,1,0:T(8,128)(2,1)}, bf16[8,256,512]{2,1,0:T(8,128)(2,1)}) custom-call(bf16[128,2048]{1,0:T(8,128)(2,1)} %fusion.36.own_ref, bf16[2,256,768]{2,1,0:T(8,128)(2,1)} %pad_maximum_fusion.5.pq_ref, bf16[2,256,512]{2,1,0:T(8,128)(2,1)} %bitcast.223), custom_call_target="tpu_custom_call" | custom-call | tf_op jit(solution)/shard_map/open_gather/pallas_call | solution.py:468
  112.3 6.2 fusion.92
  118.6 1.6 copy-done.4
  120.3 1.8 multiply_cosine_fusion
  122.2 2.0 copy.80
  125.1 1.8 multiply_reduce_fusion.2
  127.0 3.2 slice.118
  130.2 2.9 copy.79
  133.1 2.0 multiply_multiply_fusion
  136.4 8.0 fusion.89
  144.4 8.0 fusion.3
  152.4 9.3 %fusion.28 = bf16[128,4,1024]{2,0,1:T(8,128)(2,1)S(1)} fusion(f32[4,1024,1024]{1,2,0:T(8,128)} %get-tuple-element.132, f32[4,1024]{1,0:T(4,128)S(1)} %fusion.3, f32[4,1024]{1,0:T(4,128)S(1)} %get-tuple-element.131, f32[1024,768]{0,1:T(8,128)} %copy-done.4), kind=kOutput, calls=%fused_computation.70 | convolution fusion | flops 1086849024 | bytes 18120704 | tf_op jit(solution)/shard_map/hqk,kd->qhd/dot_general | solution.py:1044
  161.8 4.4 convolution_convert_fusion.1
  166.2 26.7 %rows_sum.1 = f32[128,2048]{1,0:T(8,128)} custom-call(bf16[8,128,2048]{2,1,0:T(8,128)(2,1)} %bitcast.218), custom_call_target="tpu_custom_call" | custom-call | tf_op jit(solution)/shard_map/rows_sum/pallas_call | solution.py:532
  193.0 1.5 multiply_reduce_fusion.5
  196.9 155.7 %send_rows.1 = (bf16[8,144,2048]{2,1,0:T(8,128)(2,1)}, bf16[8,144,2048]{2,1,0:T(8,128)(2,1)}, f32[4,8,128]{2,1,0:T(8,128)}, f32[4,8,128]{2,1,0:T(8,128)}) custom-call(bf16[128,2048]{1,0:T(8,128)(2,1)} %copy-done.10, bf16[128,2048]{1,0:T(8,128)(2,1)} %grad_ref.1, f32[4,8,128]{2,1,0:T(8,128)} %get-tuple-element.126.slot_ref, ...), custom_call_target="tpu_custom_call" | custom-call | tf_op jit(solution)/shard_map/send_rows/pallas_call | solution.py:632
  353.7 1.6 copy.119
  355.3 3.0 copy.85
  358.4 3.3 fusion.85
  363.3 2.4 copy.87
  365.7 3.0 select_convert_fusion.comb_ref
  368.7 6.9 fusion.15
  375.7 3.9 fusion.19
  379.6 6.4 multiply_convert_fusion
  386.0 5.9 multiply_reduce_fusion
  393.1 6.5 fusion.17
  399.6 6.0 add_convert_fusion
  405.6 127.9 %back_rows.1 = (f32[128,2048]{1,0:T(8,128)}, f32[128,2048]{1,0:T(8,128)}, f32[4,128,128]{2,1,0:T(8,128)}) custom-call(bf16[8,144,2048]{2,1,0:T(8,128)(2,1)} %bitcast.216, bf16[8,144,2048]{2,1,0:T(8,128)(2,1)} %bitcast.217, bf16[8,144,128]{2,1,0:T(8,128)(2,1)} %select_add_fusion.dot_ref, bf16[512,1152]{1,0:T(8,128)(2,1)} %select_convert_fusion.comb_ref, ...), custom_call_target="tpu_custom_call" | custom-call | tf_op jit(solution)/shard_map/back_rows/pallas_call | solution.py:737
  533.6 1.3 fusion.60
  535.0 1.7 multiply_reduce_fusion.3
  537.9 26.6 %rows_gather.1 = bf16[8,128,2048]{2,1,0:T(8,128)(2,1)} custom-call(bf16[128,2048]{1,0:T(8,128)(2,1)} %fusion.84.own_ref), custom_call_target="tpu_custom_call" | custom-call | tf_op jit(solution)/shard_map/rows_gather/pallas_call | solution.py:505
  564.7 6.1 convolution_convert_fusion.4
  570.8 2.4 convolution_convert_fusion.5
  573.3 1.3 slice-done.3
  574.6 8.6 %fusion = (f32[4,1024]{1,0:T(4,128)S(1)}, f32[1024,1024,4]{1,0,2:T(8,128)}) fusion(f32[4,1024,1024]{1,2,0:T(8,128)S(1)} %bitcast.208, f32[4,1024]{1,0:T(4,128)S(1)} %log_add_fusion, bf16[1024,4,128]{0,2,1:T(8,128)(2,1)S(1)} %bitcast.212, f32[1024,768]{0,1:T(8,128)} %copy-done.4), kind=kOutput, calls=%fused_computation.2 | convolution fusion | flops 1086320640 | bytes 34897920 | tf_op jit(solution)/shard_map/qhd,kd->hqk/dot_general | solution.py:1126
  583.3 10.5 %fusion.2 = bf16[4,1024,1024]{1,2,0:T(8,128)(2,1)} fusion(f32[1024,1024,4]{1,0,2:T(8,128)} %get-tuple-element.139, f32[4,1024,1024]{1,2,0:T(8,128)S(1)} %bitcast.208, f32[4,1024]{1,0:T(4,128)S(1)} %get-tuple-element.138, f32[4,1024]{1,0:T(4,128)S(1)} %log_add_fusion), kind=kLoop, calls=%fused_computation.4 | loop fusion | flops 16777216 | bytes 41975808 | tf_op jit(solution)/shard_map/convert_element_type | solution.py:1128
  593.8 7.0 multiply_bitcast_fusion
  602.5 2.8 multiply_reduce_fusion.1
  605.3 1.9 copy.94
  607.3 2.6 fusion.23
  610.0 6.4 fusion.32
  616.4 1.4 fusion.56
  620.2 8.9 %fusion.33 = bf16[1024,128]{0,1:T(8,128)(2,1)S(1)} fusion(bf16[1024,4,128]{0,2,1:T(8,128)(2,1)S(1)} %bitcast.213, f32[4,1024,1024]{1,2,0:T(8,128)} %get-tuple-element.132, f32[4,1024]{1,0:T(4,128)S(1)} %log_add_fusion), kind=kOutput, calls=%fused_computation.75 | convolution fusion | flops 1082261504 | bytes 18104320 | tf_op jit(solution)/shard_map/hqk,qhd->kd/dot_general | solution.py:1123
  629.1 4.9 convolution_convert_fusion.3
  634.0 5.0 convolution_convert_fusion.2
  639.0 115.1 %close_sum.1 = (f32[128,2048]{1,0:T(8,128)}, f32[2,256,768]{2,1,0:T(8,128)}, f32[2,256,512]{2,1,0:T(8,128)}) custom-call(bf16[8,128,2048]{2,1,0:T(8,128)(2,1)} %bitcast.221, bf16[4,2,256,768]{3,2,1,0:T(8,128)(2,1)} %bitcast.222, bf16[4,2,256,512]{3,2,1,0:T(8,128)(2,1)} %bitcast.226), custom_call_target="tpu_custom_call" | custom-call | tf_op jit(solution)/shard_map/close_sum/pallas_call | solution.py:880
  754.1 1.4 slice_bitcast_fusion.1
  756.6 2.5 copy.99
  761.0 22.3 %small_sum.1 = f32[8,72,128]{2,1,0:T(8,128)} custom-call(f32[8,72,128]{2,1,0:T(8,128)} %bitcast.229), custom_call_target="tpu_custom_call" | custom-call | tf_op jit(solution)/shard_map/small_sum/pallas_call | solution.py:946
  783.3 1.3 slice.112
  785.6 2.4 copy.100
  787.9 1.4 slice_bitcast_fusion.3
  790.4 1.3 fusion.87
  791.7 1.3 fusion.86
  793.1 1.7 fusion.40
  796.6 8.7 %convolution_bitcast_fusion = f32[1,768,2048]{2,1,0:T(8,128)} fusion(bf16[1152,768]{1,0:T(8,128)(2,1)S(1)} %copy-done.66, bf16[1152,2048]{1,0:T(8,128)(2,1)} %bitcast.240), kind=kOutput, calls=%fused_computation.21 | convolution fusion | flops 3623878656 | bytes 12779520 | tf_op jit(solution)/shard_map/dot_general | solution.py:1071
  805.3 6.3 convolution_bitcast_fusion.1
  811.6 6.3 convolution_bitcast_fusion.2
  (224 shorter events, 23.8 us)
Async XLA Ops:
  0.6 378.9 %copy-start = (bf16[1,768,2048]{2,1,0:T(8,128)(2,1)S(1)}, bf16[1,768,2048]{2,1,0:T(8,128)(2,1)}, u32[]{:S(2)}) copy-start(bf16[1,768,2048]{2,1,0:T(8,128)(2,1)} %param.30) | copy-start | bytes 9437188
  0.7 10.9 %copy-start.39 = (bf16[256,128]{1,0:T(8,128)(2,1)S(1)}, bf16[256,128]{1,0:T(8,128)(2,1)}, u32[]{:S(2)}) copy-start(bf16[256,128]{1,0:T(8,128)(2,1)} %param.24) | copy-start | bytes 196612
  0.7 10.9 %copy-start.38 = (bf16[256,128]{1,0:T(8,128)(2,1)S(1)}, bf16[256,128]{1,0:T(8,128)(2,1)}, u32[]{:S(2)}) copy-start(bf16[256,128]{1,0:T(8,128)(2,1)} %param.25) | copy-start | bytes 196612
  112.3 7.9 copy-start.45
  127.0 6.1 copy-start.32
  130.2 2.9 copy-start.49
  136.0 8.5 %copy-start.20 = (bf16[1024,4,64]{2,0,1:T(8,128)(2,1)}, bf16[1024,4,64]{2,0,1:T(8,128)(2,1)S(1)}, u32[]{:S(2)}) copy-start(bf16[1024,4,64]{2,0,1:T(8,128)(2,1)S(1)} %get-tuple-element.105) | copy-start | bytes 1572868
  136.0 8.5 %copy-start.22 = (bf16[1024,4,64]{2,0,1:T(8,128)(2,1)}, bf16[1024,4,64]{2,0,1:T(8,128)(2,1)S(1)}, u32[]{:S(2)}) copy-start(bf16[1024,4,64]{2,0,1:T(8,128)(2,1)S(1)} %get-tuple-element.106) | copy-start | bytes 1572868
  152.4 9.3 %copy-start.60 = (bf16[8,256,512]{2,1,0:T(8,128)(2,1)S(1)}, bf16[8,256,512]{2,1,0:T(8,128)(2,1)}, u32[]{:S(2)}) copy-start(bf16[8,256,512]{2,1,0:T(8,128)(2,1)} %get-tuple-element.29) | copy-start | bytes 6291460
  161.8 4.4 copy-start.63
  166.2 26.8 %copy-start.6 = (bf16[128,2048]{1,0:T(8,128)(2,1)S(1)}, bf16[128,2048]{1,0:T(8,128)(2,1)}, u32[]{:S(2)}) copy-start(bf16[128,2048]{1,0:T(8,128)(2,1)} %param.17) | copy-start | bytes 1572868
  166.2 29.3 %copy-start.34 = (f32[2048]{0:T(1024)S(1)}, f32[2048]{0:T(1024)}, u32[]{:S(2)}) copy-start(f32[2048]{0:T(1024)} %param.20) | copy-start | bytes 24580
  193.0 2.7 copy-start.30
  193.0 3.0 copy-start.62
  194.5 342.3 %copy-start.43 = (f32[128]{0:T(128)}, f32[128]{0:T(128)S(1)}, u32[]{:S(2)}) copy-start(f32[128]{0:T(128)S(1)} %add_rsqrt_fusion.2) | copy-start | bytes 1540
  358.3 3.4 copy-start.42
  365.6 10.0 %slice-start.4 = ((s8[4718592]{0:T(1024)(128)(4,1)}), s8[4194304]{0:T(1024)(128)(4,1)S(1)}, s32[]{:S(2)}) async-start(s8[4718592]{0:T(1024)(128)(4,1)} %bitcast.233), calls=%async_computation.4 | async-start | bytes 8388608
  368.7 7.0 slice-start.5
  368.7 7.0 copy-start.57
  368.7 10.9 %slice-start.8 = ((s8[4718592]{0:T(1024)(128)(4,1)}), s8[4194304]{0:T(1024)(128)(4,1)S(1)}, s32[]{:S(2)}) async-start(s8[4718592]{0:T(1024)(128)(4,1)} %bitcast.241), calls=%async_computation.8 | async-start | bytes 8388608
  375.6 3.9 slice-start.9
  386.0 5.9 copy-start.65
  393.1 6.5 copy-start.58
  393.1 6.5 copy-start.68
  405.6 129.4 %copy-start.3 = (f32[128,2048]{1,0:T(8,128)S(1)}, f32[128,2048]{1,0:T(8,128)}, u32[]{:S(2)}) copy-start(f32[128,2048]{1,0:T(8,128)} %copy-done.2) | copy-start | bytes 3145732
  405.6 129.4 %copy-start.31 = (bf16[2048,32]{0,1:T(8,128)(2,1)S(1)}, bf16[2048,32]{0,1:T(8,128)(2,1)}, u32[]{:S(2)}) copy-start(bf16[2048,32]{0,1:T(8,128)(2,1)} %param.27) | copy-start | bytes 393220
  533.6 3.3 copy-start.18
  536.8 27.8 %copy-start.8 = (f32[128,2048]{1,0:T(8,128)}, f32[128,2048]{1,0:T(8,128)S(1)}, u32[]{:S(2)}) copy-start(f32[128,2048]{1,0:T(8,128)S(1)} %get-tuple-element.137) | copy-start | bytes 3145732
  536.8 27.8 %copy-start.54 = (f32[128]{0:T(128)}, f32[128]{0:T(128)S(1)}, u32[]{:S(2)}) copy-start(f32[128]{0:T(128)S(1)} %broadcast_multiply_fusion.3) | copy-start | bytes 1540
  537.9 26.7 %copy-start.64 = (bf16[128,4,1024]{2,0,1:T(8,128)(2,1)S(1)}, bf16[128,4,1024]{2,0,1:T(8,128)(2,1)}, u32[]{:S(2)}) copy-start(bf16[128,4,1024]{2,0,1:T(8,128)(2,1)} %copy-done.63) | copy-start | bytes 3145732
  564.6 6.1 copy-start.26
  564.6 6.1 copy-start.61
  564.6 8.6 %slice-start = ((s8[16777216]{0:T(1024)(128)(4,1)}), s8[4194304]{0:T(1024)(128)(4,1)S(1)}, s32[]{:S(2)}) async-start(s8[16777216]{0:T(1024)(128)(4,1)} %bitcast.207), calls=%async_computation | async-start | bytes 8388608
  564.6 8.6 %slice-start.1 = ((s8[16777216]{0:T(1024)(128)(4,1)}), s8[4194304]{0:T(1024)(128)(4,1)S(1)}, s32[]{:S(2)}) async-start(s8[16777216]{0:T(1024)(128)(4,1)} %bitcast.207), calls=%async_computation.1 | async-start | bytes 8388608
  570.8 3.9 slice-start.3
  573.2 10.1 %copy-start.12 = (bf16[1024,512]{0,1:T(8,128)(2,1)}, bf16[1024,512]{0,1:T(8,128)(2,1)S(1)}, u32[]{:S(2)}) copy-start(bf16[1024,512]{0,1:T(8,128)(2,1)S(1)} %convolution_convert_fusion.5) | copy-start | bytes 3145732
  593.8 7.0 copy-start.15
  593.8 7.0 copy-start.17
  607.2 2.7 copy-start.21
  607.2 2.7 copy-start.23
  609.9 6.4 copy-start.41
  609.9 6.4 copy-start.53
  609.9 7.8 copy-start.37
  609.9 7.8 copy-start.46
  616.4 3.8 copy-start.13
  620.2 8.9 %copy-start.56 = (bf16[8,128,2048]{2,1,0:T(8,128)(2,1)S(1)}, bf16[8,128,2048]{2,1,0:T(8,128)(2,1)}, u32[]{:S(2)}) copy-start(bf16[8,128,2048]{2,1,0:T(8,128)(2,1)} %get-tuple-element.27) | copy-start | bytes 12582916
  629.0 4.9 copy-start.59
  754.1 5.0 copy-start.7
  754.1 5.0 copy-start.24
  754.1 5.0 copy-start.35
  754.1 5.0 copy-start.48
  755.5 4.0 copy-start.11
  785.6 7.5 copy-start.9
  785.6 7.5 copy-start.19
  785.6 7.5 copy-start.44
  785.6 7.5 copy-start.55
  787.9 5.1 copy-start.25
  787.9 5.1 copy-start.27
  793.1 3.5 copy-start.66
  793.1 12.2 %slice-start.6 = ((s8[4718592]{0:T(1024)(128)(4,1)}), s8[524288]{0:T(1024)(128)(4,1)S(1)}, s32[]{:S(2)}) async-start(s8[4718592]{0:T(1024)(128)(4,1)} %bitcast.236), calls=%async_computation.6 | async-start | bytes 1048576
  796.6 8.7 %slice-start.7 = ((s8[4718592]{0:T(1024)(128)(4,1)}), s8[4194304]{0:T(1024)(128)(4,1)S(1)}, s32[]{:S(2)}) async-start(s8[4718592]{0:T(1024)(128)(4,1)} %bitcast.236), calls=%async_computation.7 | async-start | bytes 8388608
  796.6 8.7 %copy-start.69 = (bf16[1152,768]{1,0:T(8,128)(2,1)S(1)}, bf16[1152,768]{1,0:T(8,128)(2,1)}, u32[]{:S(2)}) copy-start(bf16[1152,768]{1,0:T(8,128)(2,1)} %get-tuple-element.98) | copy-start | bytes 5308420
  805.3 6.3 copy-start.67
  811.6 6.3 copy-start.1
  (16 other events, 26.7 us)

commit v2 on v1

v2 whole, which is shorter than its diff:
```python
import functools

import jax
import jax.numpy as jnp
from jax import lax
from jax.experimental import pallas as pl
from jax.experimental.pallas import tpu as pltpu
from jax.sharding import PartitionSpec as P

HD = 128
TOP = 8
IMG_LEN = 256
PLANE = 8

EPSILON = 1e-06
THETA = 1000000.0
NEGATIVE = -1e30

MESH = pl.DeviceIdType.MESH
f32 = jnp.float32
bf16 = jnp.bfloat16
VMEM_LIMIT = 60 << 20


def rms_scale(values):
    return lax.rsqrt(jnp.mean(values * values, axis=-1, keepdims=True) + EPSILON)


def rotary_tables(positions, width):
    half = width // 2
    freqs = THETA ** (-(jnp.arange(half, dtype=f32) * 2.0 / width))
    angles = positions.astype(f32)[:, None] * freqs[None, :]
    return (jnp.cos(angles), jnp.sin(angles))


def rotate(values, cosine, sine):
    half = values.shape[-1] // 2
    first = values[..., :half]
    second = values[..., half:]
    return jnp.concatenate(
        [first * cosine - second * sine, second * cosine + first * sine], axis=-1
    )


def unrotate(values, cosine, sine):
    half = values.shape[-1] // 2
    first = values[..., :half]
    second = values[..., half:]
    return jnp.concatenate(
        [first * cosine + second * sine, second * cosine - first * sine], axis=-1
    )


def piece_ids(positions, starts):
    inside = (positions[:, None] >= starts[None, :]) & (
        positions[:, None] < starts[None, :] + IMG_LEN
    )
    labels = jnp.arange(1, starts.shape[0] + 1, dtype=jnp.int32)
    return jnp.sum(jnp.where(inside, labels[None, :], 0), axis=1)


def allowed_mask(query_pos, key_pos, query_piece, key_piece):
    causal = key_pos[None, :] <= query_pos[:, None]
    same = (query_piece[:, None] == key_piece[None, :]) & (query_piece[:, None] > 0)
    return causal | same


def norm_back(grad_norm, hat, rms, gain):
    scaled = grad_norm * gain
    inner_mean = jnp.mean(scaled * hat, axis=-1, keepdims=True)
    lead_axes = tuple(range(grad_norm.ndim - 1))
    return (rms * (scaled - hat * inner_mean), jnp.sum(grad_norm * hat, axis=lead_axes))


class Place:
    def __init__(self):
        self.e = lax.axis_index("exp")
        self.t = lax.axis_index("tp")
        self.z = self.e // 2
        self.y = self.e % 2
        self.x = self.t // 2
        self.c = self.t % 2
        self.p = self.y * 4 + self.t

    def at(self, z, p):
        return (z * 2 + p // 4, p % 4)

    def flip(self, dy=0, dx=0, dc=0):
        y = 1 - self.y if dy else self.y
        x = 1 - self.x if dx else self.x
        c = 1 - self.c if dc else self.c
        return y * 4 + x * 2 + c

    def peer(self, dy=0, dx=0, dc=0):
        return self.at(self.z, self.flip(dy, dx, dc))

    def by(self, k):
        return self.flip((k >> 2) & 1, (k >> 1) & 1, k & 1)


class Sends:
    def __init__(self):
        self.kept = []

    def start(self, src, dst, send_sem, recv_sem, device, when=None):
        def make():
            return pltpu.make_async_remote_copy(
                src_ref=src,
                dst_ref=dst,
                send_sem=send_sem,
                recv_sem=recv_sem,
                device_id=device,
                device_id_type=MESH,
            )

        def go():
            make().start()

        if when is None:
            go()
        else:
            pl.when(when)(go)
        self.kept.append((make, when))

    def finish(self):
        for make, when in self.kept:
            if when is None:
                make().wait_send()
            else:
                pl.when(when)(lambda make=make: make().wait_send())
        self.kept = []


def arrived(dst, recv_sem, when=None):
    def go():
        pltpu.make_async_copy(dst, dst, recv_sem).wait()

    if when is None:
        go()
    else:
        pl.when(when)(go)


def greet(place, zn, ends=False, everyone=True, planes=True):
    bar = pltpu.get_barrier_semaphore()
    count = 0
    if planes:
        for k in range(1, PLANE):
            pl.semaphore_signal(
                bar, inc=1, device_id=place.at(place.z, place.by(k)), device_id_type=MESH
            )
        count += PLANE - 1
    if everyone:
        for k in range(1, zn):
            pl.semaphore_signal(
                bar,
                inc=1,
                device_id=place.at((place.z + k) % zn, place.p),
                device_id_type=MESH,
            )
        count += zn - 1
    pl.semaphore_wait(bar, count)
    if ends:
        bar2 = 0
        del bar2


class PlaneGather:
    sems = 8

    def __init__(self, place, sends, buf, ss, rs):
        self.place, self.sends, self.buf, self.ss, self.rs = place, sends, buf, ss, rs
        half = buf.shape[2] // 2
        self.cols_a = pl.ds(0, half)
        self.cols_b = pl.ds(half, half)

    def _send(self, block, which, device, cols=None):
        ref = self.buf.at[block] if cols is None else self.buf.at[block, :, cols]
        self.sends.start(ref, ref, self.ss.at[which], self.rs.at[which], device)

    def _wait(self, block, which, cols=None):
        ref = self.buf.at[block] if cols is None else self.buf.at[block, :, cols]
        arrived(ref, self.rs.at[which])

    def first(self):
        pc = self.place
        self._send(pc.p, 0, pc.peer(dy=1))
        self._send(pc.p, 1, pc.peer(dx=1))
        self._send(pc.p, 2, pc.peer(dc=1))

    def second(self):
        pc = self.place
        px, py = pc.flip(dx=1), pc.flip(dy=1)
        self._wait(px, 1)
        self._send(px, 3, pc.peer(dy=1), self.cols_a)
        self._send(px, 4, pc.peer(dc=1))
        self._wait(py, 0)
        self._send(py, 5, pc.peer(dx=1), self.cols_b)
        self._send(py, 6, pc.peer(dc=1))

    def third(self):
        pc = self.place
        pd = pc.flip(dy=1, dx=1)
        self._wait(pd, 3, self.cols_a)
        self._wait(pd, 5, self.cols_b)
        self._send(pd, 7, pc.peer(dc=1))

    def last(self):
        pc = self.place
        self._wait(pc.flip(dc=1), 2)
        self._wait(pc.flip(dc=1, dx=1), 4)
        self._wait(pc.flip(dc=1, dy=1), 6)
        self._wait(pc.flip(dc=1, dy=1, dx=1), 7)


def add_rows(dst, first, second, rows, step=32):
    def body(i, carry):
        at = pl.ds(pl.multiple_of(i * step, step), step)
        dst(at, first(at).astype(f32) + second(at).astype(f32))
        return carry

    lax.fori_loop(0, rows // step, body, 0)


class PlaneReduce:
    sems = 4 + 4 + 2

    @staticmethod
    def scratch(rows, width):
        return [
            pltpu.VMEM((4, rows, width), bf16),
            pltpu.VMEM((4, rows, width), bf16),
            pltpu.VMEM((2, rows, width // 2), bf16),
            pltpu.VMEM((2, rows, width // 2), bf16),
            pltpu.VMEM((2, rows, width // 2), bf16),
        ]

    def __init__(self, place, sends, part, out, scratch, ss, rs):
        self.place, self.sends, self.part, self.out = place, sends, part, out
        self.c1, self.s1, self.ra, self.rb, self.last = scratch
        self.ss, self.rs = ss, rs
        self.rows = part.shape[1]
        half = part.shape[2] // 2
        self.half = half
        self.cols_a = pl.ds(0, half)
        self.cols_b = pl.ds(half, half)
        pc = place
        self.chips = [(1, 1), (0, 1), (1, 0), (0, 0)]

    def _chip(self, dy, dx):
        pc = self.place
        y = 1 - pc.y if dy else pc.y
        x = 1 - pc.x if dx else pc.x
        return y, x, y * 2 + x

    def first(self, k):
        pc = self.place
        y, x, j = self._chip(*self.chips[k])
        block = y * 4 + x * 2 + (1 - pc.c)
        self.sends.start(
            self.part.at[block], self.c1.at[j], self.ss.at[k], self.rs.at[k], pc.peer(dc=1)
        )

    def second(self, k):
        pc = self.place
        y, x, j = self._chip(*self.chips[k])
        arrived(self.c1.at[j], self.rs.at[k])
        mine = y * 4 + x * 2 + pc.c

        def put(at, v):
            self.s1[j, at, :] = v.astype(bf16)

        add_rows(put, lambda at: self.part[mine, at, :], lambda at: self.c1[j, at, :], self.rows)
        dy, dx = self.chips[k]
        if dx:
            self.sends.start(
                self.s1.at[j, :, self.cols_a],
                self.ra.at[y],
                self.ss.at[4 + (0 if dy else 1)],
                self.rs.at[4 + (0 if dy else 1)],
                pc.peer(dx=1),
            )
        if dy:
            self.sends.start(
                self.s1.at[j, :, self.cols_b],
                self.rb.at[x],
                self.ss.at[6 + (0 if dx else 1)],
                self.rs.at[6 + (0 if dx else 1)],
                pc.peer(dy=1),
            )

    def third(self):
        pc = self.place
        other_y, other_x = 1 - pc.y, 1 - pc.x
        arrived(self.ra.at[other_y], self.rs.at[4])
        j = other_y * 2 + pc.x

        def put_a(at, v):
            self.ra[other_y, at, :] = v.astype(bf16)

        add_rows(
            put_a,
            lambda at: self.s1[j, at, self.cols_a],
            lambda at: self.ra[other_y, at, :],
            self.rows,
        )
        self.sends.start(
            self.ra.at[other_y], self.last.at[0], self.ss.at[8], self.rs.at[8], pc.peer(dy=1)
        )
        arrived(self.rb.at[other_x], self.rs.at[6])
        i = pc.y * 2 + other_x

        def put_b(at, v):
            self.rb[other_x, at, :] = v.astype(bf16)

        add_rows(
            put_b,
            lambda at: self.s1[i, at, self.cols_b],
            lambda at: self.rb[other_x, at, :],
            self.rows,
        )
        self.sends.start(
            self.rb.at[other_x], self.last.at[1], self.ss.at[9], self.rs.at[9], pc.peer(dx=1)
        )

    def finish(self):
        pc = self.place
        own = pc.y * 2 + pc.x
        arrived(self.ra.at[pc.y], self.rs.at[5])
        arrived(self.rb.at[pc.x], self.rs.at[7])

        def put_a(at, v):
            self.out[at, self.cols_a] = v + self.ra[pc.y, at, :].astype(f32)

        def put_b(at, v):
            self.out[at, self.cols_b] = v + self.rb[pc.x, at, :].astype(f32)

        arrived(self.last.at[0], self.rs.at[8])
        add_rows(
            put_a,
            lambda at: self.s1[own, at, self.cols_a],
            lambda at: self.last[0, at, :],
            self.rows,
        )
        arrived(self.last.at[1], self.rs.at[9])
        add_rows(
            put_b,
            lambda at: self.s1[own, at, self.cols_b],
            lambda at: self.last[1, at, :],
            self.rows,
        )


class ColumnGather:
    def __init__(self, place, sends, zn, pack, full, pair_ss, pair_rs, ss_r, ss_l, rs):
        self.place, self.sends, self.zn = place, sends, zn
        self.pack, self.full = pack, full
        self.pair_ss, self.pair_rs, self.ss_r, self.ss_l, self.rs = pair_ss, pair_rs, ss_r, ss_l, rs

    def _on(self, src, piece, right, left):
        pc = self.place
        if right is not None:
            self.sends.start(
                src,
                self.full.at[piece],
                self.ss_r.at[piece],
                self.rs.at[piece],
                pc.at(jnp.minimum(pc.z + 1, self.zn - 1), pc.p),
                right,
            )
        if left is not None:
            self.sends.start(
                src,
                self.full.at[piece],
                self.ss_l.at[piece],
                self.rs.at[piece],
                pc.at(jnp.maximum(pc.z - 1, 0), pc.p),
                left,
            )

    def pair(self):
        pc = self.place
        self.sends.start(
            self.pack.at[1 - pc.y],
            self.full.at[pc.e],
            self.pair_ss,
            self.pair_rs,
            pc.peer(dy=1),
        )

    def own(self):
        pc = self.place
        self._on(self.pack.at[pc.y], pc.e, pc.z < self.zn - 1, pc.z > 0)

    def keep(self):
        pc = self.place
        self.full[pc.e] = self.pack[pc.y]

    def partner(self):
        pc = self.place
        other = pc.z * 2 + 1 - pc.y
        arrived(self.full.at[other], self.pair_rs)
        self._on(self.full.at[other], other, pc.z < self.zn - 1, pc.z > 0)

    def step(self, k):
        pc = self.place
        for first in (True, False):
            y = pc.y if first else 1 - pc.y
            below = jnp.maximum(pc.z - k, 0) * 2 + y
            has = pc.z - k >= 0
            arrived(self.full.at[below], self.rs.at[below], has)
            self._on(
                self.full.at[below], below, jnp.logical_and(has, pc.z < self.zn - 1), None
            )
            above = jnp.minimum(pc.z + k, self.zn - 1) * 2 + y
            has = pc.z + k < self.zn
            arrived(self.full.at[above], self.rs.at[above], has)
            self._on(self.full.at[above], above, None, jnp.logical_and(has, pc.z > 0))


def dma_sems(*shape):
    return pltpu.SemaphoreType.DMA(shape)


VSPEC = pl.BlockSpec(memory_space=pltpu.VMEM)
ASPEC = pl.BlockSpec(memory_space=pl.ANY)


def params(cid):
    return pltpu.CompilerParams(
        collective_id=cid, has_side_effects=True, vmem_limit_bytes=VMEM_LIMIT
    )


class RowChain:
    def __init__(self, place, sends, zn, src, buf, chunk, ss_r, ss_l, rs):
        self.place, self.sends, self.zn = place, sends, zn
        self.src, self.buf, self.chunk = src, buf, chunk
        self.ss_r, self.ss_l, self.rs = ss_r, ss_l, rs

    def _on(self, src, c, origin, right, left):
        pc = self.place
        dst = self.buf.at[origin, :, pl.ds(c * self.chunk, self.chunk)]
        if right is not None:
            self.sends.start(
                src,
                dst,
                self.ss_r.at[c, origin],
                self.rs.at[c, origin],
                pc.at(jnp.minimum(pc.z + 1, self.zn - 1), pc.p),
                right,
            )
        if left is not None:
            self.sends.start(
                src,
                dst,
                self.ss_l.at[c, origin],
                self.rs.at[c, origin],
                pc.at(jnp.maximum(pc.z - 1, 0), pc.p),
                left,
            )

    def own(self, c):
        pc = self.place
        src = self.src.at[:, pl.ds(c * self.chunk, self.chunk)]
        self._on(src, c, pc.z, pc.z < self.zn - 1, pc.z > 0)

    def keep(self):
        self.buf[self.place.z] = self.src[...]

    def step(self, c, k):
        pc = self.place
        cols = pl.ds(c * self.chunk, self.chunk)
        below = jnp.maximum(pc.z - k, 0)
        has = pc.z - k >= 0
        ref = self.buf.at[below, :, cols]
        arrived(ref, self.rs.at[c, below], has)
        self._on(ref, c, below, jnp.logical_and(has, pc.z < self.zn - 1), None)
        above = jnp.minimum(pc.z + k, self.zn - 1)
        has = pc.z + k < self.zn
        ref = self.buf.at[above, :, cols]
        arrived(ref, self.rs.at[c, above], has)
        self._on(ref, c, above, None, jnp.logical_and(has, pc.z > 0))


def turned(values):
    return pltpu.roll(values, HD // 2, 1)


def nt_dot(a, b):
    return lax.dot_general(a, b, (((1,), (1,)), ((), ())), preferred_element_type=f32)


def tn_dot(a, b):
    return lax.dot_general(a, b, (((0,), (0,)), ((), ())), preferred_element_type=f32)


def nn_dot(a, b):
    return jnp.dot(a, b, preferred_element_type=f32)


QBLOCK = 256


def key_limit(i, length):
    return min(length, (i + 1) * QBLOCK + IMG_LEN)


def send_slots(place, sends, zn, src, dst, ss, rs):
    for k in range(1, zn):
        d = (place.z + k) % zn
        sends.start(src.at[d], dst.at[place.z], ss.at[k], rs.at[place.z], place.at(d, place.p))


def take_slots(place, zn, src, dst, rs):
    dst[place.z] = src[place.z]
    for k in range(1, zn):
        d = (place.z + k) % zn
        arrived(dst.at[d], rs.at[d])


def make_hot(zn, cap, tok, slots_ref, hot):
    row = lax.broadcasted_iota(jnp.int32, (zn * cap, tok), 0).astype(f32)

    def body(p, carry):
        for z in range(zn):
            have = slots_ref[z, pl.ds(p, 1), :]
            want = jnp.where(have < 0, -1.0, have + float(z * cap))
            hot[p, :, pl.ds(z * tok, tok)] = jnp.where(row == want, 1.0, 0.0).astype(bf16)
        return carry

    lax.fori_loop(0, PLANE, body, 0)


class PlaneSend:
    def __init__(self, place, sends, hot, rows, buf, out, chunk, ss, rs):
        self.place, self.sends = place, sends
        self.hot, self.rows, self.buf, self.out, self.chunk = hot, rows, buf, out, chunk
        self.ss, self.rs = ss, rs

    def send(self, c):
        pc = self.place
        cols = pl.ds(c * self.chunk, self.chunk)
        zn, tok, _ = self.rows.shape
        for k in (1, 2, 3, 4, 5, 6, 7, 0):
            p = pc.by(k) if k else pc.p
            got = nn_dot(self.hot[p], self.rows[:, :, cols].reshape(zn * tok, self.chunk))
            if k:
                self.buf[p, :, cols] = got.astype(bf16)
                self.sends.start(
                    self.buf.at[p, :, cols],
                    self.out.at[pc.p, :, cols],
                    self.ss.at[c, k],
                    self.rs.at[c, k],
                    pc.at(pc.z, p),
                )
            else:
                self.out[pc.p, :, cols] = got.astype(bf16)

    def take(self, c):
        cols = pl.ds(c * self.chunk, self.chunk)
        for k in range(1, PLANE):
            arrived(self.out.at[self.place.by(k), :, cols], self.rs.at[c, k])


def front_kernel(
    zn, cap, chunk, heads,
    tok_ref, gain_ref, pq_ref, po_ref, tab_ref, hg_ref, bias_ref, grad_ref, slot_ref,
    seq_ref, wq_ref, wo_ref, pre_ref, rot_ref, val_ref, lse_ref, ctx_ref, att_ref, ag_ref, so_ref,
    part, c1, s1, ra, rb, last, gb, sn, hot,
    gs, gr, ps, pr, sr, sl, rs, hs, hr, zsr, zsl, zr, ts, tr, xs, xr,
):
    place, sends = Place(), Sends()
    pc = place
    tok, width = tok_ref.shape
    length = PLANE * tok
    own_rows = pq_ref.shape[1]
    half = heads * HD
    chunks = width // chunk
    scale = HD ** (-0.5)
    greet(place, zn)
    q = ColumnGather(
        place, sends, zn, pq_ref, wq_ref, ps.at[0], pr.at[0], sr.at[0], sl.at[0], rs.at[0]
    )
    o = ColumnGather(
        place, sends, zn, po_ref, wo_ref, ps.at[1], pr.at[1], sr.at[1], sl.at[1], rs.at[1]
    )
    g = RowChain(place, sends, zn, grad_ref, gb, chunk, zsr, zsl, zr)
    q.pair()
    q.own()

    def first_norm(i, carry):
        at = pl.ds(pl.multiple_of(i * 32, 32), 32)
        v = tok_ref[at, :].astype(f32)
        seq_ref[pc.p, at, :] = (v * rms_scale(v) * gain_ref[...]).astype(bf16)
        return carry

    lax.fori_loop(0, tok // 32, first_norm, 0)
    rows = PlaneGather(place, sends, seq_ref, gs, gr)
    rows.first()
    send_slots(place, sends, zn, slot_ref, so_ref, ts, tr)
    q.keep()
    q.partner()
    rows.second()
    o.pair()
    o.keep()
    g.keep()
    rows.third()
    take_slots(place, zn, slot_ref, so_ref, tr)
    make_hot(zn, cap, tok, so_ref, hot)
    pre_ref[...] = jnp.zeros_like(pre_ref)

    def project(origin):
        cols = pl.ds(pl.multiple_of(origin * 2 * own_rows, 2 * own_rows), 2 * own_rows)
        weight = wq_ref.at[pl.ds(2 * origin, 2)]

        def body(i, carry):
            at = pl.ds(pl.multiple_of(i * 2 * tok, 2 * tok), 2 * tok)
            lhs = seq_ref[pl.ds(2 * i, 2), :, cols].reshape(2 * tok, 2 * own_rows)
            pre_ref[at, :] += nn_dot(lhs, weight[...].reshape(2 * own_rows, half + 2 * HD))
            return carry

        lax.fori_loop(0, PLANE // 2, body, 0)

    def project_step(k):
        pl.when(pc.z - k >= 0)(lambda: project(jnp.maximum(pc.z - k, 0)))
        pl.when(pc.z + k < zn)(lambda: project(jnp.minimum(pc.z + k, zn - 1)))

    for k in range(1, zn):
        q.step(k)
        if k == 1:
            rows.last()
            project(pc.z)
        if k == zn - 1:
            for c in range(chunks):
                g.own(c)
            o.own()
            o.partner()
        project_step(k)

    def turn(i, carry):
        at = pl.ds(pl.multiple_of(i * 128, 128), 128)
        cos, sin = tab_ref[0, at, :], tab_ref[1, at, :]
        for h in range(heads + 1):
            v = pre_ref[at, h * HD : (h + 1) * HD]
            gain = hg_ref[pl.ds(0 if h < heads else 1, 1), :]
            v = v * rms_scale(v) * gain
            rot_ref[h, at, :] = (v * cos + turned(v) * sin).astype(bf16)
        val_ref[at, :] = pre_ref[at, half + HD : half + 2 * HD].astype(bf16)
        return carry

    lax.fori_loop(0, length // 128, turn, 0)
    lane = lax.broadcasted_iota(jnp.int32, (QBLOCK, 128), 1)

    def attend(i):
        limit = key_limit(i, length)
        at = slice(i * QBLOCK, (i + 1) * QBLOCK)

        def body(h, carry):
            scores = nt_dot(rot_ref[h, at, :], rot_ref[heads, :limit, :]) * scale
            scores = scores + bias_ref[at, :limit].astype(f32)
            top = jnp.max(scores, axis=1, keepdims=True)
            expo = jnp.exp(scores - top)
            total = jnp.sum(expo, axis=1, keepdims=True)
            low = (expo * (1.0 / total)).astype(bf16)
            cols = pl.ds(pl.multiple_of(h * HD, HD), HD)
            ctx_ref[at, cols] = nn_dot(low, val_ref[:limit, :]).astype(bf16)
            lse_ref[at, :] = jnp.where(lane == h, top + jnp.log(total), lse_ref[at, :])
            return carry

        lax.fori_loop(0, heads, body, 0)

    lse_ref[...] = jnp.zeros_like(lse_ref)
    hops = [(c, k) for k in range(1, zn) for c in range(chunks)]
    blocks = length // QBLOCK
    ahead = min(len(hops), 2 * (blocks - 1))
    done = 0
    for i in range(blocks):
        attend(i)
        while i < blocks - 1 and done < ahead and done < 2 * (i + 1):
            g.step(*hops[done])
            done += 1

    def output(origin):
        cols = pl.ds(pl.multiple_of(origin * 2 * own_rows, 2 * own_rows), 2 * own_rows)
        weight = wo_ref.at[pl.ds(2 * origin, 2)]

        def body(i, carry):
            at = pl.ds(pl.multiple_of(i * 2 * tok, 2 * tok), 2 * tok)
            got = nt_dot(ctx_ref[at, :], weight[...].reshape(2 * own_rows, half))
            part[pl.ds(2 * i, 2), :, cols] = got.astype(bf16).reshape(2, tok, 2 * own_rows)
            return carry

        lax.fori_loop(0, PLANE // 2, body, 0)

    def output_step(k):
        pl.when(pc.z - k >= 0)(lambda: output(jnp.maximum(pc.z - k, 0)))
        pl.when(pc.z + k < zn)(lambda: output(jnp.minimum(pc.z + k, zn - 1)))

    output(pc.z)
    give = PlaneSend(place, sends, hot, gb, sn, ag_ref, chunk, xs, xr)
    for c, k in hops[done:]:
        g.step(c, k)
        if k == zn - 1:
            give.send(c)
    for k in range(1, zn):
        o.step(k)
        output_step(k)
    red = PlaneReduce(place, sends, part, att_ref, (c1, s1, ra, rb, last), hs, hr)
    for k in range(4):
        red.first(k)
    for k in range(4):
        red.second(k)
    red.third()
    red.finish()
    for c in range(chunks):
        give.take(c)
    sends.finish()


def front(zn, cap, heads, tokens, gain, pack_q, pack_o, tables, gains, bias, grad, slot, chunk=512):
    tok, width = tokens.shape
    length = PLANE * tok
    e = 2 * zn
    slots = zn * cap
    chunks = width // chunk
    half = heads * HD
    shape = jax.ShapeDtypeStruct
    return pl.pallas_call(
        functools.partial(front_kernel, zn, cap, chunk, heads),
        out_shape=(
            shape((PLANE, tok, width), bf16),
            shape((e,) + pack_q.shape[1:], bf16),
            shape((e,) + pack_o.shape[1:], bf16),
            shape((length, half + 2 * HD), f32),
            shape((heads + 1, length, HD), bf16),
            shape((length, HD), bf16),
            shape((length, 128), f32),
            shape((length, half), bf16),
            shape((tok, width), f32),
            shape((PLANE, slots, width), bf16),
            shape(slot.shape, f32),
        ),
        in_specs=[VSPEC] * 9,
        out_specs=(VSPEC,) * 11,
        scratch_shapes=[pltpu.VMEM((PLANE, tok, width), bf16)]
        + PlaneReduce.scratch(tok, width)
        + [
            pltpu.VMEM((zn, tok, width), bf16),
            pltpu.VMEM((PLANE, slots, width), bf16),
            pltpu.VMEM((PLANE, slots, zn * tok), bf16),
            dma_sems(8),
            dma_sems(8),
            dma_sems(2),
            dma_sems(2),
            dma_sems(2, e),
            dma_sems(2, e),
            dma_sems(2, e),
            dma_sems(10),
            dma_sems(10),
            dma_sems(chunks, zn),
            dma_sems(chunks, zn),
            dma_sems(chunks, zn),
            dma_sems(zn),
            dma_sems(zn),
            dma_sems(chunks, PLANE),
            dma_sems(chunks, PLANE),
        ],
        compiler_params=params(0),
        name="front",
    )(tokens, gain, pack_q, pack_o, tables, gains, bias, grad, slot)


def send_kernel(
    zn, cap, chunk, norm_ref, slots_ref, mix_ref, an_ref, mr_ref, mo_ref,
    nb, sn, hot, mrow, zsr, zsl, zr, ts, tr, xs, xr, ys, yr,
):
    place, sends = Place(), Sends()
    pc = place
    greet(place, zn)
    tok, width = norm_ref.shape
    slots = zn * cap
    chunks = width // chunk
    n = RowChain(place, sends, zn, norm_ref, nb, chunk, zsr, zsl, zr)
    send_slots(place, sends, zn, mix_ref, mo_ref, ts, tr)
    for c in range(chunks):
        n.own(c)
    n.keep()
    make_hot(zn, cap, tok, slots_ref, hot)
    take_slots(place, zn, mix_ref, mo_ref, tr)

    def mixes(p, carry):
        row = jnp.concatenate([mo_ref[z, pl.ds(p, 1), :] for z in range(zn)], axis=1)
        high = row.astype(bf16)
        rest = row - high.astype(f32)
        middle = rest.astype(bf16)
        low = (rest - middle.astype(f32)).astype(bf16)
        zero = jnp.zeros((13, zn * tok), bf16)
        got = nt_dot(jnp.concatenate([high, middle, low, zero], axis=0), hot[p])
        mrow[p] = jnp.sum(got, axis=0, keepdims=True)
        return carry

    lax.fori_loop(0, PLANE, mixes, 0)
    for k in range(1, PLANE):
        p = pc.by(k)
        sends.start(mrow.at[p], mr_ref.at[pc.p], ys.at[k], yr.at[k], pc.at(pc.z, p))
    mr_ref[pc.p] = mrow[pc.p]
    give = PlaneSend(place, sends, hot, nb, sn, an_ref, chunk, xs, xr)
    for c in range(chunks):
        for k in range(1, zn):
            n.step(c, k)
        give.send(c)
    for k in range(1, PLANE):
        arrived(mr_ref.at[pc.by(k)], yr.at[k])
    for c in range(chunks):
        give.take(c)
    sends.finish()


def send_rows(zn, cap, norm, slots_all, mix, chunk=512):
    tok, width = norm.shape
    slots = zn * cap
    chunks = width // chunk
    return pl.pallas_call(
        functools.partial(send_kernel, zn, cap, chunk),
        out_shape=(
            jax.ShapeDtypeStruct((PLANE, slots, width), bf16),
            jax.ShapeDtypeStruct((PLANE, 1, slots), f32),
            jax.ShapeDtypeStruct(mix.shape, f32),
        ),
        in_specs=[VSPEC] * 3,
        out_specs=(VSPEC,) * 3,
        scratch_shapes=[
            pltpu.VMEM((zn, tok, width), bf16),
            pltpu.VMEM((PLANE, slots, width), bf16),
            pltpu.VMEM((PLANE, slots, zn * tok), bf16),
            pltpu.VMEM((PLANE, 1, slots), f32),
            dma_sems(chunks, zn),
            dma_sems(chunks, zn),
            dma_sems(chunks, zn),
            dma_sems(zn),
            dma_sems(zn),
            dma_sems(chunks, PLANE),
            dma_sems(chunks, PLANE),
            dma_sems(PLANE),
            dma_sems(PLANE),
        ],
        compiler_params=params(3),
        name="send_rows",
    )(norm, slots_all, mix)


def back_kernel(
    zn, chunk, pair_ref, dot_ref, hot_ref, sum_ref, dots_ref,
    rp, rd, zd, zp, ap, xs, xr, ds, dr, zs, zr, es, er,
):
    place, sends = Place(), Sends()
    pc = place
    greet(place, zn)
    _, slots, width = pair_ref.shape
    chunks = width // chunk
    tok = sum_ref.shape[0]
    far = [(pc.z + k) % zn for k in range(1, zn)]
    for k in range(1, PLANE):
        p = pc.by(k)
        sends.start(dot_ref.at[p], rd.at[pc.p], ds.at[k], dr.at[k], pc.at(pc.z, p))
    for c in range(chunks):
        cols = pl.ds(c * chunk, chunk)
        for k in range(1, PLANE):
            p = pc.by(k)
            sends.start(
                pair_ref.at[p, :, cols],
                rp.at[pc.p, :, cols],
                xs.at[c, k],
                xr.at[c, k],
                pc.at(pc.z, p),
            )
    rd[pc.p] = dot_ref[pc.p]
    rp[pc.p] = pair_ref[pc.p]
    for k in range(1, PLANE):
        arrived(rd.at[pc.by(k)], dr.at[k])
    zd[...] = nn_dot(hot_ref[...], rd[...].reshape(PLANE * slots, 128)).reshape(zn, tok, 128)
    for k, d in enumerate(far):
        sends.start(zd.at[d], dots_ref.at[pc.z], es.at[k], er.at[pc.z], pc.at(d, pc.p))
    dots_ref[pc.z] = zd[pc.z]
    for c in range(chunks):
        cols = pl.ds(c * chunk, chunk)
        for k in range(1, PLANE):
            arrived(rp.at[pc.by(k), :, cols], xr.at[c, k])
        got = nn_dot(hot_ref[...], rp[:, :, cols].reshape(PLANE * slots, chunk))
        zp[:, :, cols] = got.astype(bf16).reshape(zn, tok, chunk)
        for k, d in enumerate(far):
            sends.start(
                zp.at[d, :, cols],
                ap.at[pc.z, :, cols],
                zs.at[c, k],
                zr.at[c, pc.z],
                pc.at(d, pc.p),
            )
    for c in range(chunks):
        cols = pl.ds(c * chunk, chunk)
        total = zp[pc.z, :, cols].astype(f32)
        for d in far:
            arrived(ap.at[d, :, cols], zr.at[c, d])
            total = total + ap[d, :, cols].astype(f32)
        sum_ref[:, cols] = total
    for d in far:
        arrived(dots_ref.at[d], er.at[d])
    sends.finish()


def back_rows(zn, tok, pair, dots, hot, chunk=512):
    _, slots, width = pair.shape
    chunks = width // chunk
    return pl.pallas_call(
        functools.partial(back_kernel, zn, chunk),
        out_shape=(
            jax.ShapeDtypeStruct((tok, width), f32),
            jax.ShapeDtypeStruct((zn, tok, 128), f32),
        ),
        in_specs=[VSPEC] * 3,
        out_specs=(VSPEC,) * 2,
        scratch_shapes=[
            pltpu.VMEM((PLANE, slots, width), bf16),
            pltpu.VMEM((PLANE, slots, 128), bf16),
            pltpu.VMEM((zn, tok, 128), f32),
            pltpu.VMEM((zn, tok, width), bf16),
            pltpu.VMEM((zn, tok, width), bf16),
            dma_sems(chunks, PLANE),
            dma_sems(chunks, PLANE),
            dma_sems(PLANE),
            dma_sems(PLANE),
            dma_sems(chunks, zn),
            dma_sems(chunks, zn),
            dma_sems(zn),
            dma_sems(zn),
        ],
        compiler_params=params(4),
        name="back_rows",
    )(pair, dots, hot)


class ColumnReduce:
    def __init__(self, place, sends, zn, part, buf, ss_r, ss_l, rs_r, rs_l):
        self.place, self.sends, self.zn = place, sends, zn
        self.part, self.buf = part, buf
        self.ss_r, self.ss_l, self.rs_r, self.rs_l = ss_r, ss_l, rs_r, rs_l

    def _hop(self, slot, rs, ss, d, start, inner, device):
        rows = self.part.shape[1]

        def add():
            arrived(self.buf.at[slot], rs.at[d])

            def put(at, v):
                self.buf[slot, at, :] = v.astype(bf16)

            add_rows(put, lambda at: self.part[d, at, :], lambda at: self.buf[slot, at, :], rows)

        both = jnp.logical_and(start, inner)
        pl.when(both)(add)
        self.sends.start(
            self.buf.at[slot], self.buf.at[slot], ss.at[d], rs.at[d], device, both
        )
        self.sends.start(
            self.part.at[d],
            self.buf.at[slot],
            ss.at[d],
            rs.at[d],
            device,
            jnp.logical_and(start, jnp.logical_not(inner)),
        )

    def step(self, k):
        pc, zn = self.place, self.zn
        d = zn - 1 - k
        right = pc.at(jnp.minimum(pc.z + 1, zn - 1), pc.p)
        left = pc.at(jnp.maximum(pc.z - 1, 0), pc.p)
        self._hop(d + 1, self.rs_r, self.ss_r, d, pc.z < d, pc.z > 0, right)
        d = k
        self._hop(d, self.rs_l, self.ss_l, d, pc.z > d, pc.z < zn - 1, left)

    def own(self, use, step=32):
        pc, zn = self.place, self.zn
        lower, upper = pc.z > 0, pc.z < zn - 1
        arrived(self.buf.at[pc.z + 1], self.rs_r.at[pc.z], lower)
        arrived(self.buf.at[pc.z], self.rs_l.at[pc.z], upper)

        def body(i, carry):
            at = pl.ds(pl.multiple_of(i * step, step), step)
            v = self.part[pc.z, at, :].astype(f32)
            v = v + jnp.where(lower, self.buf[pc.z + 1, at, :].astype(f32), 0.0)
            v = v + jnp.where(upper, self.buf[pc.z, at, :].astype(f32), 0.0)
            use(at, v)
            return carry

        lax.fori_loop(0, self.part.shape[1] // step, body, 0)


class SmallSum:
    @staticmethod
    def scratch(zn, rows, lanes):
        return [
            pltpu.VMEM((PLANE, rows, lanes), f32),
            pltpu.VMEM((rows, lanes), f32),
            pltpu.VMEM((zn, rows, lanes), f32),
            dma_sems(PLANE),
            dma_sems(PLANE),
            dma_sems(zn),
            dma_sems(zn),
            dma_sems(PLANE),
            dma_sems(PLANE),
        ]

    def __init__(self, place, sends, zn, flat, out, scratch):
        self.place, self.sends, self.zn, self.flat, self.out = place, sends, zn, flat, out
        self.l1, self.mid, self.l2, self.a, self.ar, self.b, self.br, self.c, self.cr = scratch

    def first(self):
        pc = self.place
        for k in range(1, PLANE):
            p = pc.by(k)
            self.sends.start(
                self.flat.at[p], self.l1.at[pc.p], self.a.at[k], self.ar.at[k], pc.at(pc.z, p)
            )
        self.l1[pc.p] = self.flat[pc.p]

    def second(self):
        pc, zn = self.place, self.zn
        for k in range(1, PLANE):
            arrived(self.l1.at[pc.by(k)], self.ar.at[k])
        total = self.l1[0]
        for k in range(1, PLANE):
            total = total + self.l1[k]
        self.mid[...] = total
        self.l2[pc.z] = total
        for k in range(1, zn):
            d = (pc.z + k) % zn
            self.sends.start(
                self.mid, self.l2.at[pc.z], self.b.at[k], self.br.at[pc.z], pc.at(d, pc.p)
            )

    def _column(self):
        pc, zn = self.place, self.zn
        for k in range(1, zn):
            d = (pc.z + k) % zn
            arrived(self.l2.at[d], self.br.at[d])
        total = self.l2[0]
        for z in range(1, zn):
            total = total + self.l2[z]
        return total

    def third(self):
        pc = self.place
        self.out[pc.p] = self._column()
        for k in range(1, PLANE):
            p = pc.by(k)
            self.sends.start(
                self.out.at[pc.p], self.out.at[pc.p], self.c.at[k], self.cr.at[k], pc.at(pc.z, p)
            )

    def last(self):
        pc = self.place
        for k in range(1, PLANE):
            arrived(self.out.at[pc.by(k)], self.cr.at[k])


class TinySum:
    @staticmethod
    def scratch(zn, lanes):
        return [
            pltpu.VMEM((1, lanes), f32),
            pltpu.VMEM((PLANE, 1, lanes), f32),
            pltpu.VMEM((1, lanes), f32),
            pltpu.VMEM((zn, 1, lanes), f32),
            dma_sems(PLANE),
            dma_sems(PLANE),
            dma_sems(zn),
            dma_sems(zn),
        ]

    def __init__(self, place, sends, zn, out, scratch):
        self.place, self.sends, self.zn, self.out = place, sends, zn, out
        self.vec, self.l1, self.mid, self.l2, self.a, self.ar, self.b, self.br = scratch

    def first(self):
        pc = self.place
        for k in range(1, PLANE):
            p = pc.by(k)
            self.sends.start(
                self.vec, self.l1.at[pc.p], self.a.at[k], self.ar.at[k], pc.at(pc.z, p)
            )
        self.l1[pc.p] = self.vec[...]

    def second(self):
        pc, zn = self.place, self.zn
        for k in range(1, PLANE):
            arrived(self.l1.at[pc.by(k)], self.ar.at[k])
        total = self.l1[0]
        for k in range(1, PLANE):
            total = total + self.l1[k]
        self.mid[...] = total
        self.l2[pc.z] = total
        for k in range(1, zn):
            d = (pc.z + k) % zn
            self.sends.start(
                self.mid, self.l2.at[pc.z], self.b.at[k], self.br.at[pc.z], pc.at(d, pc.p)
            )

    def last(self):
        pc, zn = self.place, self.zn
        for k in range(1, zn):
            d = (pc.z + k) % zn
            arrived(self.l2.at[d], self.br.at[d])
        total = self.l2[0]
        for z in range(1, zn):
            total = total + self.l2[z]
        self.out[...] = total


class Result:
    def __init__(self, place, zn, res, comb, rr, am, rbuf, zbuf, chunk, xs, xr, zs, zr, ls, os):
        self.place, self.zn, self.res, self.comb = place, zn, res, comb
        self.rr, self.am, self.rbuf, self.zbuf, self.chunk = rr, am, rbuf, zbuf, chunk
        self.xs, self.xr, self.zs, self.zr, self.ls, self.os = xs, xr, zs, zr, ls, os
        self.flight = {}

    def first(self, sends, chunks):
        pc = self.place
        for c in range(chunks):
            cols = pl.ds(c * self.chunk, self.chunk)
            for k in range(1, PLANE):
                p = pc.by(k)
                sends.start(
                    self.res.at[p, :, cols],
                    self.rr.at[pc.p, :, cols],
                    self.xs.at[c, k],
                    self.xr.at[c, k],
                    pc.at(pc.z, p),
                )

    def mix(self, c):
        pc, zn = self.place, self.zn
        cols = pl.ds(c * self.chunk, self.chunk)
        own = pltpu.make_async_copy(self.res.at[pc.p, :, cols], self.rbuf.at[pc.p], self.ls.at[0])
        own.start()
        copies = []
        for k in range(1, PLANE):
            p = pc.by(k)
            arrived(self.rr.at[p, :, cols], self.xr.at[c, k])
            copy = pltpu.make_async_copy(self.rr.at[p, :, cols], self.rbuf.at[p], self.ls.at[k])
            copy.start()
            copies.append(copy)
        own.wait()
        for copy in copies:
            copy.wait()
        self.settle(c - 2)
        slot = c % 2
        _, slots, chunk = self.rbuf.shape
        tok = self.zbuf.shape[2]
        unit = min(512, zn * tok)
        per = unit // tok
        rows = self.rbuf[...].reshape(PLANE * slots, chunk)
        for i in range(zn * tok // unit):
            got = nn_dot(self.comb[i * unit : (i + 1) * unit, :], rows)
            self.zbuf[slot, i * per : (i + 1) * per] = got.astype(bf16).reshape(per, tok, chunk)
        flight = []
        for k in range(1, zn):
            d = (pc.z + k) % zn
            flight.append(
                pltpu.make_async_remote_copy(
                    src_ref=self.zbuf.at[slot, d],
                    dst_ref=self.am.at[pc.z, :, cols],
                    send_sem=self.zs.at[c, k],
                    recv_sem=self.zr.at[c, pc.z],
                    device_id=pc.at(d, pc.p),
                    device_id_type=MESH,
                )
            )
        for copy in flight:
            copy.start()
        keep = pltpu.make_async_copy(
            self.zbuf.at[slot, pc.z], self.am.at[pc.z, :, cols], self.os.at[c]
        )
        keep.start()
        self.flight[c] = (flight, keep)

    def settle(self, c):
        if c in self.flight:
            flight, keep = self.flight.pop(c)
            for copy in flight:
                copy.wait_send()
            keep.wait()

    def last(self, chunks):
        pc, zn = self.place, self.zn
        for c in range(chunks):
            self.settle(c)
            for k in range(1, zn):
                d = (pc.z + k) % zn
                arrived(self.am.at[d, :, pl.ds(c * self.chunk, self.chunk)], self.zr.at[c, d])


def rear_kernel(
    zn, chunk, heads,
    mid_ref, tok_ref, gain_ref, hg_ref, flat_ref, comb_ref,
    res_hbm, seq_hbm, wq_hbm, wo_hbm, pre_hbm, rot_hbm, val_hbm, lse_hbm, ctx_hbm, tab_hbm, bias_hbm,
    grad_ref, oq_ref, oo_ref, sum_ref, tiny_ref, am_hbm, rr_hbm,
    big, wq, wo, pre, rot, val, lse, ctx, tab, bias,
    lse_t, del_t, key_t, cback, aback, dk, dv, dgain,
    gq, bq, vq, tq, go, bo, vo, to,
    c1, s1, ra, rb, last, rbuf, zbuf,
    gs, gr, hs, hr, sr, sl, rr, rl, ps, pr, xs, xr, zs, zr, ls, os, loads,
    *rest,
):
    place, sends = Place(), Sends()
    pc = place
    small_scratch, tiny_scratch = rest[:9], rest[9:]
    tok, width = mid_ref.shape
    length = PLANE * tok
    half = heads * HD
    own_rows = wq.shape[1]
    chunks = width // chunk
    scale = HD ** (-0.5)
    greet(place, zn)
    pairs = (
        (wo_hbm, wo), (ctx_hbm, ctx), (rot_hbm, rot), (val_hbm, val), (lse_hbm, lse),
        (bias_hbm, bias), (pre_hbm, pre), (tab_hbm, tab), (wq_hbm, wq),
    )
    fetch = [pltpu.make_async_copy(a, b, loads.at[i]) for i, (a, b) in enumerate(pairs)]
    small = SmallSum(place, sends, zn, flat_ref, sum_ref, small_scratch)
    tiny = TinySum(place, sends, zn, tiny_ref, tiny_scratch)
    row_sends = Sends()
    rows = PlaneGather(place, row_sends, big, gs, gr)
    result = Result(
        place, zn, res_hbm, comb_ref, rr_hbm, am_hbm, rbuf, zbuf, chunk, xs, xr, zs, zr, ls, os
    )
    o = ColumnReduce(place, sends, zn, go, bo, sr.at[1], sl.at[1], rr.at[1], rl.at[1])
    q = ColumnReduce(place, sends, zn, gq, bq, sr.at[0], sl.at[0], rr.at[0], rl.at[0])

    def stage(i, carry):
        at = pl.ds(pl.multiple_of(i * 32, 32), 32)
        big[pc.p, at, :] = mid_ref[at, :].astype(bf16)
        return carry

    lax.fori_loop(0, tok // 32, stage, 0)
    rows.first()
    for copy in fetch:
        copy.start()
    small.first()
    rows.second()
    rows.third()
    for copy in fetch[:6]:
        copy.wait()
    key_t[...] = rot[heads].astype(f32).T.astype(bf16)
    lse_t[...] = lse[...].T
    small.second()
    rows.last()
    result.first(sends, chunks)

    order = []
    for k in range(zn):
        for d in (zn - 1 - k, k):
            if d not in order:
                order.append(d)

    def output_grad(d):
        cols = pl.ds(d * 2 * own_rows, 2 * own_rows)
        rhs = big[:, :, cols].reshape(length, 2 * own_rows)

        def body(i, carry):
            m = pl.ds(pl.multiple_of(i * 256, 256), 256)
            go[d, m, :] = tn_dot(ctx[:, m], rhs).astype(bf16)
            return carry

        lax.fori_loop(0, half // 256, body, 0)

    made = 0
    for k in range(1):
        while made < len(order) and not {zn - 1 - k, k} <= set(order[:made]):
            output_grad(order[made])
            made += 1
        o.step(k)

    def context_back(i, carry):
        at = pl.ds(pl.multiple_of(i * 2 * tok, 2 * tok), 2 * tok)
        lhs = big[pl.ds(2 * i, 2)].reshape(2 * tok, width)
        got = nn_dot(lhs, wo[...].reshape(width, half))
        cback[at, :] = got.astype(bf16)
        prod = got.astype(bf16).astype(f32) * ctx[at, :].astype(f32)
        for h in range(heads):
            s = jnp.sum(prod[:, h * HD : (h + 1) * HD], axis=1, keepdims=True)
            lse[at, h : h + 1] = s
        return carry

    lax.fori_loop(0, PLANE // 2, context_back, 0)
    while made < len(order):
        output_grad(order[made])
        made += 1
    del_t[...] = lse[...].T
    row_sends.finish()
    fill = pltpu.make_async_copy(seq_hbm, big, loads.at[len(pairs)])
    fill.start()
    small.third()
    dk[...] = jnp.zeros_like(dk)
    dv[...] = jnp.zeros_like(dv)
    dgain[...] = jnp.zeros_like(dgain)
    for copy in fetch[6:]:
        copy.wait()

    def norm_of(d, at, h, gain_row):
        d = d * tab[0, at, :] - turned(d) * tab[1, at, :]
        v = pre[at, pl.ds(h * HD if isinstance(h, int) else pl.multiple_of(h * HD, HD), HD)]
        r = rms_scale(v)
        hat = v * r
        s = d * hg_ref[pl.ds(gain_row, 1), :]
        got = r * (s - hat * jnp.mean(s * hat, axis=1, keepdims=True))
        dgain[pl.ds(gain_row, 1), :] += jnp.sum(d * hat, axis=0, keepdims=True)
        return got.astype(bf16)

    def attend(i):
        limit = key_limit(i, length)
        at = slice(i * QBLOCK, (i + 1) * QBLOCK)

        def body(h, carry):
            cols = pl.ds(pl.multiple_of(h * HD, HD), HD)
            query = rot[h, at, :]
            dctx = cback[at, cols]
            scores = nt_dot(rot[heads, :limit, :], query) * scale
            scores = scores + bias[:limit, at].astype(f32)
            probs = jnp.exp(scores - lse_t[pl.ds(h, 1), at])
            dprobs = nt_dot(val[:limit, :], dctx)
            dscores = (probs * (dprobs - del_t[pl.ds(h, 1), at])).astype(bf16)
            dv[:limit, :] += nn_dot(probs.astype(bf16), dctx)
            dk[:limit, :] += nn_dot(dscores, query)
            dq = nn_dot(key_t[:, :limit], dscores).T * scale
            aback[at, cols] = norm_of(dq, at, h, 0)
            return carry

        lax.fori_loop(0, heads, body, 0)

    blocks = length // QBLOCK
    hop = 1
    for i in range(blocks):
        attend(i)
        if i % 2 == 1 and hop < zn - 1:
            o.step(hop)
            hop += 1
        if i == 2:
            result.mix(0)
    while hop < zn - 1:
        o.step(hop)
        hop += 1

    def keys(i, carry):
        at = pl.ds(pl.multiple_of(i * 256, 256), 256)
        aback[at, half : half + HD] = norm_of(dk[at, :] * scale, at, heads, 1)
        aback[at, half + HD : half + 2 * HD] = dv[at, :].astype(bf16)
        return carry

    lax.fori_loop(0, length // 256, keys, 0)
    fill.wait()

    def query_grad(d):
        for h in range(2):
            cols = pl.ds((2 * d + h) * own_rows, own_rows) if own_rows % 128 == 0 else None
            if cols is None:
                lhs = big[:, :, pl.ds(2 * d * own_rows, 2 * own_rows)]
                lhs = lhs.reshape(length, 2 * own_rows)
                if h == 0:
                    gq[d] = tn_dot(lhs, aback[...]).astype(bf16)
            else:
                lhs = big[:, :, cols].reshape(length, own_rows)
                gq[d, h * own_rows : (h + 1) * own_rows, :] = tn_dot(lhs, aback[...]).astype(bf16)

    made = 0
    for k in range(zn - 1):
        while made < len(order) and not {zn - 1 - k, k} <= set(order[:made]):
            query_grad(order[made])
            made += 1
        if k == 0:
            q.step(0)
    while made < len(order):
        query_grad(order[made])
        made += 1

    red = PlaneReduce(place, sends, big, grad_ref, (c1, s1, ra, rb, last), hs, hr)

    def norm1_part(k):
        y, x, j = red._chip(*red.chips[k])
        lhs = aback[pl.ds(pl.multiple_of(j * 2 * tok, 2 * tok), 2 * tok), :]

        def body(i, carry):
            cols = pl.ds(pl.multiple_of(i * chunk, chunk), chunk)
            e = i * (chunk // own_rows)
            rhs = wq[pl.ds(e, chunk // own_rows)].reshape(chunk, half + 2 * HD)
            big[pl.ds(j * 2, 2), :, cols] = nt_dot(lhs, rhs).astype(bf16).reshape(2, tok, chunk)
            return carry

        lax.fori_loop(0, width // chunk, body, 0)

    for k in range(4):
        norm1_part(k)
        red.first(k)
    if zn > 2:
        q.step(1)
    for k in range(4):
        red.second(k)
    red.third()
    result.mix(1)
    for k in range(2, zn - 1):
        q.step(k)
    result.mix(2)
    red.finish()

    def tokens_back(i, carry):
        at = pl.ds(pl.multiple_of(i * 16, 16), 16)
        v = tok_ref[at, :].astype(f32)
        r = rms_scale(v)
        hat = v * r
        d = grad_ref[at, :]
        s = d * gain_ref[...]
        got = r * (s - hat * jnp.mean(s * hat, axis=1, keepdims=True))
        grad_ref[at, :] = mid_ref[at, :] + got
        return carry + jnp.sum(d * hat, axis=0, keepdims=True)

    total = lax.fori_loop(0, tok // 16, tokens_back, jnp.zeros((1, width), f32))
    tiny.vec[:, :width] = total
    tiny.vec[:, width : width + HD] = dgain[0:1, :]
    tiny.vec[:, width + HD : width + 2 * HD] = dgain[1:2, :]
    tiny.first()
    for c in range(3, chunks):
        result.mix(c)

    def split_o(at, v):
        first, second = v[:, :own_rows], v[:, own_rows:]
        low = pc.y == 0
        vo[at, :] = jnp.where(low, second, first).astype(bf16)
        oo_ref[pc.y, at, :] = jnp.where(low, first, second)

    o.own(split_o)
    sends.start(vo, to, ps.at[1], pr.at[1], pc.peer(dy=1))
    tiny.second()
    q_own(q, pc, zn, gq, bq, vq, oq_ref, own_rows)
    sends.start(vq, tq, ps.at[0], pr.at[0], pc.peer(dy=1))
    tiny.last()
    small.last()
    result.last(chunks)
    arrived(to, pr.at[1])
    oo_ref[1 - pc.y] = to[...].astype(f32)
    arrived(tq, pr.at[0])
    oq_ref[1 - pc.y] = tq[...].astype(f32)
    sends.finish()


def q_own(q, pc, zn, part, buf, give, out, rows, step=32):
    lower, upper = pc.z > 0, pc.z < zn - 1
    arrived(buf.at[pc.z + 1], q.rs_r.at[pc.z], lower)
    arrived(buf.at[pc.z], q.rs_l.at[pc.z], upper)

    def total(at):
        v = part[pc.z, at, :].astype(f32)
        v = v + jnp.where(lower, buf[pc.z + 1, at, :].astype(f32), 0.0)
        return v + jnp.where(upper, buf[pc.z, at, :].astype(f32), 0.0)

    def body(i, carry):
        at = pl.ds(pl.multiple_of(i * step, step), step)
        theirs = pl.ds(pl.multiple_of((1 - pc.y) * rows + i * step, step), step)
        mine = pl.ds(pl.multiple_of(pc.y * rows + i * step, step), step)
        give[at, :] = total(theirs).astype(bf16)
        out[pc.y, at, :] = total(mine)
        return carry

    lax.fori_loop(0, rows // step, body, 0)


def rear(
    zn, heads, middle, tokens, gain, gains, flat, comb, res, seq, full_q, full_o, pre, rot, val, lse,
    ctx, tables, bias, chunk=512,
):
    tok, width = tokens.shape
    length = PLANE * tok
    e, own_rows, wide = full_q.shape
    half = heads * HD
    chunks = width // chunk
    slots = res.shape[1]
    lanes = width + 2 * HD
    shape = jax.ShapeDtypeStruct
    vmem = pltpu.VMEM
    return pl.pallas_call(
        functools.partial(rear_kernel, zn, chunk, heads),
        out_shape=(
            shape((tok, width), f32),
            shape((2, own_rows, wide), f32),
            shape((2, half, own_rows), f32),
            shape(flat.shape, f32),
            shape((1, lanes), f32),
            shape((zn, tok, width), bf16),
            shape((PLANE, slots, width), bf16),
        ),
        in_specs=[VSPEC] * 6 + [ASPEC] * 11,
        out_specs=(VSPEC,) * 5 + (ASPEC,) * 2,
        scratch_shapes=[
            vmem((PLANE, tok, width), bf16),
            vmem((e, own_rows, wide), bf16),
            vmem((e, own_rows, half), bf16),
            vmem((length, wide), f32),
            vmem((heads + 1, length, HD), bf16),
            vmem((length, HD), bf16),
            vmem((length, 128), f32),
            vmem((length, half), bf16),
            vmem((2, length, HD), f32),
            vmem((length, length), bf16),
            vmem((128, length), f32),
            vmem((128, length), f32),
            vmem((HD, length), bf16),
            vmem((length, half), bf16),
            vmem((length, wide), bf16),
            vmem((length, HD), f32),
            vmem((length, HD), f32),
            vmem((8, HD), f32),
            vmem((zn, 2 * own_rows, wide), bf16),
            vmem((zn + 1, 2 * own_rows, wide), bf16),
            vmem((own_rows, wide), bf16),
            vmem((own_rows, wide), bf16),
            vmem((zn, half, 2 * own_rows), bf16),
            vmem((zn + 1, half, 2 * own_rows), bf16),
            vmem((half, own_rows), bf16),
            vmem((half, own_rows), bf16),
        ]
        + PlaneReduce.scratch(tok, width)
        + [
            vmem((PLANE, slots, chunk), bf16),
            vmem((2, zn, tok, chunk), bf16),
            dma_sems(8),
            dma_sems(8),
            dma_sems(10),
            dma_sems(10),
            dma_sems(2, zn),
            dma_sems(2, zn),
            dma_sems(2, zn),
            dma_sems(2, zn),
            dma_sems(2),
            dma_sems(2),
            dma_sems(chunks, PLANE),
            dma_sems(chunks, PLANE),
            dma_sems(chunks, zn),
            dma_sems(chunks, zn),
            dma_sems(PLANE),
            dma_sems(chunks),
            dma_sems(10),
        ]
        + SmallSum.scratch(zn, flat.shape[1], flat.shape[2])
        + TinySum.scratch(zn, lanes),
        compiler_params=params(5),
        name="rear",
    )(
        middle, tokens, gain, gains, flat, comb, res, seq, full_q, full_o, pre, rot, val, lse, ctx,
        tables, bias,
    )


def local(
    tokens,
    out_grad,
    first_gain,
    second_gain,
    query_gain,
    key_gain,
    query_weight,
    key_weight,
    value_weight,
    output_weight,
    router_weight,
    gate_weight,
    up_weight,
    down_weight,
    expert_ids,
    router_order,
    image_starts,
):
    tok, width = tokens.shape
    zn = lax.axis_size("exp") // 2
    experts = PLANE * zn
    cap = (9 * tok * TOP + 8 * experts - 1) // (8 * experts)
    slots = zn * cap
    length = PLANE * tok
    own_rows = query_weight.shape[0]
    half = query_weight.shape[1] // 2
    heads = half // HD
    scale = HD ** (-0.5)
    exp_index = lax.axis_index("exp")
    starts = lax.dynamic_slice_in_dim(image_starts, exp_index // 2, 1, 0)[0]

    expert_axis = jnp.arange(experts, dtype=jnp.int32)
    member = jnp.any(expert_ids[:, :, None] == expert_axis[None, None, :], axis=1)
    order_here = router_order[0]
    earlier = (order_here[None, :] < order_here[:, None]).astype(bf16)
    counts = jnp.dot(earlier, member.astype(bf16), preferred_element_type=f32)
    keep = member & (counts < cap)
    slot_of = jnp.where(keep, counts, -1.0)

    resid_in = tokens.astype(f32)
    first_rms = rms_scale(resid_in)
    first_hat = resid_in * first_rms
    first_norm = (first_hat * first_gain).astype(bf16)
    q_halves = query_weight.reshape(own_rows, 2, half).transpose(1, 0, 2)
    kv = jnp.concatenate([key_weight, value_weight], axis=1)
    pack_q = jnp.concatenate([q_halves, jnp.broadcast_to(kv[None], (2,) + kv.shape)], axis=2)
    pack_o = output_weight.reshape(2, half, own_rows).transpose(0, 2, 1)
    pos = jnp.arange(length, dtype=jnp.int32)
    cosine, sine = rotary_tables(pos, HD)
    tables = jnp.stack(
        [jnp.concatenate([cosine, cosine], axis=1), jnp.concatenate([-sine, sine], axis=1)]
    )
    pieces = piece_ids(pos, starts)
    mask = allowed_mask(pos, pos, pieces, pieces)
    bias = jnp.where(mask, 0.0, NEGATIVE).astype(bf16)
    slot_t = slot_of.T.reshape(zn, PLANE, tok)
    (
        seq_norm, full_q, full_o, pre, rot, value_rows, lse, context_rows, attention, rows_g, slots_all,
    ) = front(
        zn, cap, heads, tokens, first_gain[None], pack_q, pack_o, tables,
        jnp.stack([query_gain, key_gain]), bias, out_grad, slot_t,
    )
    resid_mid = resid_in + attention
    second_rms = rms_scale(resid_mid)
    second_hat = resid_mid * second_rms
    second_norm = (second_hat * second_gain).astype(bf16)
    logits = jnp.dot(second_norm, router_weight, preferred_element_type=f32)
    mix = jax.nn.softmax(jnp.where(member, logits, NEGATIVE), axis=-1)
    mix = jnp.where(member, mix, 0.0)
    keep_mix = jnp.where(keep, mix, 0.0)
    mix_t = keep_mix.T.reshape(zn, PLANE, tok)
    rows_n, mix_rows, mix_all = send_rows(zn, cap, second_norm, slots_all, mix_t)
    mix_rows = mix_rows.reshape(PLANE * slots, 1)
    arrived_n = rows_n.reshape(PLANE * slots, width)
    arrived_g = rows_g.reshape(PLANE * slots, width)

    gate_val = jnp.dot(arrived_n, gate_weight[0], preferred_element_type=f32)
    up_val = jnp.dot(arrived_n, up_weight[0], preferred_element_type=f32)
    gate_sig = jax.nn.sigmoid(gate_val)
    gate_act = gate_val * gate_sig
    inner = (gate_act * up_val).astype(bf16)
    result = jnp.dot(inner, down_weight[0], preferred_element_type=f32).astype(bf16)
    unmixed = jnp.dot(arrived_g, down_weight[0].T, preferred_element_type=f32)
    dots = mix_rows * jnp.sum(unmixed * inner.astype(f32), axis=1, keepdims=True)
    inner_grad = unmixed * mix_rows
    mixed_inner = (inner.astype(f32) * mix_rows).astype(bf16)
    down_grad = jnp.dot(mixed_inner.T, arrived_g, preferred_element_type=f32)[None]
    gate_back = (inner_grad * up_val * gate_sig * (1.0 + gate_val * (1.0 - gate_sig))).astype(bf16)
    up_back = (inner_grad * gate_act).astype(bf16)
    gate_grad = jnp.dot(arrived_n.T, gate_back, preferred_element_type=f32)[None]
    up_grad = jnp.dot(arrived_n.T, up_back, preferred_element_type=f32)[None]
    pair_back = jnp.dot(gate_back, gate_weight[0].T, preferred_element_type=f32) + jnp.dot(
        up_back, up_weight[0].T, preferred_element_type=f32
    )
    pair_back = pair_back.astype(bf16)
    dots_high = dots.astype(bf16)
    dots_low = (dots - dots_high.astype(f32)).astype(bf16)
    place = (exp_index % 2) * 4 + lax.axis_index("tp")
    lane = jnp.arange(128, dtype=jnp.int32)[None, :]
    zero = jnp.zeros((), bf16)
    dot_lanes = jnp.where(lane == place, dots_high, zero) + jnp.where(
        lane == place + PLANE, dots_low, zero
    )

    slot_col = slots_all.transpose(0, 2, 1).reshape(zn, tok, PLANE, 1)
    mix_col = mix_all.transpose(0, 2, 1).reshape(zn, tok, PLANE, 1)
    want = jnp.where(slot_col < 0, -1.0, slot_col + (jnp.arange(zn, dtype=f32) * cap)[:, None, None, None])
    hot = want == jnp.arange(slots, dtype=f32)[None, None, None, :]
    comb = jnp.where(hot, mix_col, 0.0).astype(bf16).reshape(zn * tok, PLANE * slots)
    hot = hot.astype(bf16).reshape(zn * tok, PLANE * slots)
    pairs_sum, dots_all = back_rows(
        zn, tok, pair_back.reshape(PLANE, slots, width), dot_lanes.reshape(PLANE, slots, 128), hot
    )
    grad_out = out_grad.astype(f32)
    mix_dots = dots_all[:, :, :PLANE] + dots_all[:, :, PLANE : 2 * PLANE]
    mix_dots = mix_dots.transpose(1, 0, 2).reshape(tok, experts)
    chosen_grad = mix_dots - mix * jnp.sum(mix_dots, axis=1, keepdims=True)
    logit_grad = chosen_grad.astype(bf16)
    router_part = jnp.dot(second_norm.T, logit_grad, preferred_element_type=f32)
    norm2_back = pairs_sum + jnp.dot(logit_grad, router_weight.T, preferred_element_type=f32)
    mid_from_norm, second_gain_part = norm_back(norm2_back, second_hat, second_rms, second_gain)
    middle_grad = grad_out + mid_from_norm

    flat = jnp.concatenate([router_part.reshape(-1), second_gain_part])
    count = flat.shape[0]
    unit = PLANE * 8 * 128
    padded = -(-count // unit) * unit
    flat = jnp.pad(flat, (0, padded - count)).reshape(PLANE, padded // (PLANE * 128), 128)
    tokens_grad, sum_q, sum_o, flat, tiny, mixtures, _ = rear(
        zn, heads, middle_grad, tokens, first_gain[None], jnp.stack([query_gain, key_gain]), flat, comb,
        result.reshape(PLANE, slots, width), seq_norm, full_q, full_o, pre, rot, value_rows, lse,
        context_rows, tables, bias.T,
    )
    block_out = (resid_mid + jnp.sum(mixtures.astype(f32), axis=0)).astype(bf16)
    query_grad = jnp.concatenate([sum_q[0, :, :half], sum_q[1, :, :half]], axis=1)
    kv_grad = sum_q[0, :, half:] + sum_q[1, :, half:]
    key_grad, value_grad = kv_grad[:, :HD], kv_grad[:, HD:]
    output_grad = sum_o.reshape(2 * half, own_rows)
    flat = flat.reshape(-1)
    n_router = width * experts
    router_grad = flat[:n_router].reshape(width, experts)
    second_gain_grad = flat[n_router : n_router + width]
    tiny = tiny[0]
    first_gain_grad = tiny[:width]
    query_gain_grad = tiny[width : width + HD]
    key_gain_grad = tiny[width + HD :]
    return (
        block_out,
        tokens_grad,
        first_gain_grad,
        second_gain_grad,
        query_gain_grad,
        key_gain_grad,
        query_grad,
        key_grad,
        value_grad,
        output_grad,
        router_grad,
        gate_grad,
        up_grad,
        down_grad,
    )


def solution(mesh):
    both = ("exp", "tp")
    in_specs = (
        P(both, None),
        P(both, None),
        P(),
        P(),
        P(),
        P(),
        P("exp", "tp"),
        P("exp", "tp"),
        P("exp", "tp"),
        P("tp", "exp"),
        P(),
        P(both, None, None),
        P(both, None, None),
        P(both, None, None),
        P(both, None),
        P(both, None),
        P(),
    )
    out_specs = (
        P(both, None),
        P(both, None),
        P(),
        P(),
        P(),
        P(),
        P("exp", "tp"),
        P("exp", "tp"),
        P("exp", "tp"),
        P("tp", "exp"),
        P(),
        P(both, None, None),
        P(both, None, None),
        P(both, None, None),
    )
    return jax.shard_map(local, mesh=mesh, in_specs=in_specs, out_specs=out_specs, check_vma=False)
```

time: 828 us -> 678 us (0.82)
  matrix products: 137 us -> 71.6 us
  Pallas kernels: 571 us -> 539 us
  other arithmetic: 61.2 us -> 29.6 us
  local copies, waits for them, and re-layouts: 46.4 us -> 29.4 us
    dot_general x14 -> x2, matrix products: 92.4 us -> 16.4 us  [the longest x1 10.2 us: local(): unmixed = jnp.dot(arrived_g, down_weight[0].T, preferred_element_type=f32)]
    pallas_call x1, Pallas kernels: 156 us -> 88.4 us  [send_rows(): pl.pallas_call(functools.partial(send_kernel, zn, cap, chunk), out_shape=...]
    pallas_call x6 -> x3, Pallas kernels: 415 us -> 451 us  [the longest x1 208 us: rear(): pl.pallas_call(functools.partial(rear_kernel, zn, chunk, heads), out_shap...]
    reduce_sum x6 -> x1, other arithmetic: 15.1 us -> 2.25 us  [local(): block_out = (resid_mid + jnp.sum(mixtures.astype(f32), axis=0)).astype(bf16)]
    convert_element_type x4 -> x3, other arithmetic: 13.7 us -> 4.86 us  [the longest x1 3.95 us: local(): bias = jnp.where(mask, 0.0, NEGATIVE).astype(bf16)]
where the time goes in v2:
time: 678 us; the launch traced here: 671 us
  Pallas kernels  539 us (79%)
  matrix products  71.6 us (11%)
  other arithmetic  29.6 us (4%)
  local copies, waits for them, and re-layouts  29.4 us (4%)
    pallas_call x1, Pallas kernels, rear(): pl.pallas_call(functools.partial(rear_kernel, zn, chunk, heads), out_shap...  208 us
    pallas_call x1, Pallas kernels, front(): pl.pallas_call(functools.partial(front_kernel, zn, cap, chunk, heads), ou...  162 us
    pallas_call x1, Pallas kernels, send_rows(): pl.pallas_call(functools.partial(send_kernel, zn, cap, chunk), out_shape=...  88.4 us
    pallas_call x1, Pallas kernels, back_rows(): pl.pallas_call(functools.partial(back_kernel, zn, chunk), out_shape=(jax....  81.1 us

profile of v2, /device:TPU:8, one launch (start us, length us, event | category | flops | bytes accessed | tf_op | source)
XLA Modules:
  0.0 671.4 jit_solution(16463887383122863399)
XLA Ops:
  0.7 1.0 pad_maximum_fusion.3
  1.7 2.0 copy.46
  3.8 2.0 copy.47
  5.8 2.0 pad_maximum_fusion.2.pq_ref
  7.8 2.1 copy.48
  9.9 1.9 multiply_cosine_fusion
  11.8 0.3 maximum_bitcast_fusion
  12.2 1.0 pad_maximum_fusion.tab_ref.tab_hbm
  13.2 0.6 pad_maximum_fusion.4.hg_ref
  13.8 0.2 dynamic-slice_reduce_fusion
  14.0 0.1 fusion.34
  14.1 3.9 select_convert_fusion
  18.1 0.2 fusion.21
  18.3 0.6 select_bitcast_fusion.1.slot_ref
  18.9 162.2 %front.1 = (bf16[8,128,2048]{2,1,0:T(8,128)(2,1)}, bf16[8,256,768]{2,1,0:T(8,128)(2,1)}, bf16[8,256,512]{2,1,0:T(8,128)(2,1)}, f32[1024,768]{1,0:T(8,128)}, bf16...) custom-call(bf16[128,2048]{1,0:T(8,128)(2,1)} %tok_ref.3, ...), custom_call_target="tpu_custom_call" | custom-call | tf_op jit(solution)/shard_map/front/pallas_call | solution.py:729
  181.1 1.4 multiply_reduce_fusion.2
  182.6 1.0 copy-done.1
  183.6 0.2 multiply_convert_fusion.3.norm_ref
  183.7 0.3 fusion.33
  184.1 0.6 fusion.31.mix_ref
  184.7 88.4 %send_rows.1 = (bf16[8,144,2048]{2,1,0:T(8,128)(2,1)}, f32[8,1,144]{2,1,0:T(1,128)}, f32[4,8,128]{2,1,0:T(8,128)}) custom-call(bf16[128,2048]{1,0:T(8,128)(2,1)} %copy-done.4, f32[4,8,128]{2,1,0:T(8,128)} %get-tuple-element.38.slots_ref, f32[4,8,128]{2,1,0:T(8,128)} %fusion.31.mix_ref), custom_call_target="tpu_custom_call" | custom-call | tf_op jit(solution)/shard_map/send_rows/pallas_call | solution.py:824
  273.2 9.6 %fusion.10 = f32[1152,768]{0,1:T(8,128)} fusion(bf16[1152,2048]{1,0:T(8,128)(2,1)} %bitcast.150, bf16[1,2048,768]{2,1,0:T(8,128)(2,1)} %param.29), kind=kOutput, calls=%fused_computation.26 | convolution fusion | flops 3623878656 | bytes 11403264 | tf_op jit(solution)/shard_map/dot_general | solution.py:1641
  282.8 6.6 fusion.7
  289.4 0.1 mul.156
  289.5 10.2 %fusion.2 = (f32[1152]{0:T(1024)S(1)}, bf16[1152,768]{0,1:T(8,128)(2,1)}, bf16[1152,768]{0,1:T(8,128)(2,1)S(1)}, bf16[1152,768]{0,1:T(8,128)(2,1)S(1)}) fusion(f32[1152,768]{0,1:T(8,128)} %fusion.10, f32[1152,768]{0,1:T(8,128)} %fusion.7, f32[1152]{0:T(1024)S(1)} %mul.156, bf16[1152,2048]{1,0:T(8,128)(2,1)} %bitcast.146, bf16[1,768,2048]{2,1,0:T(8,128)(2,1)S(1)} %copy-done), kind=kOutput, calls=%fused_computation.14 | convolution fusion | flops 3640687616 | bytes 20259840 | tf_op jit(solution)/shard_map/dot_general | solution.py:1646
  299.8 3.9 fusion.5
  303.7 5.6 add_convert_fusion
  309.5 1.1 select_add_fusion.dot_ref
  310.6 0.3 broadcast_in_dim.143
  310.9 1.2 copy.69
  312.1 2.4 copy.54
  314.6 0.3 eq.84
  314.9 1.6 copy.70
  316.5 3.4 copy.50
  320.0 0.1 eq.87
  320.0 3.5 select_convert_fusion.2
  323.6 1.1 convert_element_type.110.hot_ref
  324.7 81.1 %back_rows.1 = (f32[128,2048]{1,0:T(8,128)}, f32[4,128,128]{2,1,0:T(8,128)}) custom-call(bf16[8,144,2048]{2,1,0:T(8,128)(2,1)} %bitcast.129, bf16[8,144,128]{2,1,0:T(8,128)(2,1)} %select_add_fusion.dot_ref, bf16[512,1152]{1,0:T(8,128)(2,1)} %convert_element_type.110.hot_ref), custom_call_target="tpu_custom_call" | custom-call | tf_op jit(solution)/shard_map/back_rows/pallas_call | solution.py:915
  405.9 1.8 fusion.19
  407.6 0.7 copy.51
  408.3 0.9 fusion.25
  409.3 2.1 multiply_reduce_fusion
  411.4 2.0 multiply_add_fusion.mid_ref
  413.4 1.3 fusion.37
  414.7 1.5 reshape.201
  416.2 0.7 select_maximum_fusion
  416.9 7.0 %convolution_convert_fusion = bf16[1152,2048]{1,0:T(8,128)(2,1)} fusion(bf16[1152,768]{0,1:T(8,128)(2,1)} %get-tuple-element.93, bf16[1,768,2048]{2,1,0:T(8,128)(2,1)S(1)} %copy-done), kind=kOutput, calls=%fused_computation.1 | convolution fusion | flops 3626237952 | bytes 9633792 | tf_op jit(solution)/shard_map/dot_general | solution.py:1645
  423.9 207.6 %rear.1 = (f32[128,2048]{1,0:T(8,128)}, f32[2,256,768]{2,1,0:T(8,128)}, f32[2,512,256]{2,1,0:T(8,128)}, f32[8,72,128]{2,1,0:T(8,128)}, f32[1,2304]{1,0:T(1,128)}...) custom-call(f32[128,2048]{1,0:T(8,128)} %multiply_add_fusion.mid_ref, bf16[128,2048]{1,0:T(8,128)(2,1)} %tok_ref.3, ...), custom_call_target="tpu_custom_call" | custom-call | tf_op jit(solution)/shard_map/rear/pallas_call | solution.py:1490
  631.6 2.2 convert_reduce_fusion
  633.8 0.9 add_convert_fusion.1
  634.8 0.6 slice.53
  635.4 0.6 slice.68
  636.0 0.5 slice_bitcast_fusion.2
  636.5 0.1 slice_bitcast_fusion.1
  636.6 1.1 pad_maximum_fusion.1
  637.7 0.7 fusion.36
  638.4 1.3 slice.66
  639.8 2.3 slice.71
  642.0 2.2 copy.55
  644.3 10.1 %convolution_bitcast_fusion.2 = f32[1,2048,768]{2,1,0:T(8,128)} fusion(bf16[1152,2048]{1,0:T(8,128)(2,1)} %bitcast.151, bf16[1152,768]{0,1:T(8,128)(2,1)} %copy-done.33), kind=kOutput, calls=%fused_computation.13 | convolution fusion | flops 3623878656 | bytes 12779520 | tf_op jit(solution)/shard_map/dot_general | solution.py:1653
  654.3 8.7 %convolution_bitcast_fusion.1 = f32[1,2048,768]{2,1,0:T(8,128)} fusion(bf16[1152,2048]{1,0:T(8,128)(2,1)} %bitcast.152, bf16[1152,768]{0,1:T(8,128)(2,1)S(1)} %copy-done.36), kind=kOutput, calls=%fused_computation.12 | convolution fusion | flops 3623878656 | bytes 12779520 | tf_op jit(solution)/shard_map/dot_general | solution.py:1654
  663.0 6.1 convolution_bitcast_fusion
  669.2 1.0 copy.73
  670.2 1.0 copy.74
  (97 shorter events, 0.5 us)
Async XLA Ops:
  0.6 288.8 %copy-start = (bf16[1,768,2048]{2,1,0:T(8,128)(2,1)S(1)}, bf16[1,768,2048]{2,1,0:T(8,128)(2,1)}, u32[]{:S(2)}) copy-start(bf16[1,768,2048]{2,1,0:T(8,128)(2,1)} %param.30) | copy-start | bytes 9437188
  7.8 5.4 copy-start.26
  7.8 5.4 copy-start.27
  7.8 6.0 copy-start.25
  12.2 5.9 copy-start.24
  12.2 5.9 copy-start.32
  18.0 163.1 %copy-start.6 = (bf16[128,2048]{1,0:T(8,128)(2,1)S(1)}, bf16[128,2048]{1,0:T(8,128)(2,1)}, u32[]{:S(2)}) copy-start(bf16[128,2048]{1,0:T(8,128)(2,1)} %tok_ref.3) | copy-start | bytes 1572868
  18.1 166.0 %copy-start.13 = (pred[128,32]{0,1:T(8,128)(4,1)}, pred[128,32]{0,1:T(8,128)(4,1)S(1)}, u32[]{:S(2)}) copy-start(pred[128,32]{0,1:T(8,128)(4,1)S(1)} %fusion.18) | copy-start | bytes 12292
  18.9 164.6 %copy-start.14 = (f32[2048]{0:T(1024)S(1)}, f32[2048]{0:T(1024)}, u32[]{:S(2)}) copy-start(f32[2048]{0:T(1024)} %param.20) | copy-start | bytes 24580
  18.9 164.8 %copy-start.11 = (bf16[2048,32]{0,1:T(8,128)(2,1)S(1)}, bf16[2048,32]{0,1:T(8,128)(2,1)}, u32[]{:S(2)}) copy-start(bf16[2048,32]{0,1:T(8,128)(2,1)} %param.27) | copy-start | bytes 393220
  182.6 1.0 copy-start.1
  183.6 99.2 %copy-start.22 = (f32[128]{0:T(128)}, f32[128]{0:T(128)S(1)}, u32[]{:S(2)}) copy-start(f32[128]{0:T(128)S(1)} %add_rsqrt_fusion) | copy-start | bytes 1540
  183.7 1.0 copy-start.4
  184.0 98.7 %copy-start.19 = (f32[128]{0:T(128)}, f32[128]{0:T(128)S(1)}, u32[]{:S(2)}) copy-start(f32[128]{0:T(128)S(1)} %get-tuple-element.113) | copy-start | bytes 1540
  184.1 98.7 %copy-start.23 = (f32[128]{0:T(128)}, f32[128]{0:T(128)S(1)}, u32[]{:S(2)}) copy-start(f32[128]{0:T(128)S(1)} %fusion.32) | copy-start | bytes 1540
  273.2 9.6 %copy-start.28 = (bf16[8,144,2048]{2,1,0:T(8,128)(2,1)S(1)}, bf16[8,144,2048]{2,1,0:T(8,128)(2,1)}, u32[]{:S(2)}) copy-start(bf16[8,144,2048]{2,1,0:T(8,128)(2,1)} %get-tuple-element.40) | copy-start | bytes 14155780
  273.2 9.6 %copy-start.29 = (bf16[1,2048,768]{2,1,0:T(8,128)(2,1)S(1)}, bf16[1,2048,768]{2,1,0:T(8,128)(2,1)}, u32[]{:S(2)}) copy-start(bf16[1,2048,768]{2,1,0:T(8,128)(2,1)} %param.28) | copy-start | bytes 9437188
  282.8 6.6 copy-start.16
  289.5 10.3 %copy-start.20 = (f32[1152]{0:T(1024)}, f32[1152]{0:T(1024)S(1)}, u32[]{:S(2)}) copy-start(f32[1152]{0:T(1024)S(1)} %mul.156) | copy-start | bytes 13828
  289.5 10.2 %copy-start.30 = (bf16[1,2048,768]{2,1,0:T(8,128)(2,1)S(1)}, bf16[1,2048,768]{2,1,0:T(8,128)(2,1)}, u32[]{:S(2)}) copy-start(bf16[1,2048,768]{2,1,0:T(8,128)(2,1)} %param.28) | copy-start | bytes 9437188
  299.7 4.0 copy-start.33
  299.7 4.0 copy-start.35
  299.7 4.0 copy-start.31
  303.7 6.9 %copy-start.17 = (f32[4,8,128]{2,1,0:T(8,128)S(1)}, f32[4,8,128]{2,1,0:T(8,128)}, u32[]{:S(2)}) copy-start(f32[4,8,128]{2,1,0:T(8,128)} %get-tuple-element.43) | copy-start | bytes 49156
  309.4 5.1 copy-start.15
  408.3 3.0 copy-start.2
  408.3 3.0 copy-start.7
  408.3 5.0 copy-start.5
  631.5 2.3 copy-start.3
  631.5 3.2 copy-start.18
  631.6 3.8 copy-start.12
  631.6 4.9 copy-start.8
  644.3 10.1 %copy-start.36 = (bf16[1152,768]{0,1:T(8,128)(2,1)S(1)}, bf16[1152,768]{0,1:T(8,128)(2,1)}, u32[]{:S(2)}) copy-start(bf16[1152,768]{0,1:T(8,128)(2,1)} %copy-done.35) | copy-start | bytes 5308420
  644.3 18.7 %slice-start = ((s8[4718592]{0:T(1024)(128)(4,1)}), s8[4194304]{0:T(1024)(128)(4,1)S(1)}, s32[]{:S(2)}) async-start(s8[4718592]{0:T(1024)(128)(4,1)} %bitcast.147), calls=%async_computation | async-start | bytes 8388608
  654.3 8.7 %copy-start.21 = (f32[1152]{0:T(1024)S(1)}, f32[1152]{0:T(1024)}, u32[]{:S(2)}) copy-start(f32[1152]{0:T(1024)} %copy-done.20) | copy-start | bytes 13828
  654.3 8.7 %slice-start.1 = ((s8[4718592]{0:T(1024)(128)(4,1)}), s8[524288]{0:T(1024)(128)(4,1)S(1)}, s32[]{:S(2)}) async-start(s8[4718592]{0:T(1024)(128)(4,1)} %bitcast.147), calls=%async_computation.1 | async-start | bytes 1048576
  654.3 8.7 %copy-start.34 = (bf16[1152,768]{0,1:T(8,128)(2,1)S(1)}, bf16[1152,768]{0,1:T(8,128)(2,1)}, u32[]{:S(2)}) copy-start(bf16[1152,768]{0,1:T(8,128)(2,1)} %get-tuple-element.93) | copy-start | bytes 5308420
  663.0 6.2 copy-start.10
  663.0 7.1 %copy-start.9 = (f32[2,512,256]{2,1,0:T(8,128)S(1)}, f32[2,512,256]{2,1,0:T(8,128)}, u32[]{:S(2)}) copy-start(f32[2,512,256]{2,1,0:T(8,128)} %get-tuple-element.57) | copy-start | bytes 3145732

commit v3 on v2

--- a/solution.py
+++ b/solution.py
@@ -771,26 +771,73 @@
     )(tokens, gain, pack_q, pack_o, tables, gains, bias, grad, slot)
 
 
-def send_kernel(
-    zn, cap, chunk, norm_ref, slots_ref, mix_ref, an_ref, mr_ref, mo_ref,
-    nb, sn, hot, mrow, zsr, zsl, zr, ts, tr, xs, xr, ys, yr,
+class Flow:
+    def __init__(self, stage, sems):
+        self.stage, self.sems = stage, sems
+        self.count = 0
+        self.flight = [None, None]
+
+    def slot(self):
+        i = self.count % 2
+        if self.flight[i] is not None:
+            self.flight[i].wait()
+            self.flight[i] = None
+        return i
+
+    def send(self, dst):
+        i = self.count % 2
+        copy = pltpu.make_async_copy(self.stage.at[i], dst, self.sems.at[i])
+        copy.start()
+        self.flight[i] = copy
+        self.count += 1
+
+    def finish(self):
+        for i in range(2):
+            if self.flight[i] is not None:
+                self.flight[i].wait()
+                self.flight[i] = None
+
+
+def there_kernel(
+    zn, cap, chunk, norm_ref, slots_ref, mix_ref, ag_hbm, gate_hbm, up_hbm, down_hbm,
+    an_ref, mid_ref, dot_ref, hot_t_hbm, comb_hbm,
+    nb, sn, hot, mo, mrow, mr, wg, wu, wd, ag, gate, up, unmixed, stage, loads, flows,
+    zsr, zsl, zr, ts, tr, xs, xr, ys, yr,
 ):
     place, sends = Place(), Sends()
     pc = place
     greet(place, zn)
     tok, width = norm_ref.shape
     slots = zn * cap
+    rows = PLANE * slots
     chunks = width // chunk
+    hidden = wd.shape[0]
+    fetch = [
+        pltpu.make_async_copy(src, dst, loads.at[i])
+        for i, (src, dst) in enumerate(((down_hbm, wd), (gate_hbm, wg), (up_hbm, wu)))
+    ]
+    parts = [
+        pltpu.make_async_copy(
+            ag_hbm.at[:, :, pl.ds(c * chunk, chunk)], ag.at[c % 2], loads.at[3 + c % 2]
+        )
+        for c in range(chunks)
+    ]
     n = RowChain(place, sends, zn, norm_ref, nb, chunk, zsr, zsl, zr)
-    send_slots(place, sends, zn, mix_ref, mo_ref, ts, tr)
     for c in range(chunks):
         n.own(c)
+    send_slots(place, sends, zn, mix_ref, mo, ts, tr)
+    fetch[0].start()
+    parts[0].start()
+    if chunks > 1:
+        parts[1].start()
+    fetch[1].start()
+    fetch[2].start()
     n.keep()
     make_hot(zn, cap, tok, slots_ref, hot)
-    take_slots(place, zn, mix_ref, mo_ref, tr)
+    take_slots(place, zn, mix_ref, mo, tr)
 
     def mixes(p, carry):
-        row = jnp.concatenate([mo_ref[z, pl.ds(p, 1), :] for z in range(zn)], axis=1)
+        row = jnp.concatenate([mo[z, pl.ds(p, 1), :] for z in range(zn)], axis=1)
         high = row.astype(bf16)
         rest = row - high.astype(f32)
         middle = rest.astype(bf16)
@@ -803,38 +850,140 @@
     lax.fori_loop(0, PLANE, mixes, 0)
     for k in range(1, PLANE):
         p = pc.by(k)
-        sends.start(mrow.at[p], mr_ref.at[pc.p], ys.at[k], yr.at[k], pc.at(pc.z, p))
-    mr_ref[pc.p] = mrow[pc.p]
+        sends.start(mrow.at[p], mr.at[pc.p], ys.at[k], yr.at[k], pc.at(pc.z, p))
+    mr[pc.p] = mrow[pc.p]
+    fetch[0].wait()
     give = PlaneSend(place, sends, hot, nb, sn, an_ref, chunk, xs, xr)
+    half = PLANE // 2
+
+    def back_through(c):
+        cols = pl.ds(c * chunk, chunk)
+        parts[c].wait()
+
+        def body(i, carry):
+            at = pl.ds(i * half, half)
+            got = nt_dot(ag[c % 2, at].reshape(half * slots, chunk), wd[:, cols])
+            got = got.reshape(half, slots, hidden)
+            unmixed[at] = got if c == 0 else unmixed[at] + got
+            return carry
+
+        lax.fori_loop(0, 2, body, 0)
+        if c + 2 < chunks:
+            parts[c + 2].start()
+
     for c in range(chunks):
         for k in range(1, zn):
             n.step(c, k)
         give.send(c)
+        back_through(c)
+
+    lane = lax.broadcasted_iota(jnp.int32, (tok, rows), 1).astype(f32)
+
+    def tables(z, carry):
+        zero = jnp.zeros((120, tok), f32)
+        have = jnp.concatenate([slots_ref[z], zero], axis=0).T
+        mixed = jnp.concatenate([mo[z], zero], axis=0).T
+        one = jnp.zeros((tok, rows), f32)
+        mix = jnp.zeros((tok, rows), f32)
+        base = (z * cap).astype(f32)
+        for p in range(PLANE):
+            col = have[:, p : p + 1]
+            hit = lane == jnp.where(col < 0, -1.0, col + base + float(p * slots))
+            one = jnp.where(hit, 1.0, one)
+            mix = jnp.where(hit, mixed[:, p : p + 1], mix)
+        stage[0] = one.astype(bf16)
+        stage[1] = mix.astype(bf16)
+        at = pl.ds(pl.multiple_of(z * tok, tok), tok)
+        out = [
+            pltpu.make_async_copy(stage.at[i], dst.at[at, :], flows.at[i])
+            for i, dst in enumerate((hot_t_hbm, comb_hbm))
+        ]
+        for copy in out:
+            copy.start()
+        for copy in out:
+            copy.wait()
+        return carry
+
+    lax.fori_loop(0, zn, tables, 0)
+    fetch[1].wait()
+    fetch[2].wait()
+    for c in range(chunks):
+        cols = pl.ds(c * chunk, chunk)
+        give.take(c)
+
+        def into(i, carry):
+            at = pl.ds(i * half, half)
+            lhs = an_ref[at, :, cols].reshape(half * slots, chunk)
+            for weight, acc in ((wg, gate), (wu, up)):
+                got = nn_dot(lhs, weight[cols, :]).reshape(half, slots, hidden)
+                acc[at] = got if c == 0 else acc[at] + got
+            return carry
+
+        lax.fori_loop(0, 2, into, 0)
     for k in range(1, PLANE):
-        arrived(mr_ref.at[pc.by(k)], yr.at[k])
-    for c in range(chunks):
-        give.take(c)
+        arrived(mr.at[pc.by(k)], yr.at[k])
+    place_lane = lax.broadcasted_iota(jnp.int32, (slots, 128), 1)
+    r = lax.broadcasted_iota(jnp.int32, (slots, slots), 0)
+    s = lax.broadcasted_iota(jnp.int32, (slots, slots), 1)
+
+    def acts(p, carry):
+        mix = jnp.sum(jnp.where(r == s, mr[p], 0.0), axis=1, keepdims=True)
+        g, u, d = gate[p], up[p], unmixed[p]
+        sig = jax.nn.sigmoid(g)
+        act = g * sig
+        inner = (act * u).astype(bf16)
+        mid_ref[0, p] = inner
+        wide = inner.astype(f32)
+        mid_ref[1, p] = (wide * mix).astype(bf16)
+        dots = mix * jnp.sum(d * wide, axis=1, keepdims=True)
+        high = dots.astype(bf16).astype(f32)
+        dot = jnp.where(place_lane == pc.p, high, 0.0)
+        dot = jnp.where(place_lane == pc.p + PLANE, dots - high, dot)
+        dot_ref[p] = dot.astype(bf16)
+        d = d * mix
+        mid_ref[2, p] = (d * u * sig * (1.0 + g * (1.0 - sig))).astype(bf16)
+        mid_ref[3, p] = (d * act).astype(bf16)
+        return carry
+
+    lax.fori_loop(0, PLANE, acts, 0)
     sends.finish()
 
 
-def send_rows(zn, cap, norm, slots_all, mix, chunk=512):
+def there(zn, cap, norm, slots_all, mix, ag, gate, up, down, chunk=512):
     tok, width = norm.shape
     slots = zn * cap
+    hidden = down.shape[0]
     chunks = width // chunk
+    shape = jax.ShapeDtypeStruct
+    vmem = pltpu.VMEM
     return pl.pallas_call(
-        functools.partial(send_kernel, zn, cap, chunk),
+        functools.partial(there_kernel, zn, cap, chunk),
         out_shape=(
-            jax.ShapeDtypeStruct((PLANE, slots, width), bf16),
-            jax.ShapeDtypeStruct((PLANE, 1, slots), f32),
-            jax.ShapeDtypeStruct(mix.shape, f32),
+            shape((PLANE, slots, width), bf16),
+            shape((4, PLANE, slots, hidden), bf16),
+            shape((PLANE, slots, 128), bf16),
+            shape((zn * tok, PLANE * slots), bf16),
+            shape((zn * tok, PLANE * slots), bf16),
         ),
-        in_specs=[VSPEC] * 3,
-        out_specs=(VSPEC,) * 3,
+        in_specs=[VSPEC] * 3 + [ASPEC] * 4,
+        out_specs=(VSPEC,) * 3 + (ASPEC,) * 2,
         scratch_shapes=[
-            pltpu.VMEM((zn, tok, width), bf16),
-            pltpu.VMEM((PLANE, slots, width), bf16),
-            pltpu.VMEM((PLANE, slots, zn * tok), bf16),
-            pltpu.VMEM((PLANE, 1, slots), f32),
+            vmem((zn, tok, width), bf16),
+            vmem((PLANE, slots, width), bf16),
+            vmem((PLANE, slots, zn * tok), bf16),
+            vmem(mix.shape, f32),
+            vmem((PLANE, 1, slots), f32),
+            vmem((PLANE, 1, slots), f32),
+            vmem(gate.shape, bf16),
+            vmem(up.shape, bf16),
+            vmem(down.shape, bf16),
+            vmem((2, PLANE, slots, chunk), bf16),
+            vmem((PLANE, slots, hidden), f32),
+            vmem((PLANE, slots, hidden), f32),
+            vmem((PLANE, slots, hidden), f32),
+            vmem((2, tok, PLANE * slots), bf16),
+            dma_sems(5),
+            dma_sems(2),
             dma_sems(chunks, zn),
             dma_sems(chunks, zn),
             dma_sems(chunks, zn),
@@ -846,44 +995,108 @@
             dma_sems(PLANE),
         ],
         compiler_params=params(3),
-        name="send_rows",
-    )(norm, slots_all, mix)
+        name="there",
+    )(norm, slots_all, mix, ag, gate, up, down)
 
 
 def back_kernel(
-    zn, chunk, pair_ref, dot_ref, hot_ref, sum_ref, dots_ref,
-    rp, rd, zd, zp, ap, xs, xr, ds, dr, zs, zr, es, er,
+    zn, chunk, dot_ref, hot_ref, mid_hbm, an_hbm, ag_hbm, gate_hbm, up_hbm, down_hbm,
+    dots_ref, ap_hbm, res_hbm, gg_hbm, ug_hbm, dg_hbm,
+    mids, an, ag, wg, wu, wd, pb, rp, rd, zd, zp, wide, tall, flat,
+    loads, flows, xs, xr, ds, dr, zs, zr, es, er, os,
 ):
     place, sends = Place(), Sends()
     pc = place
+    fetch = [
+        pltpu.make_async_copy(src, dst, loads.at[i])
+        for i, (src, dst) in enumerate(
+            (
+                (gate_hbm, wg), (up_hbm, wu), (mid_hbm.at[2], mids.at[2]), (mid_hbm.at[3], mids.at[3]),
+                (mid_hbm.at[0], mids.at[0]), (down_hbm, wd), (mid_hbm.at[1], mids.at[1]), (ag_hbm, ag),
+                (an_hbm, an),
+            )
+        )
+    ]
+    for copy in fetch:
+        copy.start()
     greet(place, zn)
-    _, slots, width = pair_ref.shape
+    _, slots, width = pb.shape
+    hidden = wd.shape[0]
     chunks = width // chunk
-    tok = sum_ref.shape[0]
+    tok = dots_ref.shape[1]
     far = [(pc.z + k) % zn for k in range(1, zn)]
+    half = PLANE // 2
     for k in range(1, PLANE):
         p = pc.by(k)
         sends.start(dot_ref.at[p], rd.at[pc.p], ds.at[k], dr.at[k], pc.at(pc.z, p))
+    for copy in fetch[:4]:
+        copy.wait()
     for c in range(chunks):
         cols = pl.ds(c * chunk, chunk)
+
+        def pair(i, carry):
+            at = pl.ds(i * half, half)
+            got = nt_dot(mids[2, at].reshape(half * slots, hidden), wg[cols, :])
+            got = got + nt_dot(mids[3, at].reshape(half * slots, hidden), wu[cols, :])
+            pb[at, :, cols] = got.astype(bf16).reshape(half, slots, chunk)
+            return carry
+
+        lax.fori_loop(0, 2, pair, 0)
         for k in range(1, PLANE):
             p = pc.by(k)
             sends.start(
-                pair_ref.at[p, :, cols],
-                rp.at[pc.p, :, cols],
-                xs.at[c, k],
-                xr.at[c, k],
-                pc.at(pc.z, p),
+                pb.at[p, :, cols], rp.at[pc.p, :, cols], xs.at[c, k], xr.at[c, k], pc.at(pc.z, p)
             )
+        rp[pc.p, :, cols] = pb[pc.p, :, cols]
     rd[pc.p] = dot_ref[pc.p]
-    rp[pc.p] = pair_ref[pc.p]
     for k in range(1, PLANE):
         arrived(rd.at[pc.by(k)], dr.at[k])
     zd[...] = nn_dot(hot_ref[...], rd[...].reshape(PLANE * slots, 128)).reshape(zn, tok, 128)
     for k, d in enumerate(far):
         sends.start(zd.at[d], dots_ref.at[pc.z], es.at[k], er.at[pc.z], pc.at(d, pc.p))
     dots_ref[pc.z] = zd[pc.z]
-    for c in range(chunks):
+
+    flow_r, flow_g, flow_u, flow_d = (
+        Flow(buf, flows.at[i]) for i, buf in enumerate((wide, tall.at[0], tall.at[1], flat))
+    )
+    keeps = []
+
+    def result(c):
+        cols = pl.ds(c * chunk, chunk)
+        slot = flow_r.slot()
+
+        def body(i, carry):
+            at = pl.ds(i * half, half)
+            got = nn_dot(mids[0, at].reshape(half * slots, hidden), wd[:, cols])
+            wide[slot, at] = got.astype(bf16).reshape(half, slots, chunk)
+            return carry
+
+        lax.fori_loop(0, 2, body, 0)
+        flow_r.send(res_hbm.at[:, :, cols])
+
+    def down_grad(i):
+        m = pl.ds(i * 128, 128)
+        slot = flow_d.slot()
+        lhs = mids[1, :, :, m].reshape(PLANE * slots, 128)
+
+        def body(j, carry):
+            cols = pl.ds(pl.multiple_of(j * chunk, chunk), chunk)
+            flat[slot, :, cols] = tn_dot(lhs, ag[:, :, cols].reshape(PLANE * slots, chunk))
+            return carry
+
+        lax.fori_loop(0, chunks, body, 0)
+        flow_d.send(dg_hbm.at[m, :])
+
+    def gate_up_grad(i):
+        m = pl.ds(i * 256, 256)
+        lhs = an[:, :, m].reshape(PLANE * slots, 256)
+        for which, flow, dst in ((0, flow_g, gg_hbm), (1, flow_u, ug_hbm)):
+            slot = flow.slot()
+            rhs = mids[2 + which].reshape(PLANE * slots, hidden)
+            tall[which, slot] = tn_dot(lhs, rhs)
+            flow.send(dst.at[m, :])
+
+    def combine(c):
         cols = pl.ds(c * chunk, chunk)
         for k in range(1, PLANE):
             arrived(rp.at[pc.by(k), :, cols], xr.at[c, k])
@@ -892,40 +1105,75 @@
         for k, d in enumerate(far):
             sends.start(
                 zp.at[d, :, cols],
-                ap.at[pc.z, :, cols],
+                ap_hbm.at[pc.z, :, cols],
                 zs.at[c, k],
                 zr.at[c, pc.z],
                 pc.at(d, pc.p),
             )
+        keep = pltpu.make_async_copy(zp.at[pc.z, :, cols], ap_hbm.at[pc.z, :, cols], os.at[c])
+        keep.start()
+        keeps.append(keep)
+
+    for copy in fetch[4:6]:
+        copy.wait()
     for c in range(chunks):
-        cols = pl.ds(c * chunk, chunk)
-        total = zp[pc.z, :, cols].astype(f32)
+        result(c)
+    for copy in fetch[6:]:
+        copy.wait()
+    work = [functools.partial(down_grad, i) for i in range(hidden // 128)]
+    work += [functools.partial(gate_up_grad, i) for i in range(width // 256)]
+    share = -(-len(work) // chunks)
+    for c in range(chunks):
+        for item in work[c * share : (c + 1) * share]:
+            item()
+        combine(c)
+    for c in range(chunks):
         for d in far:
-            arrived(ap.at[d, :, cols], zr.at[c, d])
-            total = total + ap[d, :, cols].astype(f32)
-        sum_ref[:, cols] = total
+            arrived(ap_hbm.at[d, :, pl.ds(c * chunk, chunk)], zr.at[c, d])
+    for keep in keeps:
+        keep.wait()
     for d in far:
         arrived(dots_ref.at[d], er.at[d])
+    for flow in (flow_r, flow_g, flow_u, flow_d):
+        flow.finish()
     sends.finish()
 
 
-def back_rows(zn, tok, pair, dots, hot, chunk=512):
-    _, slots, width = pair.shape
+def back_rows(zn, tok, dots, hot, mids, an, ag, gate, up, down, chunk=512):
+    _, slots, width = an.shape
+    hidden = down.shape[0]
     chunks = width // chunk
+    shape = jax.ShapeDtypeStruct
+    vmem = pltpu.VMEM
     return pl.pallas_call(
         functools.partial(back_kernel, zn, chunk),
         out_shape=(
-            jax.ShapeDtypeStruct((tok, width), f32),
-            jax.ShapeDtypeStruct((zn, tok, 128), f32),
+            shape((zn, tok, 128), f32),
+            shape((zn, tok, width), bf16),
+            shape((PLANE, slots, width), bf16),
+            shape(gate.shape, f32),
+            shape(up.shape, f32),
+            shape(down.shape, f32),
         ),
-        in_specs=[VSPEC] * 3,
-        out_specs=(VSPEC,) * 2,
+        in_specs=[VSPEC] * 2 + [ASPEC] * 6,
+        out_specs=(VSPEC,) + (ASPEC,) * 5,
         scratch_shapes=[
-            pltpu.VMEM((PLANE, slots, width), bf16),
-            pltpu.VMEM((PLANE, slots, 128), bf16),
-            pltpu.VMEM((zn, tok, 128), f32),
-            pltpu.VMEM((zn, tok, width), bf16),
-            pltpu.VMEM((zn, tok, width), bf16),
+            vmem((4, PLANE, slots, hidden), bf16),
+            vmem((PLANE, slots, width), bf16),
+            vmem((PLANE, slots, width), bf16),
+            vmem(gate.shape, bf16),
+            vmem(up.shape, bf16),
+            vmem(down.shape, bf16),
+            vmem((PLANE, slots, width), bf16),
+            vmem((PLANE, slots, width), bf16),
+            vmem((PLANE, slots, 128), bf16),
+            vmem((zn, tok, 128), f32),
+            vmem((zn, tok, width), bf16),
+            vmem((2, PLANE, slots, chunk), bf16),
+            vmem((2, 2, 256, hidden), f32),
+            vmem((2, 128, width), f32),
+            dma_sems(9),
+            dma_sems(4, 2),
             dma_sems(chunks, PLANE),
             dma_sems(chunks, PLANE),
             dma_sems(PLANE),
@@ -934,10 +1182,11 @@
             dma_sems(chunks, zn),
             dma_sems(zn),
             dma_sems(zn),
+            dma_sems(chunks),
         ],
         compiler_params=params(4),
         name="back_rows",
-    )(pair, dots, hot)
+    )(dots, hot, mids, an, ag, gate, up, down)
 
 
 class ColumnReduce:
@@ -1632,48 +1881,14 @@
     mix = jnp.where(member, mix, 0.0)
     keep_mix = jnp.where(keep, mix, 0.0)
     mix_t = keep_mix.T.reshape(zn, PLANE, tok)
-    rows_n, mix_rows, mix_all = send_rows(zn, cap, second_norm, slots_all, mix_t)
-    mix_rows = mix_rows.reshape(PLANE * slots, 1)
-    arrived_n = rows_n.reshape(PLANE * slots, width)
-    arrived_g = rows_g.reshape(PLANE * slots, width)
-
-    gate_val = jnp.dot(arrived_n, gate_weight[0], preferred_element_type=f32)
-    up_val = jnp.dot(arrived_n, up_weight[0], preferred_element_type=f32)
-    gate_sig = jax.nn.sigmoid(gate_val)
-    gate_act = gate_val * gate_sig
-    inner = (gate_act * up_val).astype(bf16)
-    result = jnp.dot(inner, down_weight[0], preferred_element_type=f32).astype(bf16)
-    unmixed = jnp.dot(arrived_g, down_weight[0].T, preferred_element_type=f32)
-    dots = mix_rows * jnp.sum(unmixed * inner.astype(f32), axis=1, keepdims=True)
-    inner_grad = unmixed * mix_rows
-    mixed_inner = (inner.astype(f32) * mix_rows).astype(bf16)
-    down_grad = jnp.dot(mixed_inner.T, arrived_g, preferred_element_type=f32)[None]
-    gate_back = (inner_grad * up_val * gate_sig * (1.0 + gate_val * (1.0 - gate_sig))).astype(bf16)
-    up_back = (inner_grad * gate_act).astype(bf16)
-    gate_grad = jnp.dot(arrived_n.T, gate_back, preferred_element_type=f32)[None]
-    up_grad = jnp.dot(arrived_n.T, up_back, preferred_element_type=f32)[None]
-    pair_back = jnp.dot(gate_back, gate_weight[0].T, preferred_element_type=f32) + jnp.dot(
-        up_back, up_weight[0].T, preferred_element_type=f32
+    gate_w, up_w, down_w = gate_weight[0], up_weight[0], down_weight[0]
+    rows_n, mids, dot_lanes, hot, comb = there(
+        zn, cap, second_norm, slots_all, mix_t, rows_g, gate_w, up_w, down_w
     )
-    pair_back = pair_back.astype(bf16)
-    dots_high = dots.astype(bf16)
-    dots_low = (dots - dots_high.astype(f32)).astype(bf16)
-    place = (exp_index % 2) * 4 + lax.axis_index("tp")
-    lane = jnp.arange(128, dtype=jnp.int32)[None, :]
-    zero = jnp.zeros((), bf16)
-    dot_lanes = jnp.where(lane == place, dots_high, zero) + jnp.where(
-        lane == place + PLANE, dots_low, zero
+    dots_all, pairs, result, gate_grad, up_grad, down_grad = back_rows(
+        zn, tok, dot_lanes, hot, mids, rows_n, rows_g, gate_w, up_w, down_w
     )
-
-    slot_col = slots_all.transpose(0, 2, 1).reshape(zn, tok, PLANE, 1)
-    mix_col = mix_all.transpose(0, 2, 1).reshape(zn, tok, PLANE, 1)
-    want = jnp.where(slot_col < 0, -1.0, slot_col + (jnp.arange(zn, dtype=f32) * cap)[:, None, None, None])
-    hot = want == jnp.arange(slots, dtype=f32)[None, None, None, :]
-    comb = jnp.where(hot, mix_col, 0.0).astype(bf16).reshape(zn * tok, PLANE * slots)
-    hot = hot.astype(bf16).reshape(zn * tok, PLANE * slots)
-    pairs_sum, dots_all = back_rows(
-        zn, tok, pair_back.reshape(PLANE, slots, width), dot_lanes.reshape(PLANE, slots, 128), hot
-    )
+    pairs_sum = jnp.sum(pairs.astype(f32), axis=0)
     grad_out = out_grad.astype(f32)
     mix_dots = dots_all[:, :, :PLANE] + dots_all[:, :, PLANE : 2 * PLANE]
     mix_dots = mix_dots.transpose(1, 0, 2).reshape(tok, experts)
@@ -1691,7 +1906,7 @@
     flat = jnp.pad(flat, (0, padded - count)).reshape(PLANE, padded // (PLANE * 128), 128)
     tokens_grad, sum_q, sum_o, flat, tiny, mixtures, _ = rear(
         zn, heads, middle_grad, tokens, first_gain[None], jnp.stack([query_gain, key_gain]), flat, comb,
-        result.reshape(PLANE, slots, width), seq_norm, full_q, full_o, pre, rot, value_rows, lse,
+        result, seq_norm, full_q, full_o, pre, rot, value_rows, lse,
         context_rows, tables, bias.T,
     )
     block_out = (resid_mid + jnp.sum(mixtures.astype(f32), axis=0)).astype(bf16)
@@ -1719,9 +1934,9 @@
         value_grad,
         output_grad,
         router_grad,
-        gate_grad,
-        up_grad,
-        down_grad,
+        gate_grad[None],
+        up_grad[None],
+        down_grad[None],
     )
 
 

time: 678 us -> 613 us (0.904)
  matrix products: 71.6 us -> 2.78 us
  Pallas kernels: 539 us -> 553 us
    dot_general x9 -> x0, matrix products: 67.7 us -> none  [the longest x1 10.2 us: local(): unmixed = jnp.dot(arrived_g, down_weight[0].T, preferred_element_type=f32)]
    pallas_call x2, Pallas kernels: 170 us -> 183 us  [the longest x1 105 us: there(): pl.pallas_call(functools.partial(there_kernel, zn, cap, chunk), out_shape...]
    unnamed x84 -> x47, local copies, waits for them, and re-layouts: 10.2 us -> 18.1 us
where the time goes in v3:
time: 613 us; the launch traced here: 607 us
  Pallas kernels  553 us (90%)
  other arithmetic  26.7 us (4%)
  local copies, waits for them, and re-layouts  23.2 us (4%)
    pallas_call x1, Pallas kernels, rear(): pl.pallas_call(functools.partial(rear_kernel, zn, chunk, heads), out_shap...  208 us
    pallas_call x1, Pallas kernels, front(): pl.pallas_call(functools.partial(front_kernel, zn, cap, chunk, heads), ou...  162 us
    pallas_call x1, Pallas kernels, there(): pl.pallas_call(functools.partial(there_kernel, zn, cap, chunk), out_shape...  105 us
    pallas_call x1, Pallas kernels, back_rows(): pl.pallas_call(functools.partial(back_kernel, zn, chunk), out_shape=(shap...  78.4 us
    unnamed x47, local copies, waits for them, and re-layouts  18.1 us

profile of v3, /device:TPU:8, one launch (start us, length us, event | category | flops | bytes accessed | tf_op | source)
XLA Modules:
  0.0 606.7 jit_solution(10072191526681766190)
XLA Ops:
  0.6 0.0 copy-start
  0.7 0.0 copy-start.8
  0.7 1.0 dynamic-slice_reduce_fusion
  1.7 1.2 pad_maximum_fusion.4.hg_ref
  2.9 0.1 fusion.19
  3.0 0.7 fusion.3
  3.7 0.0 copy-start.10
  3.8 0.9 fusion.6
  4.7 0.6 select_bitcast_fusion.slot_ref
  5.3 0.9 pad_maximum_fusion.3
  6.3 1.2 copy.40
  7.5 0.2 copy.41
  7.7 0.9 pad_maximum_fusion.2.pq_ref
  8.7 0.0 copy-done.8
  8.7 1.0 copy.42
  9.7 1.9 multiply_cosine_fusion
  11.6 0.3 maximum_bitcast_fusion
  11.9 1.0 pad_maximum_fusion.tab_ref.tab_hbm
  12.9 3.9 select_convert_fusion
  16.9 162.1 %front.1 = (bf16[8,128,2048]{2,1,0:T(8,128)(2,1)}, bf16[8,256,768]{2,1,0:T(8,128)(2,1)}, bf16[8,256,512]{2,1,0:T(8,128)(2,1)}, f32[1024,768]{1,0:T(8,128)}, bf16...) custom-call(bf16[128,2048]{1,0:T(8,128)(2,1)} %tok_ref.3, ...), custom_call_target="tpu_custom_call" | custom-call | tf_op jit(solution)/shard_map/front/pallas_call | solution.py:729
  179.0 1.4 multiply_reduce_fusion.2
  180.4 0.5 copy-done.14
  181.0 0.2 multiply_convert_fusion.norm_ref
  181.1 0.0 copy-start.2
  181.1 0.3 fusion.18
  181.4 0.0 copy-start.13
  181.5 0.0 copy-start.15
  181.5 0.6 fusion.16.mix_ref
  182.1 104.7 %there.1 = (bf16[8,144,2048]{2,1,0:T(8,128)(2,1)}, bf16[4,8,144,768]{3,2,1,0:T(8,128)(2,1)}, bf16[8,144,128]{2,1,0:T(8,128)(2,1)}, bf16[512,1152]{1,0:T(8,128)(2,1)}, bf16[512,1152]{1,0:T(8,128)(2,1)}) custom-call(bf16[128,2048]{1,0:T(8,128)(2,1)} %copy-done.2, f32[4,8,128]{2,1,0:T(8,128)} %get-tuple-element.43.slots_ref, f32[4,8,128]{2,1,0:T(8,128)} %fusion.16.mix_ref, ...), custom_call_target="tpu_custom_call" | custom-call | tf_op jit(solution)/shard_map/there/pallas_call | solution.py:959
  286.8 0.0 copy-done.13
  286.8 0.0 copy-done.15
  286.8 78.4 %back_rows.1 = (f32[4,128,128]{2,1,0:T(8,128)}, bf16[4,128,2048]{2,1,0:T(8,128)(2,1)}, bf16[8,144,2048]{2,1,0:T(8,128)(2,1)}, f32[2048,768]{1,0:T(8,128)}, f32[2048,768]{1,0:T(8,128)}, /*index=5*/f32[768,2048]{1,0:T(8,128)}) custom-call(bf16[8,144,128]{2,1,0:T(8,128)(2,1)} %get-tuple-element.45.dot_ref, bf16[512,1152]{1,0:T(8,128)(2,1)} %get-tuple-element.46.hot_ref, ...), custom_call_target="tpu_custom_call" | custom-call | tf_op jit(solution)/shard_map/back_rows/pallas_call | solution.py:1148
  365.2 0.0 copy-start.5
  365.2 2.1 convert_reduce_fusion.1
  367.3 0.0 copy-start.3
  367.3 1.8 fusion.4
  369.2 0.7 copy.43
  369.9 0.8 fusion.10
  370.6 1.2 multiply_reduce_fusion
  371.9 2.0 multiply_add_fusion.mid_ref
  373.9 0.0 copy-done.3
  373.9 0.3 fusion.21
  374.2 0.3 reshape.106
  374.5 0.7 select_maximum_fusion
  375.3 207.6 %rear.1 = (f32[128,2048]{1,0:T(8,128)}, f32[2,256,768]{2,1,0:T(8,128)}, f32[2,512,256]{2,1,0:T(8,128)}, f32[8,72,128]{2,1,0:T(8,128)}, f32[1,2304]{1,0:T(1,128)}...) custom-call(f32[128,2048]{1,0:T(8,128)} %multiply_add_fusion.mid_ref, bf16[128,2048]{1,0:T(8,128)(2,1)} %tok_ref.3, ...), custom_call_target="tpu_custom_call" | custom-call | tf_op jit(solution)/shard_map/rear/pallas_call | solution.py:1739
  582.9 2.2 convert_reduce_fusion
  585.1 0.9 add_convert_fusion
  586.1 0.5 slice_bitcast_fusion.2
  586.6 0.6 slice.53
  587.2 0.6 slice.68
  587.9 0.1 slice_bitcast_fusion.1
  588.0 1.1 pad_maximum_fusion.1
  589.1 0.7 fusion.20
  589.8 0.3 slice.66
  590.1 0.1 slice.71
  590.2 1.0 copy.45
  591.2 2.4 copy.52
  593.6 1.0 copy.53
  594.6 6.1 copy.54
  600.7 0.0 slice-done.3
  600.7 0.0 copy-start.1
  600.7 2.9 copy.55
  603.5 0.2 slice-done.1
  603.7 2.7 copy.56
  (35 shorter events, 0.2 us)
Async XLA Ops:
  0.6 180.5 %copy-start = (bf16[2048,32]{0,1:T(8,128)(2,1)S(1)}, bf16[2048,32]{0,1:T(8,128)(2,1)}, u32[]{:S(2)}) copy-start(bf16[2048,32]{0,1:T(8,128)(2,1)} %param.27) | copy-start | bytes 393220
  0.7 8.0 %copy-start.8 = (bf16[1024,256]{1,0:T(8,128)(2,1)S(1)}, bf16[1024,256]{1,0:T(8,128)(2,1)}, u32[]{:S(2)}) copy-start(bf16[1024,256]{1,0:T(8,128)(2,1)} %param.26) | copy-start | bytes 1572868
  3.7 177.7 %copy-start.10 = (pred[128,32]{0,1:T(8,128)(4,1)}, pred[128,32]{0,1:T(8,128)(4,1)S(1)}, u32[]{:S(2)}) copy-start(pred[128,32]{0,1:T(8,128)(4,1)S(1)} %fusion.3) | copy-start | bytes 12292
  12.9 166.0 %copy-start.4 = (bf16[128,2048]{1,0:T(8,128)(2,1)S(1)}, bf16[128,2048]{1,0:T(8,128)(2,1)}, u32[]{:S(2)}) copy-start(bf16[128,2048]{1,0:T(8,128)(2,1)} %tok_ref.3) | copy-start | bytes 1572868
  16.9 164.1 %copy-start.11 = (f32[2048]{0:T(1024)S(1)}, f32[2048]{0:T(1024)}, u32[]{:S(2)}) copy-start(f32[2048]{0:T(1024)} %param.20) | copy-start | bytes 24580
  180.4 0.5 copy-start.14
  181.1 1.0 copy-start.2
  181.4 105.4 %copy-start.13 = (f32[128]{0:T(128)}, f32[128]{0:T(128)S(1)}, u32[]{:S(2)}) copy-start(f32[128]{0:T(128)S(1)} %get-tuple-element.117) | copy-start | bytes 1540
  181.5 105.3 %copy-start.15 = (f32[128]{0:T(128)}, f32[128]{0:T(128)S(1)}, u32[]{:S(2)}) copy-start(f32[128]{0:T(128)S(1)} %fusion.17) | copy-start | bytes 1540
  365.2 6.7 %copy-start.5 = (bf16[128,2048]{1,0:T(8,128)(2,1)S(1)}, bf16[128,2048]{1,0:T(8,128)(2,1)}, u32[]{:S(2)}) copy-start(bf16[128,2048]{1,0:T(8,128)(2,1)} %grad_ref.1) | copy-start | bytes 1572868
  367.3 6.6 %copy-start.3 = (bf16[128,2048]{1,0:T(8,128)(2,1)S(1)}, bf16[128,2048]{1,0:T(8,128)(2,1)}, u32[]{:S(2)}) copy-start(bf16[128,2048]{1,0:T(8,128)(2,1)} %copy-done.2) | copy-start | bytes 1572868
  582.9 3.2 copy-start.12
  582.9 4.3 copy-start.9
  582.9 4.9 copy-start.6
  589.1 4.5 copy-start.7
  591.2 9.5 %slice-start.2 = ((s8[6291456]{0:T(1024)(128)(4,1)}), s8[4194304]{0:T(1024)(128)(4,1)S(1)}, s32[]{:S(2)}) async-start(s8[6291456]{0:T(1024)(128)(4,1)} %bitcast.79), calls=%async_computation.2 | async-start | bytes 8388608
  594.6 6.1 slice-start.3
  594.6 9.0 %slice-start = ((s8[6291456]{0:T(1024)(128)(4,1)}), s8[4194304]{0:T(1024)(128)(4,1)S(1)}, s32[]{:S(2)}) async-start(s8[6291456]{0:T(1024)(128)(4,1)} %bitcast.76), calls=%async_computation | async-start | bytes 8388608
  600.7 3.1 slice-start.1
  600.7 5.8 copy-start.1

commit v4 on v3

--- a/solution.py
+++ b/solution.py
@@ -2,6 +2,7 @@
 
 import jax
 import jax.numpy as jnp
+import numpy as np
 from jax import lax
 from jax.experimental import pallas as pl
 from jax.experimental.pallas import tpu as pltpu
@@ -26,43 +27,13 @@
     return lax.rsqrt(jnp.mean(values * values, axis=-1, keepdims=True) + EPSILON)
 
 
-def rotary_tables(positions, width):
-    half = width // 2
-    freqs = THETA ** (-(jnp.arange(half, dtype=f32) * 2.0 / width))
-    angles = positions.astype(f32)[:, None] * freqs[None, :]
-    return (jnp.cos(angles), jnp.sin(angles))
-
-
-def rotate(values, cosine, sine):
-    half = values.shape[-1] // 2
-    first = values[..., :half]
-    second = values[..., half:]
-    return jnp.concatenate(
-        [first * cosine - second * sine, second * cosine + first * sine], axis=-1
-    )
-
-
-def unrotate(values, cosine, sine):
-    half = values.shape[-1] // 2
-    first = values[..., :half]
-    second = values[..., half:]
-    return jnp.concatenate(
-        [first * cosine + second * sine, second * cosine - first * sine], axis=-1
-    )
-
-
-def piece_ids(positions, starts):
-    inside = (positions[:, None] >= starts[None, :]) & (
-        positions[:, None] < starts[None, :] + IMG_LEN
-    )
-    labels = jnp.arange(1, starts.shape[0] + 1, dtype=jnp.int32)
-    return jnp.sum(jnp.where(inside, labels[None, :], 0), axis=1)
-
-
-def allowed_mask(query_pos, key_pos, query_piece, key_piece):
-    causal = key_pos[None, :] <= query_pos[:, None]
-    same = (query_piece[:, None] == key_piece[None, :]) & (query_piece[:, None] > 0)
-    return causal | same
+def rotary_tables(length):
+    freqs = np.float32(THETA) ** (-(np.arange(HD // 2, dtype=np.float32) * np.float32(2.0 / HD)))
+    angles = np.arange(length, dtype=np.float32)[:, None] * freqs.astype(np.float32)[None, :]
+    cosine, sine = np.cos(angles.astype(np.float64)), np.sin(angles.astype(np.float64))
+    first = np.concatenate([cosine, cosine], axis=1)
+    second = np.concatenate([-sine, sine], axis=1)
+    return np.stack([first, second]).astype(np.float32)
 
 
 def norm_back(grad_norm, hat, rms, gain):
@@ -141,28 +112,17 @@
         pl.when(when)(go)
 
 
-def greet(place, zn, ends=False, everyone=True, planes=True):
+def greet(place, zn, cross=False):
     bar = pltpu.get_barrier_semaphore()
-    count = 0
-    if planes:
-        for k in range(1, PLANE):
-            pl.semaphore_signal(
-                bar, inc=1, device_id=place.at(place.z, place.by(k)), device_id_type=MESH
-            )
-        count += PLANE - 1
-    if everyone:
-        for k in range(1, zn):
-            pl.semaphore_signal(
-                bar,
-                inc=1,
-                device_id=place.at((place.z + k) % zn, place.p),
-                device_id_type=MESH,
-            )
-        count += zn - 1
-    pl.semaphore_wait(bar, count)
-    if ends:
-        bar2 = 0
-        del bar2
+    met = [place.at(place.z, place.by(k)) for k in range(1, PLANE)]
+    for k in range(1, zn):
+        z = (place.z + k) % zn
+        met.append(place.at(z, place.p))
+        if cross:
+            met.append(place.at(z, place.flip(dy=1)))
+    for device in met:
+        pl.semaphore_signal(bar, inc=1, device_id=device, device_id_type=MESH)
+    pl.semaphore_wait(bar, len(met))
 
 
 class PlaneGather:
@@ -184,9 +144,11 @@
 
     def first(self):
         pc = self.place
-        self._send(pc.p, 0, pc.peer(dy=1))
         self._send(pc.p, 1, pc.peer(dx=1))
         self._send(pc.p, 2, pc.peer(dc=1))
+
+    def along(self):
+        self._send(self.place.p, 0, self.place.peer(dy=1))
 
     def second(self):
         pc = self.place
@@ -213,7 +175,11 @@
         self._wait(pc.flip(dc=1, dy=1, dx=1), 7)
 
 
-def add_rows(dst, first, second, rows, step=32):
+def add_rows(dst, first, second, rows, step=32, when=None):
+    if when is not None:
+        pl.when(when)(lambda: add_rows(dst, first, second, rows, step))
+        return
+
     def body(i, carry):
         at = pl.ds(pl.multiple_of(i * step, step), step)
         dst(at, first(at).astype(f32) + second(at).astype(f32))
@@ -223,132 +189,113 @@
 
 
 class PlaneReduce:
-    sems = 4 + 4 + 2
-
     @staticmethod
-    def scratch(rows, width):
+    def scratch(rows, width, windows=1):
         return [
-            pltpu.VMEM((4, rows, width), bf16),
-            pltpu.VMEM((4, rows, width), bf16),
-            pltpu.VMEM((2, rows, width // 2), bf16),
-            pltpu.VMEM((2, rows, width // 2), bf16),
-            pltpu.VMEM((2, rows, width // 2), bf16),
+            pltpu.VMEM((windows, 4, rows, width), bf16),
+            pltpu.VMEM((windows, 4, rows, width), bf16),
+            pltpu.VMEM((windows, 2, rows // 2, width), bf16),
+            pltpu.VMEM((windows, 2, rows // 2, width), bf16),
+            pltpu.VMEM((windows, 2, rows // 2, width), bf16),
         ]
 
-    def __init__(self, place, sends, part, out, scratch, ss, rs):
+    def __init__(self, place, sends, part, out, scratch, ss, rs, cols, slot=0, when=None):
         self.place, self.sends, self.part, self.out = place, sends, part, out
-        self.c1, self.s1, self.ra, self.rb, self.last = scratch
-        self.ss, self.rs = ss, rs
+        self.c1, self.s1, self.ra, self.rb, self.late = (ref.at[slot] for ref in scratch)
+        self.ss, self.rs = ss.at[slot], rs.at[slot]
+        self.cols, self.when = cols, when
         self.rows = part.shape[1]
-        half = part.shape[2] // 2
-        self.half = half
-        self.cols_a = pl.ds(0, half)
-        self.cols_b = pl.ds(half, half)
-        pc = place
+        self.half = self.rows // 2
         self.chips = [(1, 1), (0, 1), (1, 0), (0, 0)]
 
-    def _chip(self, dy, dx):
+    def chip(self, dy, dx):
         pc = self.place
         y = 1 - pc.y if dy else pc.y
         x = 1 - pc.x if dx else pc.x
         return y, x, y * 2 + x
 
+    def _send(self, src, dst, i, device):
+        self.sends.start(src, dst, self.ss.at[i], self.rs.at[i], device, self.when)
+
+    def _take(self, dst, i):
+        arrived(dst, self.rs.at[i], self.when)
+
+    def _add(self, dst, first, second, rows):
+        add_rows(dst, first, second, rows, when=self.when)
+
     def first(self, k):
         pc = self.place
-        y, x, j = self._chip(*self.chips[k])
+        y, x, j = self.chip(*self.chips[k])
         block = y * 4 + x * 2 + (1 - pc.c)
-        self.sends.start(
-            self.part.at[block], self.c1.at[j], self.ss.at[k], self.rs.at[k], pc.peer(dc=1)
-        )
+        self._send(self.part.at[block, :, self.cols], self.c1.at[j], k, pc.peer(dc=1))
 
     def second(self, k):
         pc = self.place
-        y, x, j = self._chip(*self.chips[k])
-        arrived(self.c1.at[j], self.rs.at[k])
+        dy, dx = self.chips[k]
+        y, x, j = self.chip(dy, dx)
+        self._take(self.c1.at[j], k)
         mine = y * 4 + x * 2 + pc.c
 
         def put(at, v):
             self.s1[j, at, :] = v.astype(bf16)
 
-        add_rows(put, lambda at: self.part[mine, at, :], lambda at: self.c1[j, at, :], self.rows)
-        dy, dx = self.chips[k]
+        self._add(
+            put, lambda at: self.part[mine, at, self.cols], lambda at: self.c1[j, at, :], self.rows
+        )
         if dx:
-            self.sends.start(
-                self.s1.at[j, :, self.cols_a],
+            self._send(
+                self.s1.at[j, pl.ds(0, self.half), :],
                 self.ra.at[y],
-                self.ss.at[4 + (0 if dy else 1)],
-                self.rs.at[4 + (0 if dy else 1)],
+                4 + (0 if dy else 1),
                 pc.peer(dx=1),
             )
         if dy:
-            self.sends.start(
-                self.s1.at[j, :, self.cols_b],
+            self._send(
+                self.s1.at[j, pl.ds(self.half, self.half), :],
                 self.rb.at[x],
-                self.ss.at[6 + (0 if dx else 1)],
-                self.rs.at[6 + (0 if dx else 1)],
+                6 + (0 if dx else 1),
                 pc.peer(dy=1),
             )
 
     def third(self):
         pc = self.place
-        other_y, other_x = 1 - pc.y, 1 - pc.x
-        arrived(self.ra.at[other_y], self.rs.at[4])
-        j = other_y * 2 + pc.x
-
-        def put_a(at, v):
-            self.ra[other_y, at, :] = v.astype(bf16)
-
-        add_rows(
-            put_a,
-            lambda at: self.s1[j, at, self.cols_a],
-            lambda at: self.ra[other_y, at, :],
-            self.rows,
-        )
-        self.sends.start(
-            self.ra.at[other_y], self.last.at[0], self.ss.at[8], self.rs.at[8], pc.peer(dy=1)
-        )
-        arrived(self.rb.at[other_x], self.rs.at[6])
-        i = pc.y * 2 + other_x
-
-        def put_b(at, v):
-            self.rb[other_x, at, :] = v.astype(bf16)
-
-        add_rows(
-            put_b,
-            lambda at: self.s1[i, at, self.cols_b],
-            lambda at: self.rb[other_x, at, :],
-            self.rows,
-        )
-        self.sends.start(
-            self.rb.at[other_x], self.last.at[1], self.ss.at[9], self.rs.at[9], pc.peer(dx=1)
-        )
+        for buf, slot, base, sem, other, out_sem in (
+            (self.ra, 1 - pc.y, 0, 4, pc.peer(dy=1), 8),
+            (self.rb, 1 - pc.x, self.half, 6, pc.peer(dx=1), 9),
+        ):
+            self._take(buf.at[slot], sem)
+            j = (1 - pc.y) * 2 + pc.x if base == 0 else pc.y * 2 + 1 - pc.x
+
+            def put(at, v, buf=buf, slot=slot):
+                buf[slot, at, :] = v.astype(bf16)
+
+            self._add(
+                put,
+                lambda at, j=j, base=base: self.s1[j, pl.ds(at.start + base, at.size), :],
+                lambda at, buf=buf, slot=slot: buf[slot, at, :],
+                self.half,
+            )
+            self._send(buf.at[slot], self.late.at[out_sem - 8], out_sem, other)
 
     def finish(self):
         pc = self.place
         own = pc.y * 2 + pc.x
-        arrived(self.ra.at[pc.y], self.rs.at[5])
-        arrived(self.rb.at[pc.x], self.rs.at[7])
-
-        def put_a(at, v):
-            self.out[at, self.cols_a] = v + self.ra[pc.y, at, :].astype(f32)
-
-        def put_b(at, v):
-            self.out[at, self.cols_b] = v + self.rb[pc.x, at, :].astype(f32)
-
-        arrived(self.last.at[0], self.rs.at[8])
-        add_rows(
-            put_a,
-            lambda at: self.s1[own, at, self.cols_a],
-            lambda at: self.last[0, at, :],
-            self.rows,
-        )
-        arrived(self.last.at[1], self.rs.at[9])
-        add_rows(
-            put_b,
-            lambda at: self.s1[own, at, self.cols_b],
-            lambda at: self.last[1, at, :],
-            self.rows,
-        )
+        for i, (buf, slot, base, sem) in enumerate(
+            ((self.ra, pc.y, 0, 5), (self.rb, pc.x, self.half, 7))
+        ):
+            self._take(buf.at[slot], sem)
+            self._take(self.late.at[i], 8 + i)
+
+            def put(at, v, buf=buf, slot=slot, base=base):
+                to = pl.ds(at.start + base, at.size)
+                self.out[to, self.cols] = v + buf[slot, at, :].astype(f32)
+
+            self._add(
+                put,
+                lambda at, base=base: self.s1[own, pl.ds(at.start + base, at.size), :],
+                lambda at, i=i: self.late[i, at, :],
+                self.half,
+            )
 
 
 class ColumnGather:
@@ -424,6 +371,7 @@
 
 VSPEC = pl.BlockSpec(memory_space=pltpu.VMEM)
 ASPEC = pl.BlockSpec(memory_space=pl.ANY)
+SSPEC = pl.BlockSpec(memory_space=pltpu.SMEM)
 
 
 def params(cid):
@@ -432,55 +380,32 @@
     )
 
 
-class RowChain:
-    def __init__(self, place, sends, zn, src, buf, chunk, ss_r, ss_l, rs):
+class RowPush:
+    def __init__(self, place, sends, zn, src, buf, chunk, ss, rs):
         self.place, self.sends, self.zn = place, sends, zn
         self.src, self.buf, self.chunk = src, buf, chunk
-        self.ss_r, self.ss_l, self.rs = ss_r, ss_l, rs
-
-    def _on(self, src, c, origin, right, left):
-        pc = self.place
-        dst = self.buf.at[origin, :, pl.ds(c * self.chunk, self.chunk)]
-        if right is not None:
+        self.ss, self.rs = ss, rs
+
+    def own(self, c):
+        pc = self.place
+        cols = pl.ds(c * self.chunk, self.chunk)
+        for k in range(1, self.zn):
             self.sends.start(
-                src,
-                dst,
-                self.ss_r.at[c, origin],
-                self.rs.at[c, origin],
-                pc.at(jnp.minimum(pc.z + 1, self.zn - 1), pc.p),
-                right,
+                self.src.at[:, cols],
+                self.buf.at[pc.z, :, cols],
+                self.ss.at[c, k],
+                self.rs.at[c, pc.z],
+                pc.at((pc.z + k) % self.zn, pc.p),
             )
-        if left is not None:
-            self.sends.start(
-                src,
-                dst,
-                self.ss_l.at[c, origin],
-                self.rs.at[c, origin],
-                pc.at(jnp.maximum(pc.z - 1, 0), pc.p),
-                left,
-            )
-
-    def own(self, c):
-        pc = self.place
-        src = self.src.at[:, pl.ds(c * self.chunk, self.chunk)]
-        self._on(src, c, pc.z, pc.z < self.zn - 1, pc.z > 0)
 
     def keep(self):
         self.buf[self.place.z] = self.src[...]
 
-    def step(self, c, k):
-        pc = self.place
-        cols = pl.ds(c * self.chunk, self.chunk)
-        below = jnp.maximum(pc.z - k, 0)
-        has = pc.z - k >= 0
-        ref = self.buf.at[below, :, cols]
-        arrived(ref, self.rs.at[c, below], has)
-        self._on(ref, c, below, jnp.logical_and(has, pc.z < self.zn - 1), None)
-        above = jnp.minimum(pc.z + k, self.zn - 1)
-        has = pc.z + k < self.zn
-        ref = self.buf.at[above, :, cols]
-        arrived(ref, self.rs.at[c, above], has)
-        self._on(ref, c, above, None, jnp.logical_and(has, pc.z > 0))
+    def take(self, c):
+        pc = self.place
+        for k in range(1, self.zn):
+            d = (pc.z + k) % self.zn
+            arrived(self.buf.at[d, :, pl.ds(c * self.chunk, self.chunk)], self.rs.at[c, d])
 
 
 def turned(values):
@@ -504,6 +429,18 @@
 
 def key_limit(i, length):
     return min(length, (i + 1) * QBLOCK + IMG_LEN)
+
+
+def bias_block(starts, at, length, turn):
+    limit = length
+    shape = (limit, QBLOCK) if turn else (QBLOCK, limit)
+    query = lax.broadcasted_iota(jnp.int32, shape, 1 if turn else 0) + at
+    key = lax.broadcasted_iota(jnp.int32, shape, 0 if turn else 1)
+    allowed = key <= query
+    for start in starts:
+        low = (query >= start) & (query < start + IMG_LEN)
+        allowed = allowed | (low & (key >= start) & (key < start + IMG_LEN))
+    return jnp.where(allowed, 0.0, NEGATIVE)
 
 
 def send_slots(place, sends, zn, src, dst, ss, rs):
@@ -545,8 +482,8 @@
         for k in (1, 2, 3, 4, 5, 6, 7, 0):
             p = pc.by(k) if k else pc.p
             got = nn_dot(self.hot[p], self.rows[:, :, cols].reshape(zn * tok, self.chunk))
+            self.buf[p, :, cols] = got.astype(bf16)
             if k:
-                self.buf[p, :, cols] = got.astype(bf16)
                 self.sends.start(
                     self.buf.at[p, :, cols],
                     self.out.at[pc.p, :, cols],
@@ -555,69 +492,81 @@
                     pc.at(pc.z, p),
                 )
             else:
-                self.out[pc.p, :, cols] = got.astype(bf16)
+                self._own(c).start()
+
+    def _own(self, c):
+        p = self.place.p
+        cols = pl.ds(c * self.chunk, self.chunk)
+        return pltpu.make_async_copy(self.buf.at[p, :, cols], self.out.at[p, :, cols], self.rs.at[c, 0])
 
     def take(self, c):
         cols = pl.ds(c * self.chunk, self.chunk)
+        self._own(c).wait()
         for k in range(1, PLANE):
             arrived(self.out.at[self.place.by(k), :, cols], self.rs.at[c, k])
 
 
 def front_kernel(
-    zn, cap, chunk, heads,
-    tok_ref, gain_ref, pq_ref, po_ref, tab_ref, hg_ref, bias_ref, grad_ref, slot_ref,
-    seq_ref, wq_ref, wo_ref, pre_ref, rot_ref, val_ref, lse_ref, ctx_ref, att_ref, ag_ref, so_ref,
+    zn, cap, chunk, heads, starts_ref,
+    tok_ref, gain_ref, q_ref, k_ref, v_ref, o_ref, hg_ref, grad_ref, slot_ref, tab_hbm,
+    lse_ref, att_ref, so_ref, seq_hbm, wq_hbm, wo_hbm, pre_hbm, rot_hbm, val_hbm, ctx_hbm, ag_hbm,
+    seq, wq, wo, pre, rot, val, ctx, tab, bias, pq, po,
     part, c1, s1, ra, rb, last, gb, sn, hot,
-    gs, gr, ps, pr, sr, sl, rs, hs, hr, zsr, zsl, zr, ts, tr, xs, xr,
+    gs, gr, ps, pr, sr, sl, rs, hs, hr, zs, zr, ts, tr, xs, xr, out_sems,
 ):
     place, sends = Place(), Sends()
     pc = place
     tok, width = tok_ref.shape
     length = PLANE * tok
-    own_rows = pq_ref.shape[1]
+    own_rows = pq.shape[1]
     half = heads * HD
     chunks = width // chunk
     scale = HD ** (-0.5)
+    table = pltpu.make_async_copy(tab_hbm, tab, out_sems.at[7])
+    table.start()
+    for y in range(2):
+        pq[y, :, :half] = q_ref[:, y * half : (y + 1) * half]
+        pq[y, :, half : half + HD] = k_ref[...]
+        pq[y, :, half + HD :] = v_ref[...]
     greet(place, zn)
-    q = ColumnGather(
-        place, sends, zn, pq_ref, wq_ref, ps.at[0], pr.at[0], sr.at[0], sl.at[0], rs.at[0]
-    )
-    o = ColumnGather(
-        place, sends, zn, po_ref, wo_ref, ps.at[1], pr.at[1], sr.at[1], sl.at[1], rs.at[1]
-    )
-    g = RowChain(place, sends, zn, grad_ref, gb, chunk, zsr, zsl, zr)
+    q = ColumnGather(place, sends, zn, pq, wq, ps.at[0], pr.at[0], sr.at[0], sl.at[0], rs.at[0])
+    o = ColumnGather(place, sends, zn, po, wo, ps.at[1], pr.at[1], sr.at[1], sl.at[1], rs.at[1])
+    g = RowPush(place, sends, zn, grad_ref, gb, chunk, zs, zr)
     q.pair()
     q.own()
 
     def first_norm(i, carry):
         at = pl.ds(pl.multiple_of(i * 32, 32), 32)
         v = tok_ref[at, :].astype(f32)
-        seq_ref[pc.p, at, :] = (v * rms_scale(v) * gain_ref[...]).astype(bf16)
+        seq[pc.p, at, :] = (v * rms_scale(v) * gain_ref[...]).astype(bf16)
         return carry
 
     lax.fori_loop(0, tok // 32, first_norm, 0)
-    rows = PlaneGather(place, sends, seq_ref, gs, gr)
+    rows = PlaneGather(place, sends, seq, gs, gr)
     rows.first()
-    send_slots(place, sends, zn, slot_ref, so_ref, ts, tr)
     q.keep()
     q.partner()
+    rows.along()
+    send_slots(place, sends, zn, slot_ref, so_ref, ts, tr)
+    for y in range(2):
+        po[y] = o_ref[y * half : (y + 1) * half, :].astype(f32).T.astype(bf16)
+    o.keep()
+    g.keep()
     rows.second()
     o.pair()
-    o.keep()
-    g.keep()
-    rows.third()
     take_slots(place, zn, slot_ref, so_ref, tr)
     make_hot(zn, cap, tok, so_ref, hot)
-    pre_ref[...] = jnp.zeros_like(pre_ref)
+    rows.third()
+    pre[...] = jnp.zeros_like(pre)
 
     def project(origin):
         cols = pl.ds(pl.multiple_of(origin * 2 * own_rows, 2 * own_rows), 2 * own_rows)
-        weight = wq_ref.at[pl.ds(2 * origin, 2)]
+        weight = wq.at[pl.ds(2 * origin, 2)]
 
         def body(i, carry):
             at = pl.ds(pl.multiple_of(i * 2 * tok, 2 * tok), 2 * tok)
-            lhs = seq_ref[pl.ds(2 * i, 2), :, cols].reshape(2 * tok, 2 * own_rows)
-            pre_ref[at, :] += nn_dot(lhs, weight[...].reshape(2 * own_rows, half + 2 * HD))
+            lhs = seq[pl.ds(2 * i, 2), :, cols].reshape(2 * tok, 2 * own_rows)
+            pre[at, :] += nn_dot(lhs, weight[...].reshape(2 * own_rows, half + 2 * HD))
             return carry
 
         lax.fori_loop(0, PLANE // 2, body, 0)
@@ -626,129 +575,194 @@
         pl.when(pc.z - k >= 0)(lambda: project(jnp.maximum(pc.z - k, 0)))
         pl.when(pc.z + k < zn)(lambda: project(jnp.minimum(pc.z + k, zn - 1)))
 
+    kept = []
+
+    def keep(i, src, dst):
+        copy = pltpu.make_async_copy(src, dst, out_sems.at[i])
+        copy.start()
+        kept.append(copy)
+
     for k in range(1, zn):
         q.step(k)
+        if k == max(1, zn - 2):
+            g.own(0)
         if k == 1:
             rows.last()
+            keep(0, seq, seq_hbm)
             project(pc.z)
-        if k == zn - 1:
-            for c in range(chunks):
-                g.own(c)
-            o.own()
-            o.partner()
         project_step(k)
+    g.own(1)
+    keep(1, wq, wq_hbm)
+    keep(2, pre, pre_hbm)
+    table.wait()
 
     def turn(i, carry):
         at = pl.ds(pl.multiple_of(i * 128, 128), 128)
-        cos, sin = tab_ref[0, at, :], tab_ref[1, at, :]
+        cos, sin = tab[0, at, :], tab[1, at, :]
         for h in range(heads + 1):
-            v = pre_ref[at, h * HD : (h + 1) * HD]
+            v = pre[at, h * HD : (h + 1) * HD]
             gain = hg_ref[pl.ds(0 if h < heads else 1, 1), :]
             v = v * rms_scale(v) * gain
-            rot_ref[h, at, :] = (v * cos + turned(v) * sin).astype(bf16)
-        val_ref[at, :] = pre_ref[at, half + HD : half + 2 * HD].astype(bf16)
+            rot[h, at, :] = (v * cos + turned(v) * sin).astype(bf16)
+        val[at, :] = pre[at, half + HD : half + 2 * HD].astype(bf16)
         return carry
 
     lax.fori_loop(0, length // 128, turn, 0)
+    keep(3, rot, rot_hbm)
+    keep(4, val, val_hbm)
     lane = lax.broadcasted_iota(jnp.int32, (QBLOCK, 128), 1)
+    starts = [starts_ref[pc.z, j] for j in range(starts_ref.shape[1])]
 
     def attend(i):
         limit = key_limit(i, length)
         at = slice(i * QBLOCK, (i + 1) * QBLOCK)
+        bias[:, :limit] = bias_block(starts, i * QBLOCK, limit, False)
 
         def body(h, carry):
-            scores = nt_dot(rot_ref[h, at, :], rot_ref[heads, :limit, :]) * scale
-            scores = scores + bias_ref[at, :limit].astype(f32)
+            scores = nt_dot(rot[h, at, :], rot[heads, :limit, :]) * scale + bias[:, :limit]
             top = jnp.max(scores, axis=1, keepdims=True)
             expo = jnp.exp(scores - top)
             total = jnp.sum(expo, axis=1, keepdims=True)
             low = (expo * (1.0 / total)).astype(bf16)
             cols = pl.ds(pl.multiple_of(h * HD, HD), HD)
-            ctx_ref[at, cols] = nn_dot(low, val_ref[:limit, :]).astype(bf16)
+            ctx[at, cols] = nn_dot(low, val[:limit, :]).astype(bf16)
             lse_ref[at, :] = jnp.where(lane == h, top + jnp.log(total), lse_ref[at, :])
             return carry
 
-        lax.fori_loop(0, heads, body, 0)
+        lax.fori_loop(0, heads, body, 0, unroll=2)
 
     lse_ref[...] = jnp.zeros_like(lse_ref)
-    hops = [(c, k) for k in range(1, zn) for c in range(chunks)]
+    give = PlaneSend(place, sends, hot, gb, sn, ag_hbm, chunk, xs, xr)
     blocks = length // QBLOCK
-    ahead = min(len(hops), 2 * (blocks - 1))
-    done = 0
+    given = 0
     for i in range(blocks):
         attend(i)
-        while i < blocks - 1 and done < ahead and done < 2 * (i + 1):
-            g.step(*hops[done])
-            done += 1
+        if given < chunks - 1:
+            g.take(given)
+            if given < chunks - 3:
+                g.own(given + 2)
+            if given == max(chunks - 3, 0):
+                o.own()
+                o.partner()
+            give.send(given)
+            given += 1
+    keep(5, ctx, ctx_hbm)
 
     def output(origin):
         cols = pl.ds(pl.multiple_of(origin * 2 * own_rows, 2 * own_rows), 2 * own_rows)
-        weight = wo_ref.at[pl.ds(2 * origin, 2)]
+        weight = wo.at[pl.ds(2 * origin, 2)]
 
         def body(i, carry):
             at = pl.ds(pl.multiple_of(i * 2 * tok, 2 * tok), 2 * tok)
-            got = nt_dot(ctx_ref[at, :], weight[...].reshape(2 * own_rows, half))
+            got = nt_dot(ctx[at, :], weight[...].reshape(2 * own_rows, half))
             part[pl.ds(2 * i, 2), :, cols] = got.astype(bf16).reshape(2, tok, 2 * own_rows)
             return carry
 
         lax.fori_loop(0, PLANE // 2, body, 0)
 
-    def output_step(k):
-        pl.when(pc.z - k >= 0)(lambda: output(jnp.maximum(pc.z - k, 0)))
-        pl.when(pc.z + k < zn)(lambda: output(jnp.minimum(pc.z + k, zn - 1)))
-
-    output(pc.z)
-    give = PlaneSend(place, sends, hot, gb, sn, ag_ref, chunk, xs, xr)
-    for c, k in hops[done:]:
-        g.step(c, k)
-        if k == zn - 1:
-            give.send(c)
+    def visit(origin, when):
+        cols = pl.ds(pl.multiple_of(origin * 2 * own_rows, 2 * own_rows), 2 * own_rows)
+        red = PlaneReduce(
+            place, sends, part, att_ref, (c1, s1, ra, rb, last), hs, hr, cols, origin, when
+        )
+        if when is None:
+            output(origin)
+        else:
+            pl.when(when)(lambda: output(origin))
+        for j in range(4):
+            red.first(j)
+        visits.append(red)
+
+    def push_on():
+        for lag, stage in ((2, 2), (3, 3), (4, 4)):
+            if len(visits) >= lag:
+                step_on(visits[-lag], stage)
+
+    def step_on(red, stage):
+        if stage == 2:
+            for j in range(4):
+                red.second(j)
+        elif stage == 3:
+            red.third()
+        else:
+            red.finish()
+
+    visits = []
+    visit(pc.z, None)
     for k in range(1, zn):
         o.step(k)
-        output_step(k)
-    red = PlaneReduce(place, sends, part, att_ref, (c1, s1, ra, rb, last), hs, hr)
-    for k in range(4):
-        red.first(k)
-    for k in range(4):
-        red.second(k)
-    red.third()
-    red.finish()
+        if k == max(1, zn - 2):
+            g.own(chunks - 1)
+        visit(jnp.maximum(pc.z - k, 0), pc.z - k >= 0)
+        push_on()
+        visit(jnp.minimum(pc.z + k, zn - 1), pc.z + k < zn)
+        push_on()
+    keep(6, wo, wo_hbm)
+    step_on(visits[-1], 2)
+    while given < chunks:
+        g.take(given)
+        give.send(given)
+        given += 1
+    step_on(visits[-2], 3)
+    step_on(visits[-1], 3)
+    for red in visits[-3:]:
+        step_on(red, 4)
     for c in range(chunks):
         give.take(c)
+    for copy in kept:
+        copy.wait()
     sends.finish()
 
 
-def front(zn, cap, heads, tokens, gain, pack_q, pack_o, tables, gains, bias, grad, slot, chunk=512):
+def front(
+    zn, cap, heads, starts, tokens, gain, query, key, value, output, gains, grad, slot, tables, chunk=512
+):
     tok, width = tokens.shape
     length = PLANE * tok
+    own_rows = query.shape[0]
     e = 2 * zn
     slots = zn * cap
     chunks = width // chunk
     half = heads * HD
+    wide = half + 2 * HD
     shape = jax.ShapeDtypeStruct
+    vmem = pltpu.VMEM
     return pl.pallas_call(
         functools.partial(front_kernel, zn, cap, chunk, heads),
         out_shape=(
+            shape((length, 128), f32),
+            shape((tok, width), f32),
+            shape(slot.shape, f32),
             shape((PLANE, tok, width), bf16),
-            shape((e,) + pack_q.shape[1:], bf16),
-            shape((e,) + pack_o.shape[1:], bf16),
-            shape((length, half + 2 * HD), f32),
+            shape((e, own_rows, wide), bf16),
+            shape((e, own_rows, half), bf16),
+            shape((length, wide), f32),
             shape((heads + 1, length, HD), bf16),
             shape((length, HD), bf16),
-            shape((length, 128), f32),
             shape((length, half), bf16),
-            shape((tok, width), f32),
             shape((PLANE, slots, width), bf16),
-            shape(slot.shape, f32),
         ),
-        in_specs=[VSPEC] * 9,
-        out_specs=(VSPEC,) * 11,
-        scratch_shapes=[pltpu.VMEM((PLANE, tok, width), bf16)]
-        + PlaneReduce.scratch(tok, width)
+        in_specs=[SSPEC] + [VSPEC] * 9 + [ASPEC],
+        out_specs=(VSPEC,) * 3 + (ASPEC,) * 8,
+        scratch_shapes=[
+            vmem((PLANE, tok, width), bf16),
+            vmem((e, own_rows, wide), bf16),
+            vmem((e, own_rows, half), bf16),
+            vmem((length, wide), f32),
+            vmem((heads + 1, length, HD), bf16),
+            vmem((length, HD), bf16),
+            vmem((length, half), bf16),
+            vmem((2, length, HD), f32),
+            vmem((QBLOCK, length), f32),
+            vmem((2, own_rows, wide), bf16),
+            vmem((2, own_rows, half), bf16),
+            vmem((PLANE, tok, width), bf16),
+        ]
+        + PlaneReduce.scratch(tok, 2 * own_rows, zn)
         + [
-            pltpu.VMEM((zn, tok, width), bf16),
-            pltpu.VMEM((PLANE, slots, width), bf16),
-            pltpu.VMEM((PLANE, slots, zn * tok), bf16),
+            vmem((zn, tok, width), bf16),
+            vmem((PLANE, slots, width), bf16),
+            vmem((PLANE, slots, zn * tok), bf16),
             dma_sems(8),
             dma_sems(8),
             dma_sems(2),
@@ -756,19 +770,19 @@
             dma_sems(2, e),
             dma_sems(2, e),
             dma_sems(2, e),
-            dma_sems(10),
-            dma_sems(10),
-            dma_sems(chunks, zn),
+            dma_sems(zn, 10),
+            dma_sems(zn, 10),
             dma_sems(chunks, zn),
             dma_sems(chunks, zn),
             dma_sems(zn),
             dma_sems(zn),
             dma_sems(chunks, PLANE),
             dma_sems(chunks, PLANE),
+            dma_sems(8),
         ],
         compiler_params=params(0),
         name="front",
-    )(tokens, gain, pack_q, pack_o, tables, gains, bias, grad, slot)
+    )(starts, tokens, gain, query, key, value, output, gains, grad, slot, tables)
 
 
 class Flow:
@@ -800,9 +814,9 @@
 
 def there_kernel(
     zn, cap, chunk, norm_ref, slots_ref, mix_ref, ag_hbm, gate_hbm, up_hbm, down_hbm,
-    an_ref, mid_ref, dot_ref, hot_t_hbm, comb_hbm,
-    nb, sn, hot, mo, mrow, mr, wg, wu, wd, ag, gate, up, unmixed, stage, loads, flows,
-    zsr, zsl, zr, ts, tr, xs, xr, ys, yr,
+    dot_ref, an_hbm, mid_hbm, hot_t_hbm, comb_hbm,
+    an_ref, mid_ref, nb, sn, hot, mo, mrow, mr, wg, wu, wd, ag, gate, up, unmixed, stage, loads, flows, keeps,
+    zs, zr, ts, tr, xs, xr, ys, yr,
 ):
     place, sends = Place(), Sends()
     pc = place
@@ -822,9 +836,8 @@
         )
         for c in range(chunks)
     ]
-    n = RowChain(place, sends, zn, norm_ref, nb, chunk, zsr, zsl, zr)
-    for c in range(chunks):
-        n.own(c)
+    n = RowPush(place, sends, zn, norm_ref, nb, chunk, zs, zr)
+    n.own(0)
     send_slots(place, sends, zn, mix_ref, mo, ts, tr)
     fetch[0].start()
     parts[0].start()
@@ -852,6 +865,8 @@
         p = pc.by(k)
         sends.start(mrow.at[p], mr.at[pc.p], ys.at[k], yr.at[k], pc.at(pc.z, p))
     mr[pc.p] = mrow[pc.p]
+    if chunks > 1:
+        n.own(1)
     fetch[0].wait()
     give = PlaneSend(place, sends, hot, nb, sn, an_ref, chunk, xs, xr)
     half = PLANE // 2
@@ -872,8 +887,9 @@
             parts[c + 2].start()
 
     for c in range(chunks):
-        for k in range(1, zn):
-            n.step(c, k)
+        n.take(c)
+        if c + 2 < chunks:
+            n.own(c + 2)
         give.send(c)
         back_through(c)
 
@@ -907,9 +923,13 @@
     lax.fori_loop(0, zn, tables, 0)
     fetch[1].wait()
     fetch[2].wait()
+    saves = []
     for c in range(chunks):
         cols = pl.ds(c * chunk, chunk)
         give.take(c)
+        save = pltpu.make_async_copy(an_ref.at[:, :, cols], an_hbm.at[:, :, cols], keeps.at[PLANE + c])
+        save.start()
+        saves.append(save)
 
         def into(i, carry):
             at = pl.ds(i * half, half)
@@ -943,9 +963,14 @@
         d = d * mix
         mid_ref[2, p] = (d * u * sig * (1.0 + g * (1.0 - sig))).astype(bf16)
         mid_ref[3, p] = (d * act).astype(bf16)
+        pltpu.make_async_copy(mid_ref.at[:, p], mid_hbm.at[:, p], keeps.at[p]).start()
         return carry
 
     lax.fori_loop(0, PLANE, acts, 0)
+    for p in range(PLANE):
+        saves.append(pltpu.make_async_copy(mid_ref.at[:, p], mid_hbm.at[:, p], keeps.at[p]))
+    for save in saves:
+        save.wait()
     sends.finish()
 
 
@@ -959,15 +984,17 @@
     return pl.pallas_call(
         functools.partial(there_kernel, zn, cap, chunk),
         out_shape=(
+            shape((PLANE, slots, 128), bf16),
             shape((PLANE, slots, width), bf16),
             shape((4, PLANE, slots, hidden), bf16),
-            shape((PLANE, slots, 128), bf16),
             shape((zn * tok, PLANE * slots), bf16),
             shape((zn * tok, PLANE * slots), bf16),
         ),
         in_specs=[VSPEC] * 3 + [ASPEC] * 4,
-        out_specs=(VSPEC,) * 3 + (ASPEC,) * 2,
+        out_specs=(VSPEC,) + (ASPEC,) * 4,
         scratch_shapes=[
+            vmem((PLANE, slots, width), bf16),
+            vmem((4, PLANE, slots, hidden), bf16),
             vmem((zn, tok, width), bf16),
             vmem((PLANE, slots, width), bf16),
             vmem((PLANE, slots, zn * tok), bf16),
@@ -984,7 +1011,7 @@
             vmem((2, tok, PLANE * slots), bf16),
             dma_sems(5),
             dma_sems(2),
-            dma_sems(chunks, zn),
+            dma_sems(PLANE + chunks),
             dma_sems(chunks, zn),
             dma_sems(chunks, zn),
             dma_sems(zn),
@@ -1001,9 +1028,9 @@
 
 def back_kernel(
     zn, chunk, dot_ref, hot_ref, mid_hbm, an_hbm, ag_hbm, gate_hbm, up_hbm, down_hbm,
-    dots_ref, ap_hbm, res_hbm, gg_hbm, ug_hbm, dg_hbm,
+    dots_ref, ap_hbm, res_hbm, gg_hbm, ug_hbm, dg_hbm, rr_hbm,
     mids, an, ag, wg, wu, wd, pb, rp, rd, zd, zp, wide, tall, flat,
-    loads, flows, xs, xr, ds, dr, zs, zr, es, er, os,
+    loads, flows, xs, xr, ds, dr, zs, zr, es, er, os, vs, vr,
 ):
     place, sends = Place(), Sends()
     pc = place
@@ -1031,7 +1058,7 @@
         sends.start(dot_ref.at[p], rd.at[pc.p], ds.at[k], dr.at[k], pc.at(pc.z, p))
     for copy in fetch[:4]:
         copy.wait()
-    for c in range(chunks):
+    def pair_chunk(c):
         cols = pl.ds(c * chunk, chunk)
 
         def pair(i, carry):
@@ -1042,12 +1069,20 @@
             return carry
 
         lax.fori_loop(0, 2, pair, 0)
+        rp[pc.p, :, cols] = pb[pc.p, :, cols]
+
+    def pair_send(c):
+        cols = pl.ds(c * chunk, chunk)
         for k in range(1, PLANE):
             p = pc.by(k)
             sends.start(
                 pb.at[p, :, cols], rp.at[pc.p, :, cols], xs.at[c, k], xr.at[c, k], pc.at(pc.z, p)
             )
-        rp[pc.p, :, cols] = pb[pc.p, :, cols]
+
+    for c in range(chunks):
+        pair_chunk(c)
+        if c < 2:
+            pair_send(c)
     rd[pc.p] = dot_ref[pc.p]
     for k in range(1, PLANE):
         arrived(rd.at[pc.by(k)], dr.at[k])
@@ -1100,6 +1135,19 @@
         cols = pl.ds(c * chunk, chunk)
         for k in range(1, PLANE):
             arrived(rp.at[pc.by(k), :, cols], xr.at[c, k])
+        if c + 2 < chunks:
+            pair_send(c + 2)
+        if c == chunks - 1:
+            flow_r.finish()
+            for k in range(1, PLANE):
+                p = pc.by(k)
+                sends.start(
+                    res_hbm.at[p, :, pl.ds(0, chunk)],
+                    rr_hbm.at[pc.p],
+                    vs.at[k],
+                    vr.at[k],
+                    pc.at(pc.z, p),
+                )
         got = nn_dot(hot_ref[...], rp[:, :, cols].reshape(PLANE * slots, chunk))
         zp[:, :, cols] = got.astype(bf16).reshape(zn, tok, chunk)
         for k, d in enumerate(far):
@@ -1132,6 +1180,8 @@
             arrived(ap_hbm.at[d, :, pl.ds(c * chunk, chunk)], zr.at[c, d])
     for keep in keeps:
         keep.wait()
+    for k in range(1, PLANE):
+        arrived(rr_hbm.at[pc.by(k)], vr.at[k])
     for d in far:
         arrived(dots_ref.at[d], er.at[d])
     for flow in (flow_r, flow_g, flow_u, flow_d):
@@ -1154,9 +1204,10 @@
             shape(gate.shape, f32),
             shape(up.shape, f32),
             shape(down.shape, f32),
+            shape((PLANE, slots, chunk), bf16),
         ),
         in_specs=[VSPEC] * 2 + [ASPEC] * 6,
-        out_specs=(VSPEC,) + (ASPEC,) * 5,
+        out_specs=(VSPEC,) + (ASPEC,) * 6,
         scratch_shapes=[
             vmem((4, PLANE, slots, hidden), bf16),
             vmem((PLANE, slots, width), bf16),
@@ -1183,6 +1234,8 @@
             dma_sems(zn),
             dma_sems(zn),
             dma_sems(chunks),
+            dma_sems(PLANE),
+            dma_sems(PLANE),
         ],
         compiler_params=params(4),
         name="back_rows",
@@ -1368,27 +1421,27 @@
 
 
 class Result:
-    def __init__(self, place, zn, res, comb, rr, am, rbuf, zbuf, chunk, xs, xr, zs, zr, ls, os):
-        self.place, self.zn, self.res, self.comb = place, zn, res, comb
+    def __init__(self, place, sends, zn, res, first, comb, rr, am, rbuf, zbuf, chunk, xs, xr, zs, zr, ls, os):
+        self.place, self.sends, self.zn, self.res, self.comb = place, sends, zn, res, comb
         self.rr, self.am, self.rbuf, self.zbuf, self.chunk = rr, am, rbuf, zbuf, chunk
         self.xs, self.xr, self.zs, self.zr, self.ls, self.os = xs, xr, zs, zr, ls, os
+        self.early = first
         self.flight = {}
 
-    def first(self, sends, chunks):
-        pc = self.place
-        for c in range(chunks):
-            cols = pl.ds(c * self.chunk, self.chunk)
-            for k in range(1, PLANE):
-                p = pc.by(k)
-                sends.start(
-                    self.res.at[p, :, cols],
-                    self.rr.at[pc.p, :, cols],
-                    self.xs.at[c, k],
-                    self.xr.at[c, k],
-                    pc.at(pc.z, p),
-                )
-
-    def mix(self, c):
+    def first(self, c):
+        pc = self.place
+        cols = pl.ds(c * self.chunk, self.chunk)
+        for k in range(1, PLANE):
+            p = pc.by(k)
+            self.sends.start(
+                self.res.at[p, :, cols],
+                self.rr.at[pc.p, :, cols],
+                self.xs.at[c, k],
+                self.xr.at[c, k],
+                pc.at(pc.z, p),
+            )
+
+    def mix(self, c, chunks):
         pc, zn = self.place, self.zn
         cols = pl.ds(c * self.chunk, self.chunk)
         own = pltpu.make_async_copy(self.res.at[pc.p, :, cols], self.rbuf.at[pc.p], self.ls.at[0])
@@ -1396,10 +1449,14 @@
         copies = []
         for k in range(1, PLANE):
             p = pc.by(k)
-            arrived(self.rr.at[p, :, cols], self.xr.at[c, k])
-            copy = pltpu.make_async_copy(self.rr.at[p, :, cols], self.rbuf.at[p], self.ls.at[k])
+            if c:
+                arrived(self.rr.at[p, :, cols], self.xr.at[c, k])
+            src = self.rr.at[p, :, cols] if c else self.early.at[p]
+            copy = pltpu.make_async_copy(src, self.rbuf.at[p], self.ls.at[k])
             copy.start()
             copies.append(copy)
+        if c and c + 2 < chunks:
+            self.first(c + 2)
         own.wait()
         for copy in copies:
             copy.wait()
@@ -1451,9 +1508,9 @@
 
 
 def rear_kernel(
-    zn, chunk, heads,
+    zn, chunk, heads, starts_ref,
     mid_ref, tok_ref, gain_ref, hg_ref, flat_ref, comb_ref,
-    res_hbm, seq_hbm, wq_hbm, wo_hbm, pre_hbm, rot_hbm, val_hbm, lse_hbm, ctx_hbm, tab_hbm, bias_hbm,
+    res_hbm, early_hbm, seq_hbm, wq_hbm, wo_hbm, pre_hbm, rot_hbm, val_hbm, lse_hbm, ctx_hbm, tab_hbm,
     grad_ref, oq_ref, oo_ref, sum_ref, tiny_ref, am_hbm, rr_hbm,
     big, wq, wo, pre, rot, val, lse, ctx, tab, bias,
     lse_t, del_t, key_t, cback, aback, dk, dv, dgain,
@@ -1474,7 +1531,7 @@
     greet(place, zn)
     pairs = (
         (wo_hbm, wo), (ctx_hbm, ctx), (rot_hbm, rot), (val_hbm, val), (lse_hbm, lse),
-        (bias_hbm, bias), (pre_hbm, pre), (tab_hbm, tab), (wq_hbm, wq),
+        (pre_hbm, pre), (tab_hbm, tab), (wq_hbm, wq),
     )
     fetch = [pltpu.make_async_copy(a, b, loads.at[i]) for i, (a, b) in enumerate(pairs)]
     small = SmallSum(place, sends, zn, flat_ref, sum_ref, small_scratch)
@@ -1482,7 +1539,7 @@
     row_sends = Sends()
     rows = PlaneGather(place, row_sends, big, gs, gr)
     result = Result(
-        place, zn, res_hbm, comb_ref, rr_hbm, am_hbm, rbuf, zbuf, chunk, xs, xr, zs, zr, ls, os
+        place, sends, zn, res_hbm, early_hbm, comb_ref, rr_hbm, am_hbm, rbuf, zbuf, chunk, xs, xr, zs, zr, ls, os
     )
     o = ColumnReduce(place, sends, zn, go, bo, sr.at[1], sl.at[1], rr.at[1], rl.at[1])
     q = ColumnReduce(place, sends, zn, gq, bq, sr.at[0], sl.at[0], rr.at[0], rl.at[0])
@@ -1494,18 +1551,21 @@
 
     lax.fori_loop(0, tok // 32, stage, 0)
     rows.first()
+    rows.along()
     for copy in fetch:
         copy.start()
     small.first()
     rows.second()
     rows.third()
-    for copy in fetch[:6]:
+    result.mix(0, chunks)
+    for copy in fetch[:5]:
         copy.wait()
     key_t[...] = rot[heads].astype(f32).T.astype(bf16)
     lse_t[...] = lse[...].T
     small.second()
     rows.last()
-    result.first(sends, chunks)
+    for c in range(1, min(3, chunks)):
+        result.first(c)
 
     order = []
     for k in range(zn):
@@ -1554,7 +1614,7 @@
     dk[...] = jnp.zeros_like(dk)
     dv[...] = jnp.zeros_like(dv)
     dgain[...] = jnp.zeros_like(dgain)
-    for copy in fetch[6:]:
+    for copy in fetch[5:]:
         copy.wait()
 
     def norm_of(d, at, h, gain_row):
@@ -1567,16 +1627,19 @@
         dgain[pl.ds(gain_row, 1), :] += jnp.sum(d * hat, axis=0, keepdims=True)
         return got.astype(bf16)
 
+    starts = [starts_ref[pc.z, j] for j in range(starts_ref.shape[1])]
+
     def attend(i):
         limit = key_limit(i, length)
         at = slice(i * QBLOCK, (i + 1) * QBLOCK)
+        bias[:limit, :] = bias_block(starts, i * QBLOCK, limit, True)
 
         def body(h, carry):
             cols = pl.ds(pl.multiple_of(h * HD, HD), HD)
             query = rot[h, at, :]
             dctx = cback[at, cols]
             scores = nt_dot(rot[heads, :limit, :], query) * scale
-            scores = scores + bias[:limit, at].astype(f32)
+            scores = scores + bias[:limit, :]
             probs = jnp.exp(scores - lse_t[pl.ds(h, 1), at])
             dprobs = nt_dot(val[:limit, :], dctx)
             dscores = (probs * (dprobs - del_t[pl.ds(h, 1), at])).astype(bf16)
@@ -1586,20 +1649,10 @@
             aback[at, cols] = norm_of(dq, at, h, 0)
             return carry
 
-        lax.fori_loop(0, heads, body, 0)
-
-    blocks = length // QBLOCK
-    hop = 1
-    for i in range(blocks):
+        lax.fori_loop(0, heads, body, 0, unroll=2)
+
+    for i in range(length // QBLOCK):
         attend(i)
-        if i % 2 == 1 and hop < zn - 1:
-            o.step(hop)
-            hop += 1
-        if i == 2:
-            result.mix(0)
-    while hop < zn - 1:
-        o.step(hop)
-        hop += 1
 
     def keys(i, carry):
         at = pl.ds(pl.multiple_of(i * 256, 256), 256)
@@ -1629,14 +1682,19 @@
             made += 1
         if k == 0:
             q.step(0)
+            if zn > 2:
+                o.step(1)
     while made < len(order):
         query_grad(order[made])
         made += 1
 
-    red = PlaneReduce(place, sends, big, grad_ref, (c1, s1, ra, rb, last), hs, hr)
+    mixed = 1
+    red = PlaneReduce(
+        place, sends, big, grad_ref, (c1, s1, ra, rb, last), hs, hr, pl.ds(0, width)
+    )
 
     def norm1_part(k):
-        y, x, j = red._chip(*red.chips[k])
+        y, x, j = red.chip(*red.chips[k])
         lhs = aback[pl.ds(pl.multiple_of(j * 2 * tok, 2 * tok), 2 * tok), :]
 
         def body(i, carry):
@@ -1651,15 +1709,30 @@
     for k in range(4):
         norm1_part(k)
         red.first(k)
-    if zn > 2:
-        q.step(1)
-    for k in range(4):
-        red.second(k)
-    red.third()
-    result.mix(1)
-    for k in range(2, zn - 1):
+    if mixed < chunks:
+        result.mix(mixed, chunks)
+        mixed += 1
+    for j in range(4):
+        red.second(j)
+    for k in range(1, zn - 1):
         q.step(k)
-    result.mix(2)
+        if k + 1 < zn - 1:
+            o.step(k + 1)
+        if k == 1:
+            red.third()
+        if mixed < chunks:
+            result.mix(mixed, chunks)
+            mixed += 1
+    def split_o(at, v):
+        first, second = v[:, :own_rows], v[:, own_rows:]
+        low = pc.y == 0
+        vo[at, :] = jnp.where(low, second, first).astype(bf16)
+        oo_ref[pc.y, at, :] = jnp.where(low, first, second)
+
+    o.own(split_o)
+    sends.start(vo, to, ps.at[1], pr.at[1], pc.peer(dy=1))
+    if zn <= 2:
+        red.third()
     red.finish()
 
     def tokens_back(i, carry):
@@ -1678,17 +1751,10 @@
     tiny.vec[:, width : width + HD] = dgain[0:1, :]
     tiny.vec[:, width + HD : width + 2 * HD] = dgain[1:2, :]
     tiny.first()
-    for c in range(3, chunks):
-        result.mix(c)
-
-    def split_o(at, v):
-        first, second = v[:, :own_rows], v[:, own_rows:]
-        low = pc.y == 0
-        vo[at, :] = jnp.where(low, second, first).astype(bf16)
-        oo_ref[pc.y, at, :] = jnp.where(low, first, second)
-
-    o.own(split_o)
-    sends.start(vo, to, ps.at[1], pr.at[1], pc.peer(dy=1))
+    while mixed < chunks:
+        result.mix(mixed, chunks)
+        mixed += 1
+
     tiny.second()
     q_own(q, pc, zn, gq, bq, vq, oq_ref, own_rows)
     sends.start(vq, tq, ps.at[0], pr.at[0], pc.peer(dy=1))
@@ -1724,8 +1790,8 @@
 
 
 def rear(
-    zn, heads, middle, tokens, gain, gains, flat, comb, res, seq, full_q, full_o, pre, rot, val, lse,
-    ctx, tables, bias, chunk=512,
+    zn, heads, starts, middle, tokens, gain, gains, flat, comb, res, early, seq, full_q, full_o, pre, rot, val, lse,
+    ctx, tables, chunk=512,
 ):
     tok, width = tokens.shape
     length = PLANE * tok
@@ -1747,7 +1813,7 @@
             shape((zn, tok, width), bf16),
             shape((PLANE, slots, width), bf16),
         ),
-        in_specs=[VSPEC] * 6 + [ASPEC] * 11,
+        in_specs=[SSPEC] + [VSPEC] * 6 + [ASPEC] * 11,
         out_specs=(VSPEC,) * 5 + (ASPEC,) * 2,
         scratch_shapes=[
             vmem((PLANE, tok, width), bf16),
@@ -1759,7 +1825,7 @@
             vmem((length, 128), f32),
             vmem((length, half), bf16),
             vmem((2, length, HD), f32),
-            vmem((length, length), bf16),
+            vmem((length, QBLOCK), f32),
             vmem((128, length), f32),
             vmem((128, length), f32),
             vmem((HD, length), bf16),
@@ -1783,8 +1849,8 @@
             vmem((2, zn, tok, chunk), bf16),
             dma_sems(8),
             dma_sems(8),
-            dma_sems(10),
-            dma_sems(10),
+            dma_sems(1, 10),
+            dma_sems(1, 10),
             dma_sems(2, zn),
             dma_sems(2, zn),
             dma_sems(2, zn),
@@ -1804,8 +1870,8 @@
         compiler_params=params(5),
         name="rear",
     )(
-        middle, tokens, gain, gains, flat, comb, res, seq, full_q, full_o, pre, rot, val, lse, ctx,
-        tables, bias,
+        starts, middle, tokens, gain, gains, flat, comb, res, early, seq, full_q, full_o, pre, rot, val, lse,
+        ctx, tables,
     )
 
 
@@ -1837,10 +1903,6 @@
     own_rows = query_weight.shape[0]
     half = query_weight.shape[1] // 2
     heads = half // HD
-    scale = HD ** (-0.5)
-    exp_index = lax.axis_index("exp")
-    starts = lax.dynamic_slice_in_dim(image_starts, exp_index // 2, 1, 0)[0]
-
     expert_axis = jnp.arange(experts, dtype=jnp.int32)
     member = jnp.any(expert_ids[:, :, None] == expert_axis[None, None, :], axis=1)
     order_here = router_order[0]
@@ -1850,27 +1912,14 @@
     slot_of = jnp.where(keep, counts, -1.0)
 
     resid_in = tokens.astype(f32)
-    first_rms = rms_scale(resid_in)
-    first_hat = resid_in * first_rms
-    first_norm = (first_hat * first_gain).astype(bf16)
-    q_halves = query_weight.reshape(own_rows, 2, half).transpose(1, 0, 2)
-    kv = jnp.concatenate([key_weight, value_weight], axis=1)
-    pack_q = jnp.concatenate([q_halves, jnp.broadcast_to(kv[None], (2,) + kv.shape)], axis=2)
-    pack_o = output_weight.reshape(2, half, own_rows).transpose(0, 2, 1)
-    pos = jnp.arange(length, dtype=jnp.int32)
-    cosine, sine = rotary_tables(pos, HD)
-    tables = jnp.stack(
-        [jnp.concatenate([cosine, cosine], axis=1), jnp.concatenate([-sine, sine], axis=1)]
-    )
-    pieces = piece_ids(pos, starts)
-    mask = allowed_mask(pos, pos, pieces, pieces)
-    bias = jnp.where(mask, 0.0, NEGATIVE).astype(bf16)
+    tables = jnp.asarray(rotary_tables(length))
     slot_t = slot_of.T.reshape(zn, PLANE, tok)
+    gains = jnp.stack([query_gain, key_gain])
     (
-        seq_norm, full_q, full_o, pre, rot, value_rows, lse, context_rows, attention, rows_g, slots_all,
+        lse, attention, slots_all, seq_norm, full_q, full_o, pre, rot, value_rows, context_rows, rows_g,
     ) = front(
-        zn, cap, heads, tokens, first_gain[None], pack_q, pack_o, tables,
-        jnp.stack([query_gain, key_gain]), bias, out_grad, slot_t,
+        zn, cap, heads, image_starts, tokens, first_gain[None], query_weight, key_weight, value_weight,
+        output_weight, gains, out_grad, slot_t, tables,
     )
     resid_mid = resid_in + attention
     second_rms = rms_scale(resid_mid)
@@ -1882,10 +1931,10 @@
     keep_mix = jnp.where(keep, mix, 0.0)
     mix_t = keep_mix.T.reshape(zn, PLANE, tok)
     gate_w, up_w, down_w = gate_weight[0], up_weight[0], down_weight[0]
-    rows_n, mids, dot_lanes, hot, comb = there(
+    dot_lanes, rows_n, mids, hot, comb = there(
         zn, cap, second_norm, slots_all, mix_t, rows_g, gate_w, up_w, down_w
     )
-    dots_all, pairs, result, gate_grad, up_grad, down_grad = back_rows(
+    dots_all, pairs, result, gate_grad, up_grad, down_grad, result_first = back_rows(
         zn, tok, dot_lanes, hot, mids, rows_n, rows_g, gate_w, up_w, down_w
     )
     pairs_sum = jnp.sum(pairs.astype(f32), axis=0)
@@ -1905,9 +1954,9 @@
     padded = -(-count // unit) * unit
     flat = jnp.pad(flat, (0, padded - count)).reshape(PLANE, padded // (PLANE * 128), 128)
     tokens_grad, sum_q, sum_o, flat, tiny, mixtures, _ = rear(
-        zn, heads, middle_grad, tokens, first_gain[None], jnp.stack([query_gain, key_gain]), flat, comb,
-        result, seq_norm, full_q, full_o, pre, rot, value_rows, lse,
-        context_rows, tables, bias.T,
+        zn, heads, image_starts, middle_grad, tokens, first_gain[None], gains, flat, comb,
+        result, result_first, seq_norm, full_q, full_o, pre, rot, value_rows, lse,
+        context_rows, tables,
     )
     block_out = (resid_mid + jnp.sum(mixtures.astype(f32), axis=0)).astype(bf16)
     query_grad = jnp.concatenate([sum_q[0, :, :half], sum_q[1, :, :half]], axis=1)

time: 613 us -> 576 us (0.940)
  Pallas kernels: 553 us -> 529 us
  other arithmetic: 26.7 us -> 13.6 us
    pallas_call x1, Pallas kernels: 162 us -> 148 us  [front(): pl.pallas_call(functools.partial(front_kernel, zn, cap, chunk, heads), ou...]
    pallas_call x1, Pallas kernels: 105 us -> 94.1 us  [there(): pl.pallas_call(functools.partial(there_kernel, zn, cap, chunk), out_shape...]
    pallas_call x1, Pallas kernels: 78.4 us -> 85.9 us  [back_rows(): pl.pallas_call(functools.partial(back_kernel, zn, chunk), out_shape=(shap...]
    pallas_call x1, Pallas kernels: 208 us -> 201 us  [rear(): pl.pallas_call(functools.partial(rear_kernel, zn, chunk, heads), out_shap...]
    unnamed x47 -> x39, local copies, waits for them, and re-layouts: 18.1 us -> 17.7 us
where the time goes in v4:
time: 576 us; the launch traced here: 567 us
  Pallas kernels  529 us (92%)
  local copies, waits for them, and re-layouts  21 us (4%)
  other arithmetic  13.6 us (2%)
    pallas_call x1, Pallas kernels, rear(): pl.pallas_call(functools.partial(rear_kernel, zn, chunk, heads), out_shap...  201 us
    pallas_call x1, Pallas kernels, front(): pl.pallas_call(functools.partial(front_kernel, zn, cap, chunk, heads), ou...  148 us
    pallas_call x1, Pallas kernels, there(): pl.pallas_call(functools.partial(there_kernel, zn, cap, chunk), out_shape...  94.1 us
    pallas_call x1, Pallas kernels, back_rows(): pl.pallas_call(functools.partial(back_kernel, zn, chunk), out_shape=(shap...  85.9 us
    unnamed x39, local copies, waits for them, and re-layouts  17.7 us

profile of v4, /device:TPU:8, one launch (start us, length us, event | category | flops | bytes accessed | tf_op | source)
XLA Modules:
  0.0 567.5 jit_solution(8423672390945870351)
XLA Ops:
  0.6 0.0 copy-start
  0.7 0.0 copy-start.10
  0.7 0.0 copy-start.4
  0.7 1.3 pad_maximum_fusion.1.hg_ref
  2.0 1.3 copy.42.starts_ref
  3.3 0.7 fusion
  4.0 0.9 fusion.3
  5.0 0.6 select_bitcast_fusion.slot_ref
  5.6 148.0 %front.1 = (f32[1024,128]{1,0:T(8,128)}, f32[128,2048]{1,0:T(8,128)}, f32[4,8,128]{2,1,0:T(8,128)}, bf16[8,128,2048]{2,1,0:T(8,128)(2,1)}, bf16[8,256,768]{2,1,0...) custom-call(s32[4,2]{1,0:T(4,128)} %copy.42.starts_ref, ...), custom_call_target="tpu_custom_call" | custom-call | tf_op jit(solution)/shard_map/front/pallas_call | solution.py:730
  153.6 0.0 copy-done.4
  153.6 1.4 multiply_reduce_fusion.2
  155.1 0.0 copy-done.10
  155.1 0.2 multiply_convert_fusion.norm_ref
  155.3 0.0 copy-done
  155.3 0.0 copy-start.2
  155.3 0.3 fusion.15
  155.6 0.6 fusion.13.mix_ref
  156.2 0.0 copy-done.2
  156.3 94.1 %there.1 = (bf16[8,144,128]{2,1,0:T(8,128)(2,1)}, bf16[8,144,2048]{2,1,0:T(8,128)(2,1)}, bf16[4,8,144,768]{3,2,1,0:T(8,128)(2,1)}, bf16[512,1152]{1,0:T(8,128)(2,1)}, bf16[512,1152]{1,0:T(8,128)(2,1)}) custom-call(bf16[128,2048]{1,0:T(8,128)(2,1)} %copy-done.2, f32[4,8,128]{2,1,0:T(8,128)} %get-tuple-element.44.slots_ref, f32[4,8,128]{2,1,0:T(8,128)} %fusion.13.mix_ref, ...), custom_call_target="tpu_custom_call" | custom-call | tf_op jit(solution)/shard_map/there/pallas_call | solution.py:984
  250.3 85.9 %back_rows.1 = (f32[4,128,128]{2,1,0:T(8,128)}, bf16[4,128,2048]{2,1,0:T(8,128)(2,1)}, bf16[8,144,2048]{2,1,0:T(8,128)(2,1)}, f32[2048,768]{1,0:T(8,128)}, f32[2...) custom-call(bf16[8,144,128]{2,1,0:T(8,128)(2,1)} %get-tuple-element.46.dot_ref, ...), custom_call_target="tpu_custom_call" | custom-call | tf_op jit(solution)/shard_map/back_rows/pallas_call | solution.py:1198
  336.2 0.0 copy-start.8
  336.2 0.0 copy-start.5
  336.2 2.1 convert_reduce_fusion.1
  338.4 0.0 copy-done.8
  338.4 0.2 fusion.1
  338.6 0.1 copy.43
  338.7 0.0 copy-start.3
  338.7 0.5 multiply_reduce_fusion
  339.3 0.0 copy-done.5
  339.3 1.3 multiply_add_fusion.mid_ref
  340.6 0.0 copy-done.3
  340.6 0.3 fusion.17
  341.0 0.3 reshape.77
  341.2 0.7 select_maximum_fusion
  342.0 201.5 %rear.1 = (f32[128,2048]{1,0:T(8,128)}, f32[2,256,768]{2,1,0:T(8,128)}, f32[2,512,256]{2,1,0:T(8,128)}, f32[8,72,128]{2,1,0:T(8,128)}, f32[1,2304]{1,0:T(1,128)}...) custom-call(s32[4,2]{1,0:T(4,128)} %copy.42.starts_ref, f32[128,2048]{1,0:T(8,128)} %multiply_add_fusion.mid_ref, ...), custom_call_target="tpu_custom_call" | custom-call | tf_op jit(solution)/shard_map/rear/pallas_call | solution.py:1805
  543.4 0.0 copy-start.11
  543.5 0.0 copy-start.9
  543.5 0.0 copy-start.6
  543.5 2.2 convert_reduce_fusion
  545.7 0.9 add_convert_fusion
  546.6 0.0 copy-done.11
  546.6 0.5 slice_bitcast_fusion.2
  547.2 0.6 slice.53
  547.8 0.0 copy-done.9
  547.8 0.6 slice.68
  548.4 0.0 copy-done.6
  548.4 0.1 slice_bitcast_fusion.1
  548.6 1.1 pad_maximum_fusion
  549.6 0.7 fusion.16
  550.3 0.3 slice.66
  550.6 0.1 slice.71
  550.7 1.0 copy.46
  551.7 0.0 slice-start.2
  551.7 2.4 copy.53
  554.2 0.0 copy-done.7
  554.2 1.0 copy.54
  555.1 6.1 %copy.55 = f32[1,2048,768]{2,1,0:T(8,128)} copy(f32[1,2048,768]{2,1,0:T(8,128)} %bitcast.74) | data formatting | bytes 12582912
  561.2 0.0 slice-done.2
  561.2 0.0 slice-done.3
  561.2 2.8 copy.56
  564.0 0.0 slice-done
  564.1 0.3 slice-done.1
  564.3 2.7 copy.57
  567.0 0.0 copy-done.1
  (12 shorter events, 0.1 us)
Async XLA Ops:
  0.6 154.6 %copy-start = (bf16[2048,32]{0,1:T(8,128)(2,1)S(1)}, bf16[2048,32]{0,1:T(8,128)(2,1)}, u32[]{:S(2)}) copy-start(bf16[2048,32]{0,1:T(8,128)(2,1)} %param.28) | copy-start | bytes 393220
  0.7 154.4 %copy-start.10 = (f32[2048]{0:T(1024)S(1)}, f32[2048]{0:T(1024)}, u32[]{:S(2)}) copy-start(f32[2048]{0:T(1024)} %param.21) | copy-start | bytes 24580
  0.7 153.0 %copy-start.4 = (bf16[128,2048]{1,0:T(8,128)(2,1)S(1)}, bf16[128,2048]{1,0:T(8,128)(2,1)}, u32[]{:S(2)}) copy-start(bf16[128,2048]{1,0:T(8,128)(2,1)} %tok_ref.3) | copy-start | bytes 1572868
  155.3 1.0 copy-start.2
  336.2 2.2 copy-start.8
  336.2 3.1 copy-start.5
  338.7 1.9 copy-start.3
  543.4 3.2 copy-start.11
  543.5 4.3 copy-start.9
  543.5 4.9 copy-start.6
  550.3 3.8 copy-start.7
  551.7 9.5 %slice-start.2 = ((s8[6291456]{0:T(1024)(128)(4,1)}), s8[4194304]{0:T(1024)(128)(4,1)S(1)}, s32[]{:S(2)}) async-start(s8[6291456]{0:T(1024)(128)(4,1)} %bitcast.71), calls=%async_computation.2 | async-start | bytes 8388608
  555.1 6.1 %slice-start.3 = ((s8[6291456]{0:T(1024)(128)(4,1)}), s8[2097152]{0:T(1024)(128)(4,1)S(1)}, s32[]{:S(2)}) async-start(s8[6291456]{0:T(1024)(128)(4,1)} %bitcast.71), calls=%async_computation.3 | async-start | bytes 4194304
  555.1 8.9 %slice-start = ((s8[6291456]{0:T(1024)(128)(4,1)}), s8[4194304]{0:T(1024)(128)(4,1)S(1)}, s32[]{:S(2)}) async-start(s8[6291456]{0:T(1024)(128)(4,1)} %bitcast.68), calls=%async_computation | async-start | bytes 8388608
  561.2 3.1 slice-start.1
  564.3 2.7 copy-start.1

commit v5 on v4

--- a/solution.py
+++ b/solution.py
@@ -1116,7 +1116,8 @@
 
         def body(j, carry):
             cols = pl.ds(pl.multiple_of(j * chunk, chunk), chunk)
-            flat[slot, :, cols] = tn_dot(lhs, ag[:, :, cols].reshape(PLANE * slots, chunk))
+            got = tn_dot(lhs, ag[:, :, cols].reshape(PLANE * slots, chunk))
+            flat[slot, :, cols] = got.astype(bf16)
             return carry
 
         lax.fori_loop(0, chunks, body, 0)
@@ -1128,7 +1129,7 @@
         for which, flow, dst in ((0, flow_g, gg_hbm), (1, flow_u, ug_hbm)):
             slot = flow.slot()
             rhs = mids[2 + which].reshape(PLANE * slots, hidden)
-            tall[which, slot] = tn_dot(lhs, rhs)
+            tall[which, slot] = tn_dot(lhs, rhs).astype(bf16)
             flow.send(dst.at[m, :])
 
     def combine(c):
@@ -1201,9 +1202,9 @@
             shape((zn, tok, 128), f32),
             shape((zn, tok, width), bf16),
             shape((PLANE, slots, width), bf16),
-            shape(gate.shape, f32),
-            shape(up.shape, f32),
-            shape(down.shape, f32),
+            shape(gate.shape, bf16),
+            shape(up.shape, bf16),
+            shape(down.shape, bf16),
             shape((PLANE, slots, chunk), bf16),
         ),
         in_specs=[VSPEC] * 2 + [ASPEC] * 6,
@@ -1221,8 +1222,8 @@
             vmem((zn, tok, 128), f32),
             vmem((zn, tok, width), bf16),
             vmem((2, PLANE, slots, chunk), bf16),
-            vmem((2, 2, 256, hidden), f32),
-            vmem((2, 128, width), f32),
+            vmem((2, 2, 256, hidden), bf16),
+            vmem((2, 128, width), bf16),
             dma_sems(9),
             dma_sems(4, 2),
             dma_sems(chunks, PLANE),
@@ -1455,8 +1456,9 @@
             copy = pltpu.make_async_copy(src, self.rbuf.at[p], self.ls.at[k])
             copy.start()
             copies.append(copy)
-        if c and c + 2 < chunks:
-            self.first(c + 2)
+        if c == 1:
+            for later in range(2, chunks):
+                self.first(later)
         own.wait()
         for copy in copies:
             copy.wait()
@@ -1564,8 +1566,8 @@
     lse_t[...] = lse[...].T
     small.second()
     rows.last()
-    for c in range(1, min(3, chunks)):
-        result.first(c)
+    if chunks > 1:
+        result.first(1)
 
     order = []
     for k in range(zn):
@@ -1660,6 +1662,8 @@
         aback[at, half + HD : half + 2 * HD] = dv[at, :].astype(bf16)
         return carry
 
+    if chunks > 1:
+        result.mix(1, chunks)
     lax.fori_loop(0, length // 256, keys, 0)
     fill.wait()
 
@@ -1688,7 +1692,7 @@
         query_grad(order[made])
         made += 1
 
-    mixed = 1
+    mixed = min(2, chunks)
     red = PlaneReduce(
         place, sends, big, grad_ref, (c1, s1, ra, rb, last), hs, hr, pl.ds(0, width)
     )
@@ -1709,9 +1713,6 @@
     for k in range(4):
         norm1_part(k)
         red.first(k)
-    if mixed < chunks:
-        result.mix(mixed, chunks)
-        mixed += 1
     for j in range(4):
         red.second(j)
     for k in range(1, zn - 1):
@@ -1983,9 +1984,9 @@
         value_grad,
         output_grad,
         router_grad,
-        gate_grad[None],
-        up_grad[None],
-        down_grad[None],
+        gate_grad[None].astype(f32),
+        up_grad[None].astype(f32),
+        down_grad[None].astype(f32),
     )
 
 

time: 576 us -> 558 us (0.969)
  Pallas kernels: 529 us -> 514 us
  local copies, waits for them, and re-layouts: 21 us -> 7.67 us
  other arithmetic: 13.6 us -> 25 us
    unnamed x39 -> x34, local copies, waits for them, and re-layouts: 17.7 us -> 4.37 us
    convert_element_type x0 -> x2, other arithmetic: none -> 11.4 us  [the longest x1 5.77 us: local(): up_grad[None].astype(f32)]
    pallas_call x1, Pallas kernels: 85.9 us -> 76.8 us  [back_rows(): pl.pallas_call(functools.partial(back_kernel, zn, chunk), out_shape=(shap...]
    pallas_call x1, Pallas kernels: 201 us -> 195 us  [rear(): pl.pallas_call(functools.partial(rear_kernel, zn, chunk, heads), out_shap...]
where the time goes in v5:
time: 558 us; the launch traced here: 549 us
  Pallas kernels  514 us (92%)
  other arithmetic  25 us (4%)
  local copies, waits for them, and re-layouts  7.67 us (1%)
    pallas_call x1, Pallas kernels, rear(): pl.pallas_call(functools.partial(rear_kernel, zn, chunk, heads), out_shap...  195 us
    pallas_call x1, Pallas kernels, front(): pl.pallas_call(functools.partial(front_kernel, zn, cap, chunk, heads), ou...  148 us
    pallas_call x1, Pallas kernels, there(): pl.pallas_call(functools.partial(there_kernel, zn, cap, chunk), out_shape...  94.1 us
    pallas_call x1, Pallas kernels, back_rows(): pl.pallas_call(functools.partial(back_kernel, zn, chunk), out_shape=(shap...  76.8 us

profile of v5, /device:TPU:8, one launch (start us, length us, event | category | flops | bytes accessed | tf_op | source)
XLA Modules:
  0.0 549.5 jit_solution(12093449538242639967)
XLA Ops:
  0.6 0.0 copy-start
  0.7 0.0 copy-start.13
  0.7 0.0 copy-start.4
  0.7 1.3 pad_maximum_fusion.1.hg_ref
  2.0 1.3 copy.42.starts_ref
  3.3 0.7 fusion
  4.0 0.9 fusion.3
  5.0 0.6 select_bitcast_fusion.slot_ref
  5.6 148.1 %front.1 = (f32[1024,128]{1,0:T(8,128)}, f32[128,2048]{1,0:T(8,128)}, f32[4,8,128]{2,1,0:T(8,128)}, bf16[8,128,2048]{2,1,0:T(8,128)(2,1)}, bf16[8,256,768]{2,1,0...) custom-call(s32[4,2]{1,0:T(4,128)} %copy.42.starts_ref, ...), custom_call_target="tpu_custom_call" | custom-call | tf_op jit(solution)/shard_map/front/pallas_call | solution.py:730
  153.7 0.0 copy-done.4
  153.7 1.4 multiply_reduce_fusion.2
  155.2 0.0 copy-done.13
  155.2 0.2 multiply_convert_fusion.norm_ref
  155.4 0.0 copy-done
  155.4 0.0 copy-start.2
  155.4 0.3 fusion.15
  155.7 0.6 fusion.13.mix_ref
  156.3 0.0 copy-done.2
  156.3 94.1 %there.1 = (bf16[8,144,128]{2,1,0:T(8,128)(2,1)}, bf16[8,144,2048]{2,1,0:T(8,128)(2,1)}, bf16[4,8,144,768]{3,2,1,0:T(8,128)(2,1)}, bf16[512,1152]{1,0:T(8,128)(2,1)}, bf16[512,1152]{1,0:T(8,128)(2,1)}) custom-call(bf16[128,2048]{1,0:T(8,128)(2,1)} %copy-done.2, f32[4,8,128]{2,1,0:T(8,128)} %get-tuple-element.44.slots_ref, f32[4,8,128]{2,1,0:T(8,128)} %fusion.13.mix_ref, ...), custom_call_target="tpu_custom_call" | custom-call | tf_op jit(solution)/shard_map/there/pallas_call | solution.py:984
  250.5 76.8 %back_rows.1 = (f32[4,128,128]{2,1,0:T(8,128)}, bf16[4,128,2048]{2,1,0:T(8,128)(2,1)}, bf16[8,144,2048]{2,1,0:T(8,128)(2,1)}, bf16[2048,768]{1,0:T(8,128)(2,1)},...) custom-call(bf16[8,144,128]{2,1,0:T(8,128)(2,1)} %get-tuple-element.46.dot_ref, ...), custom_call_target="tpu_custom_call" | custom-call | tf_op jit(solution)/shard_map/back_rows/pallas_call | solution.py:1199
  327.3 0.0 copy-start.11
  327.3 0.0 copy-start.7
  327.3 2.1 convert_reduce_fusion.1
  329.4 0.0 copy-done.11
  329.4 0.2 fusion.1
  329.6 0.1 copy.43
  329.8 0.0 copy-start.3
  329.8 0.5 multiply_reduce_fusion
  330.3 0.0 copy-done.7
  330.3 1.3 multiply_add_fusion.mid_ref
  331.7 0.0 copy-done.3
  331.7 0.3 fusion.17
  332.0 0.3 reshape.83
  332.3 0.7 select_maximum_fusion
  333.0 194.7 %rear.1 = (f32[128,2048]{1,0:T(8,128)}, f32[2,256,768]{2,1,0:T(8,128)}, f32[2,512,256]{2,1,0:T(8,128)}, f32[8,72,128]{2,1,0:T(8,128)}, f32[1,2304]{1,0:T(1,128)}...) custom-call(s32[4,2]{1,0:T(4,128)} %copy.42.starts_ref, f32[128,2048]{1,0:T(8,128)} %multiply_add_fusion.mid_ref, ...), custom_call_target="tpu_custom_call" | custom-call | tf_op jit(solution)/shard_map/rear/pallas_call | solution.py:1806
  527.7 0.0 copy-start.14
  527.7 0.0 copy-start.12
  527.7 0.0 copy-start.8
  527.7 2.2 convert_reduce_fusion
  530.0 0.9 add_convert_fusion
  530.9 0.0 copy-done.14
  530.9 0.5 slice_bitcast_fusion.2
  531.4 0.6 slice.53
  532.0 0.0 copy-done.12
  532.0 0.6 slice.68
  532.6 0.0 copy-done.8
  532.7 0.1 slice_bitcast_fusion.1
  532.8 1.1 pad_maximum_fusion
  533.9 0.7 fusion.16
  534.6 0.3 slice.66
  534.9 0.1 slice.71
  535.0 1.0 copy.46
  536.0 0.0 copy-start.5
  536.0 0.0 copy-start.6
  536.0 5.6 %bitcast_convert_fusion = f32[1,768,2048]{2,1,0:T(8,128)} fusion(bf16[768,2048]{1,0:T(8,128)(2,1)} %get-tuple-element.71), kind=kLoop, calls=%fused_computation.2 | loop fusion | flops 1572864 | bytes 9437184 | tf_op jit(solution)/shard_map/convert_element_type | solution.py:1989
  541.6 0.0 copy-done.5
  541.6 0.0 copy-done.6
  541.6 0.0 copy-start.1
  541.6 5.8 %bitcast_convert_fusion.1 = (f32[1,2048,768]{2,1,0:T(8,128)}, f32[1,2048,768]{2,1,0:T(8,128)}) fusion(bf16[2048,768]{1,0:T(8,128)(2,1)S(1)} %copy-done.6, bf16[2048,768]{1,0:T(8,128)(2,1)S(1)} %copy-done.5), kind=kLoop, calls=%fused_computation.3 | loop fusion | flops 3145728 | bytes 18874368 | tf_op jit(solution)/shard_map/convert_element_type | solution.py:1988
  547.4 0.0 copy-done.10
  547.4 1.0 copy.50
  548.3 0.0 copy-done.9
  548.3 1.0 copy.51
  549.3 0.0 copy-done.1
  (7 shorter events, 0.1 us)
Async XLA Ops:
  0.6 154.7 %copy-start = (bf16[2048,32]{0,1:T(8,128)(2,1)S(1)}, bf16[2048,32]{0,1:T(8,128)(2,1)}, u32[]{:S(2)}) copy-start(bf16[2048,32]{0,1:T(8,128)(2,1)} %param.28) | copy-start | bytes 393220
  0.7 154.5 %copy-start.13 = (f32[2048]{0:T(1024)S(1)}, f32[2048]{0:T(1024)}, u32[]{:S(2)}) copy-start(f32[2048]{0:T(1024)} %param.21) | copy-start | bytes 24580
  0.7 153.0 %copy-start.4 = (bf16[128,2048]{1,0:T(8,128)(2,1)S(1)}, bf16[128,2048]{1,0:T(8,128)(2,1)}, u32[]{:S(2)}) copy-start(bf16[128,2048]{1,0:T(8,128)(2,1)} %tok_ref.3) | copy-start | bytes 1572868
  155.4 1.0 copy-start.2
  327.3 2.2 copy-start.11
  327.3 3.1 copy-start.7
  329.8 1.9 copy-start.3
  527.7 3.2 copy-start.14
  527.7 4.3 copy-start.12
  527.7 4.9 copy-start.8
  536.0 5.6 %copy-start.5 = (bf16[2048,768]{1,0:T(8,128)(2,1)S(1)}, bf16[2048,768]{1,0:T(8,128)(2,1)}, u32[]{:S(2)}) copy-start(bf16[2048,768]{1,0:T(8,128)(2,1)} %get-tuple-element.69) | copy-start | bytes 9437188
  536.0 5.6 %copy-start.6 = (bf16[2048,768]{1,0:T(8,128)(2,1)S(1)}, bf16[2048,768]{1,0:T(8,128)(2,1)}, u32[]{:S(2)}) copy-start(bf16[2048,768]{1,0:T(8,128)(2,1)} %get-tuple-element.70) | copy-start | bytes 9437188
  541.6 5.8 %copy-start.10 = (f32[128,2048]{1,0:T(8,128)S(1)}, f32[128,2048]{1,0:T(8,128)}, u32[]{:S(2)}) copy-start(f32[128,2048]{1,0:T(8,128)} %get-tuple-element.132) | copy-start | bytes 3145732
  541.6 6.8 %copy-start.9 = (f32[2,512,256]{2,1,0:T(8,128)S(1)}, f32[2,512,256]{2,1,0:T(8,128)}, u32[]{:S(2)}) copy-start(f32[2,512,256]{2,1,0:T(8,128)} %get-tuple-element.68) | copy-start | bytes 3145732
  541.6 7.7 %copy-start.1 = (bf16[2048,32]{0,1:T(8,128)(2,1)S(1)}, bf16[2048,32]{0,1:T(8,128)(2,1)}, u32[]{:S(2)}) copy-start(bf16[2048,32]{0,1:T(8,128)(2,1)} %param.28) | copy-start | bytes 393220
